TPU v7x, 128 devices: a whole 4x4x4 slice. The times are simulated.
128 devices in a mesh: grp: 4 (over x_lo, core), wide: 32 (over y, x_hi, z).
Axes of the slice: x: 4 (x_hi: 2, x_lo: 2; x = x_hi * 2 + x_lo), y: 4, z: 4, core: 2. Of those that a mesh axis runs over, the one named last changes fastest.
Arguments:
- token_ids: int32 [4, 8192], P('grp', 'wide'), may hold values from 0 to 49151
- targets: int32 [4, 8192], P('grp', 'wide'), may hold values from 0 to 49151
- segment_ids: int32 [4, 8192], P('grp', 'wide'), may hold values from 0 to 127, never falling along the last dimension, each value on 1 to 128 neighbouring positions
- row_counts: int32 [4, 32, 3], P('grp', 'wide'), may hold values from 0 to 1, as said below
- embed_table_master: float32 [4, 49152, 576], P('grp', 'wide')
- embed_table_first: float32 [4, 49152, 576], P('grp', 'wide'), may hold values from -2.861023e-06 to 2.861023e-06
- embed_table_second: float32 [4, 49152, 576], P('grp', 'wide'), may hold values from 1.5697491e-15 to 2.5115985e-14
- embed_table_anchor: float32 [49152, 576], P('wide')
- embed_table_momentum: float32 [49152, 576], P('wide'), may hold values from -0.3125 to 0.3125
- attn_in_master: float32 [4, 576, 960], P('grp', None, 'wide')
- attn_in_first: float32 [4, 576, 960], P('grp', None, 'wide'), may hold values from -2.861023e-06 to 2.861023e-06
- attn_in_second: float32 [4, 576, 960], P('grp', None, 'wide'), may hold values from 1.5697491e-15 to 2.5115985e-14
- attn_in_anchor: float32 [576, 960], P(None, 'wide')
- attn_in_momentum: float32 [576, 960], P(None, 'wide'), may hold values from -0.3125 to 0.3125
- ffn_in_master: float32 [4, 576, 3072], P('grp', None, 'wide')
- ffn_in_first: float32 [4, 576, 3072], P('grp', None, 'wide'), may hold values from -2.861023e-06 to 2.861023e-06
- ffn_in_second: float32 [4, 576, 3072], P('grp', None, 'wide'), may hold values from 1.5697491e-15 to 2.5115985e-14
- ffn_in_anchor: float32 [576, 3072], P(None, 'wide')
- ffn_in_momentum: float32 [576, 3072], P(None, 'wide'), may hold values from -0.3125 to 0.3125
- proj_out_master: float32 [4, 2112, 576], P('grp', None, 'wide')
- proj_out_first: float32 [4, 2112, 576], P('grp', None, 'wide'), may hold values from -2.861023e-06 to 2.861023e-06
- proj_out_second: float32 [4, 2112, 576], P('grp', None, 'wide'), may hold values from 1.5697491e-15 to 2.5115985e-14
- proj_out_anchor: float32 [2112, 576], P(None, 'wide')
- proj_out_momentum: float32 [2112, 576], P(None, 'wide'), may hold values from -0.3125 to 0.3125
- norm_gains_master: float32 [4, 3, 576], P('grp')
- norm_gains_first: float32 [4, 3, 576], P('grp'), may hold values from -3.0517578e-05 to 3.0517578e-05
- norm_gains_second: float32 [4, 3, 576], P('grp'), may hold values from 1.5697491e-13 to 2.5115986e-12
- norm_gains_anchor: float32 [3, 576], replicated
- norm_gains_momentum: float32 [3, 576], replicated, may hold values from -0.75 to 0.75
Outputs:
- loss_sum: float32 [4], P('grp')
- weight_total: float32 [4], P('grp')
- grad_norm: float32 [4], P('grp')
- embed_table_diff: float32 [49152, 576], P('wide')
- embed_table_outer: float32 [49152, 576], P('wide')
- embed_table_weight: float32 [49152, 576], P('wide')
- embed_table_first_new: float32 [4, 49152, 576], P('grp', 'wide')
- embed_table_second_new: float32 [4, 49152, 576], P('grp', 'wide')
- attn_in_diff: float32 [576, 960], P(None, 'wide')
- attn_in_outer: float32 [576, 960], P(None, 'wide')
- attn_in_weight: float32 [576, 960], P(None, 'wide')
- attn_in_first_new: float32 [4, 576, 960], P('grp', None, 'wide')
- attn_in_second_new: float32 [4, 576, 960], P('grp', None, 'wide')
- ffn_in_diff: float32 [576, 3072], P(None, 'wide')
- ffn_in_outer: float32 [576, 3072], P(None, 'wide')
- ffn_in_weight: float32 [576, 3072], P(None, 'wide')
- ffn_in_first_new: float32 [4, 576, 3072], P('grp', None, 'wide')
- ffn_in_second_new: float32 [4, 576, 3072], P('grp', None, 'wide')
- proj_out_diff: float32 [2112, 576], P(None, 'wide')
- proj_out_outer: float32 [2112, 576], P(None, 'wide')
- proj_out_weight: float32 [2112, 576], P(None, 'wide')
- proj_out_first_new: float32 [4, 2112, 576], P('grp', None, 'wide')
- proj_out_second_new: float32 [4, 2112, 576], P('grp', None, 'wide')
- norm_gains_diff: float32 [3, 576], replicated
- norm_gains_outer: float32 [3, 576], replicated
- norm_gains_weight: float32 [3, 576], replicated
- norm_gains_first_new: float32 [4, 3, 576], P('grp')
- norm_gains_second_new: float32 [4, 3, 576], P('grp')
Inputs may be any that keep to these rules, and one draw needn't show every extreme that they name: `row_counts`: each device's three counts sum to 1 (one row); along wide the source never falls within a group; each group's first device holds a web row and its last a math row.
All inputs are finite; a program needn't handle non-finite values.
Results may differ from a plain program's by a relative error of at most 0.019.
The roundings to bfloat16 on the way count: a program that leaves them out, or rounds other values in their place, can miss the bound.
Values may be sent and summed in bfloat16 or wider, within the bound.
A program may use at most 192 MiB of HBM per device.

v0:
```python
import math

import jax
import jax.numpy as jnp
from jax import lax
from jax.sharding import PartitionSpec as P

D = 576
H = 9
KVH = 3
HD = 64
FF = 1536
STEP = 8


beta_one = 0.9
beta_two = 0.999
adam_eps = 1e-08
weight_decay = 0.1
inner_rate = 0.02
gain_rate = 0.2
clip_norm = 0.01
penalty_weight = 0.005
outer_rate = 0.7
outer_momentum = 0.9
rope_base = 100000.0
norm_eps = 1e-05
masked_score = -1e30


def in_blocks(count):
    size = math.gcd(count, 1024)
    return (size, count // size)


def rms_normed(values, gain):
    return values * lax.rsqrt(jnp.mean(values * values, -1, keepdims=True) + norm_eps) * gain


def norm_back(values, gain, grad):
    output, pull = jax.vjp(rms_normed, values, gain)
    return pull(grad)


def rotary(length, head_size):
    half = head_size // 2
    freqs = rope_base ** (-(jnp.arange(half, dtype=jnp.float32) * 2.0) / head_size)
    angles = jnp.arange(length, dtype=jnp.float32)[:, None] * freqs[None, :]
    return (jnp.concatenate([jnp.cos(angles)] * 2, -1), jnp.concatenate([jnp.sin(angles)] * 2, -1))


def rotate(values, cosine, sine):
    half = values.shape[-1] // 2
    turned = jnp.concatenate([-values[..., half:], values[..., :half]], -1)
    return values * cosine[:, None, :] + turned * sine[:, None, :]


def unrotate(grad, cosine, sine):
    return jax.vjp(lambda vals: rotate(vals, cosine, sine), grad)[1](grad)[0]


def swiglu(gate_up):
    return jax.nn.silu(gate_up[:, :FF]) * gate_up[:, FF:]


def score_block(queries, keys, allowed):
    scores = jnp.einsum(
        "qkgc,tkc->kgqt", queries, keys, preferred_element_type=jnp.float32
    ) * HD ** (-0.5)
    return jnp.where(allowed, scores, masked_score)


def attend(queries, keys, values, allowed):
    scores = score_block(queries, keys, allowed)
    peak = jnp.max(scores, -1, keepdims=True)
    expo = jnp.exp(scores - peak)
    expo_sum = jnp.sum(expo, -1, keepdims=True)
    probs = (expo / expo_sum).astype(jnp.bfloat16)
    attended = jnp.einsum("kgqt,tkc->qkgc", probs, values, preferred_element_type=jnp.float32)
    return (attended, peak + jnp.log(expo_sum))


def attend_back(queries, keys, values, allowed, normalizer, grad_out):
    probs = jnp.exp(score_block(queries, keys, allowed) - normalizer)
    grad_probs = jnp.einsum("qkgc,tkc->kgqt", grad_out, values, preferred_element_type=jnp.float32)
    grad_scores = (probs * (grad_probs - jnp.sum(probs * grad_probs, -1, keepdims=True))).astype(
        jnp.bfloat16
    )
    grad_q = jnp.einsum(
        "kgqt,tkc->qkgc", grad_scores, keys, preferred_element_type=jnp.float32
    ) * HD ** (-0.5)
    grad_k = jnp.einsum(
        "kgqt,qkgc->tkc", grad_scores, queries, preferred_element_type=jnp.float32
    ) * HD ** (-0.5)
    grad_v = jnp.einsum(
        "kgqt,qkgc->tkc", probs.astype(jnp.bfloat16), grad_out, preferred_element_type=jnp.float32
    )
    return (grad_q, grad_k, grad_v)


def layer_forward(hidden0, gains, attn_full, ffn_full, proj_full, allowed, cosine, sine):
    length = hidden0.shape[0]
    kv_width = KVH * HD
    normed1 = rms_normed(hidden0, gains[0]).astype(jnp.bfloat16)
    mixed = jnp.dot(normed1, attn_full, preferred_element_type=jnp.float32)
    queries = rotate(mixed[:, :D].reshape(length, H, HD), cosine, sine).astype(jnp.bfloat16)
    queries = queries.reshape(length, KVH, H // KVH, HD)
    keys = rotate(mixed[:, D : D + kv_width].reshape(length, KVH, HD), cosine, sine).astype(
        jnp.bfloat16
    )
    values = mixed[:, D + kv_width :].reshape(length, KVH, HD).astype(jnp.bfloat16)
    attended, normalizer = attend(queries, keys, values, allowed)
    attended = attended.reshape(length, D).astype(jnp.bfloat16)
    hidden1 = hidden0 + jnp.dot(attended, proj_full[:D], preferred_element_type=jnp.float32)
    normed2 = rms_normed(hidden1, gains[1]).astype(jnp.bfloat16)
    gate_up = jnp.dot(normed2, ffn_full, preferred_element_type=jnp.float32)
    inner = swiglu(gate_up).astype(jnp.bfloat16)
    hidden2 = hidden1 + jnp.dot(inner, proj_full[D:], preferred_element_type=jnp.float32)
    final = rms_normed(hidden2, gains[2]).astype(jnp.bfloat16)
    kept = (
        hidden0,
        normed1,
        queries,
        keys,
        values,
        normalizer,
        attended,
        hidden1,
        normed2,
        gate_up,
        inner,
        hidden2,
    )
    return (final, kept)


def layer_backward(grad_final, kept, gains, attn_full, ffn_full, proj_full, allowed, cosine, sine):
    (
        hidden0,
        normed1,
        queries,
        keys,
        values,
        normalizer,
        attended,
        hidden1,
        normed2,
        gate_up,
        inner,
        hidden2,
    ) = kept
    length = hidden0.shape[0]
    grad_h2, grad_g3 = norm_back(hidden2, gains[2], grad_final)
    branch_grad = grad_h2.astype(jnp.bfloat16)
    grad_down = jnp.einsum("tf,td->fd", inner, branch_grad, preferred_element_type=jnp.float32)
    grad_inner = jnp.einsum(
        "td,fd->tf", branch_grad, proj_full[D:], preferred_element_type=jnp.float32
    )
    grad_gate_up = jax.vjp(swiglu, gate_up)[1](grad_inner)[0].astype(jnp.bfloat16)
    grad_ffn = jnp.einsum("td,te->de", normed2, grad_gate_up, preferred_element_type=jnp.float32)
    grad_normed2 = jnp.einsum(
        "te,de->td", grad_gate_up, ffn_full, preferred_element_type=jnp.float32
    )
    grad_h1_part, grad_g2 = norm_back(hidden1, gains[1], grad_normed2)
    grad_h1 = grad_h2 + grad_h1_part
    branch_grad = grad_h1.astype(jnp.bfloat16)
    grad_wo = jnp.einsum("td,te->de", attended, branch_grad, preferred_element_type=jnp.float32)
    grad_att = jnp.einsum(
        "te,de->td", branch_grad, proj_full[:D], preferred_element_type=jnp.float32
    )
    grad_att = grad_att.astype(jnp.bfloat16).reshape(length, KVH, H // KVH, HD)
    grad_q, grad_k, grad_v = attend_back(queries, keys, values, allowed, normalizer, grad_att)
    grad_q = unrotate(grad_q.reshape(length, H, HD), cosine, sine).reshape(length, D)
    grad_k = unrotate(grad_k, cosine, sine).reshape(length, KVH * HD)
    grad_mixed = jnp.concatenate([grad_q, grad_k, grad_v.reshape(length, KVH * HD)], -1).astype(
        jnp.bfloat16
    )
    grad_attn = jnp.einsum("td,te->de", normed1, grad_mixed, preferred_element_type=jnp.float32)
    grad_normed1 = jnp.einsum(
        "te,de->td", grad_mixed, attn_full, preferred_element_type=jnp.float32
    )
    grad_h0_part, grad_g1 = norm_back(hidden0, gains[0], grad_normed1)
    grad_proj = jnp.concatenate([grad_wo, grad_down], 0)
    return (
        grad_h1 + grad_h0_part,
        grad_attn,
        grad_ffn,
        grad_proj,
        jnp.stack([grad_g1, grad_g2, grad_g3]),
    )


def adam_update(weight, grad, first, second, rate, decay):
    first = beta_one * first + (1.0 - beta_one) * grad
    second = beta_two * second + (1.0 - beta_two) * grad * grad
    ratio = first / (1.0 - beta_one**STEP) / (jnp.sqrt(second / (1.0 - beta_two**STEP)) + adam_eps)
    return (weight - rate * (ratio + decay * weight), first, second)


def on_device(
    token_ids,
    targets,
    segment_ids,
    row_counts,
    embed_table_master,
    embed_table_first,
    embed_table_second,
    embed_table_anchor,
    embed_table_momentum,
    attn_in_master,
    attn_in_first,
    attn_in_second,
    attn_in_anchor,
    attn_in_momentum,
    ffn_in_master,
    ffn_in_first,
    ffn_in_second,
    ffn_in_anchor,
    ffn_in_momentum,
    proj_out_master,
    proj_out_first,
    proj_out_second,
    proj_out_anchor,
    proj_out_momentum,
    norm_gains_master,
    norm_gains_first,
    norm_gains_second,
    norm_gains_anchor,
    norm_gains_momentum,
):
    length = token_ids.shape[1]
    vocab_shard = embed_table_master.shape[1]
    member = lax.axis_index("wide")
    offset = member * vocab_shard
    columns = jnp.arange(vocab_shard)
    table_low = embed_table_master[0].astype(jnp.bfloat16)
    gains = norm_gains_master[0]
    attn_full, ffn_full, proj_full = (
        lax.all_gather(attn_in_master[0].astype(jnp.bfloat16), "wide", axis=1, tiled=True),
        lax.all_gather(ffn_in_master[0].astype(jnp.bfloat16), "wide", axis=1, tiled=True),
        lax.all_gather(proj_out_master[0].astype(jnp.bfloat16), "wide", axis=1, tiled=True),
    )
    all_ids, all_targets, all_counts = (
        lax.all_gather(token_ids, "wide", axis=1, tiled=True),
        lax.all_gather(targets, "wide", axis=1, tiled=True),
        lax.all_gather(row_counts, "wide", axis=1, tiled=True),
    )
    all_ids = all_ids[0]
    all_targets = all_targets[0]
    row_weight = jnp.sum(
        all_counts[0].astype(jnp.float32) * jnp.arange(1, 4).astype(jnp.float32), -1
    )
    token_weight = jnp.repeat(row_weight, length)
    total = jnp.sum(token_weight)
    total_rows = all_ids.shape[0]
    embed_size, number = in_blocks(length * lax.axis_size("wide"))

    def one_block(begin):
        local = lax.dynamic_slice_in_dim(all_ids, begin, embed_size) - offset
        picks = (local[:, None] == columns[None, :]).astype(jnp.bfloat16)
        return jnp.dot(picks, table_low, preferred_element_type=jnp.float32)

    hidden0 = lax.psum_scatter(
        lax.map(one_block, jnp.arange(number) * embed_size)
        .reshape(length * lax.axis_size("wide"), D)
        .astype(jnp.bfloat16),
        "wide",
        scatter_dimension=0,
        tiled=True,
    ).astype(jnp.float32)
    place = jnp.arange(length)
    segments = segment_ids[0]
    allowed = ((place[:, None] >= place[None, :]) & (segments[:, None] == segments[None, :]))[
        None, None
    ]
    cosine, sine = rotary(length, HD)
    final, kept = layer_forward(
        hidden0, gains, attn_full, ffn_full, proj_full, allowed, cosine, sine
    )
    all_final = lax.all_gather(final, "wide", axis=0, tiled=True)
    size, number = in_blocks(total_rows)
    starts = jnp.arange(number) * size

    def logits_at(begin, rows):
        rows_blk = lax.dynamic_slice_in_dim(all_final, begin, rows)
        logits = jnp.einsum("td,vd->tv", rows_blk, table_low, preferred_element_type=jnp.float32)
        local = lax.dynamic_slice_in_dim(all_targets, begin, rows) - offset
        return (rows_blk, logits, local[:, None] == columns[None, :])

    def block_stats(begin):
        rows_blk, logits, hits = logits_at(begin, size)
        peak = jnp.max(logits, -1)
        expsum = jnp.sum(jnp.exp(logits - peak[:, None]), -1)
        picked = jnp.sum(jnp.where(hits, logits, 0.0), -1)
        return (peak, expsum, picked)

    peaks, expsums, pickeds = lax.map(block_stats, starts)
    peaks = peaks.reshape(total_rows)
    expsums = expsums.reshape(total_rows)
    pickeds = pickeds.reshape(total_rows)
    peak = lax.pmax(peaks, "wide")
    expsum, picked = lax.psum((expsums * jnp.exp(peaks - peak), pickeds), "wide")
    normalizer = peak + jnp.log(expsum)
    loss_total = jnp.sum(
        token_weight * (normalizer - picked + penalty_weight * normalizer * normalizer)
    )
    soft_coef = token_weight * (1.0 + 2.0 * penalty_weight * normalizer) / total
    pick_coef = token_weight / total

    def grad_at(begin, rows):
        rows_blk, logits, hits = logits_at(begin, rows)
        soft_blk = lax.dynamic_slice_in_dim(soft_coef, begin, rows)
        pick_blk = lax.dynamic_slice_in_dim(pick_coef, begin, rows)
        norm_blk = lax.dynamic_slice_in_dim(normalizer, begin, rows)
        soft = jnp.exp(logits - norm_blk[:, None])
        grad_logits = (soft_blk[:, None] * soft - jnp.where(hits, pick_blk[:, None], 0.0)).astype(
            jnp.bfloat16
        )
        return (rows_blk, grad_logits)

    head_zero = jnp.zeros((vocab_shard, D), jnp.float32)

    def block_back(head_acc, begin):
        rows_blk, grad_logits = grad_at(begin, size)
        return (
            head_acc
            + jnp.einsum("tv,td->vd", grad_logits, rows_blk, preferred_element_type=jnp.float32),
            grad_logits,
        )

    head_grad, kept_logits = lax.scan(block_back, head_zero, starts)
    kept_logits = kept_logits.reshape(total_rows, vocab_shard)
    grad_final = lax.psum_scatter(
        jnp.dot(kept_logits, table_low, preferred_element_type=jnp.float32),
        "wide",
        scatter_dimension=0,
        tiled=True,
    )
    grad_hidden0, grad_attn, grad_ffn, grad_proj, grad_gains = layer_backward(
        grad_final, kept, gains, attn_full, ffn_full, proj_full, allowed, cosine, sine
    )
    piece = lax.all_gather(grad_hidden0.astype(jnp.bfloat16), "wide", axis=0, tiled=True)
    count = piece.shape[0]
    block, blocks = in_blocks(count)
    local = all_ids - offset

    def one_block(acc, pair):
        picks = (pair[0][:, None] == columns[None, :]).astype(jnp.bfloat16)
        return (
            acc + jnp.einsum("tv,td->vd", picks, pair[1], preferred_element_type=jnp.float32),
            None,
        )

    table_grad = lax.scan(
        one_block, head_grad, (local.reshape(blocks, block), piece.reshape(blocks, block, D))
    )[0]
    attn_share = attn_in_master.shape[2]
    ffn_share = ffn_in_master.shape[2]
    proj_share = proj_out_master.shape[2]
    sum_attn, sum_ffn, sum_proj, grad_gains = lax.psum(
        (grad_attn, grad_ffn, grad_proj, grad_gains), "wide"
    )
    sum_attn = lax.dynamic_slice_in_dim(sum_attn, member * attn_share, attn_share, 1)
    sum_ffn = lax.dynamic_slice_in_dim(sum_ffn, member * ffn_share, ffn_share, 1)
    sum_proj = lax.dynamic_slice_in_dim(sum_proj, member * proj_share, proj_share, 1)
    local_squares = (
        jnp.sum(table_grad * table_grad)
        + jnp.sum(sum_attn * sum_attn)
        + jnp.sum(sum_ffn * sum_ffn)
        + jnp.sum(sum_proj * sum_proj)
    )
    norm_squares = lax.psum(local_squares, "wide") + jnp.sum(grad_gains * grad_gains)
    norm = jnp.sqrt(norm_squares)
    factor = jnp.minimum(1.0, clip_norm / norm)
    kinds = (
        (
            embed_table_master[0],
            table_grad,
            embed_table_first[0],
            embed_table_second[0],
            embed_table_anchor,
            embed_table_momentum,
            inner_rate,
            weight_decay,
        ),
        (
            attn_in_master[0],
            sum_attn,
            attn_in_first[0],
            attn_in_second[0],
            attn_in_anchor,
            attn_in_momentum,
            inner_rate,
            weight_decay,
        ),
        (
            ffn_in_master[0],
            sum_ffn,
            ffn_in_first[0],
            ffn_in_second[0],
            ffn_in_anchor,
            ffn_in_momentum,
            inner_rate,
            weight_decay,
        ),
        (
            proj_out_master[0],
            sum_proj,
            proj_out_first[0],
            proj_out_second[0],
            proj_out_anchor,
            proj_out_momentum,
            inner_rate,
            weight_decay,
        ),
        (
            gains,
            grad_gains,
            norm_gains_first[0],
            norm_gains_second[0],
            norm_gains_anchor,
            norm_gains_momentum,
            gain_rate,
            0.0,
        ),
    )
    updated = [
        adam_update(kind[0], kind[1] * factor, kind[2], kind[3], kind[6], kind[7]) for kind in kinds
    ]
    diffs = tuple((kinds[index][4] - updated[index][0] for index in range(5)))
    summed = lax.psum((diffs[0], diffs[1], diffs[2], diffs[3], diffs[4]), "grp")
    groups = lax.axis_size("grp")
    results = [loss_total.reshape(1), total.reshape(1), norm.reshape(1)]
    for index in range(5):
        average = summed[index] / groups
        outer = outer_momentum * kinds[index][5] + average
        weight = kinds[index][4] - outer_rate * (average + outer_momentum * outer)
        results += [average, outer, weight, updated[index][1][None], updated[index][2][None]]
    return tuple(results)


def solution(mesh):
    in_specs = (
        P("grp", "wide"),
        P("grp", "wide"),
        P("grp", "wide"),
        P("grp", "wide", None),
        P("grp", "wide", None),
        P("grp", "wide", None),
        P("grp", "wide", None),
        P("wide", None),
        P("wide", None),
        P("grp", None, "wide"),
        P("grp", None, "wide"),
        P("grp", None, "wide"),
        P(None, "wide"),
        P(None, "wide"),
        P("grp", None, "wide"),
        P("grp", None, "wide"),
        P("grp", None, "wide"),
        P(None, "wide"),
        P(None, "wide"),
        P("grp", None, "wide"),
        P("grp", None, "wide"),
        P("grp", None, "wide"),
        P(None, "wide"),
        P(None, "wide"),
        P("grp", None, None),
        P("grp", None, None),
        P("grp", None, None),
        P(),
        P(),
    )
    out_specs = (
        P("grp"),
        P("grp"),
        P("grp"),
        P("wide", None),
        P("wide", None),
        P("wide", None),
        P("grp", "wide", None),
        P("grp", "wide", None),
        P(None, "wide"),
        P(None, "wide"),
        P(None, "wide"),
        P("grp", None, "wide"),
        P("grp", None, "wide"),
        P(None, "wide"),
        P(None, "wide"),
        P(None, "wide"),
        P("grp", None, "wide"),
        P("grp", None, "wide"),
        P(None, "wide"),
        P(None, "wide"),
        P(None, "wide"),
        P("grp", None, "wide"),
        P("grp", None, "wide"),
        P(),
        P(),
        P(),
        P("grp", None, None),
        P("grp", None, None),
    )
    return jax.shard_map(
        on_device, mesh=mesh, in_specs=in_specs, out_specs=out_specs, check_vma=False
    )
```

profile of v0, /device:TPU:1, one launch (start us, length us, event | category | flops | bytes accessed | tf_op | source)
XLA Modules:
  0.0 2522.7 jit_solution(3902509667742229490)
XLA Ops:
  15.0 83.1 %all_gather.25 = s32[1,8192]{1,0:T(1,128)S(1)} all-gather(s32[1,256]{1,0:T(1,128)S(1)} %copy-done.64), channel_id=1, replica_groups=mesh['grp'=4,'wide'=32] {'wide'}, dimensions={1}, use_global_device_ids=true | all-gather | bytes 33792 | tf_op jit(solution)/shard_map/all_gather | solution.py:244
  98.1 59.7 %while.50 = (s32[]{:T(128)}, bf16[8,1024,576]{1,2,0:T(8,128)(2,1)}, s32[8]{0:T(128)S(1)}, s32[8192]{0:T(1024)S(1)}, s32[]{:T(128)}, /*index=5*/bf16[1536,576]{1,0:T(8,128)(2,1)}, s32[]{:T(128)}, s32[]{:T(128)}, s32[]{:T(128)}) while((s32[]{:T(128)}, bf16[8,1024,576]{1,2,0:T(8,128)(2,1)}, s32[8]{0:T(128)S(1)}, s32[8192]{0:T(1024)S(1)}, ...), condition=%wide.region_2.3_spmd.clone, body=%wide.region_1.0_spmd.clone.sunk | while | flops 1813513216 | bytes 4337823 | solution.py:264
  100.7 4.8 bitcast_dynamic-update-slice_fusion.4
  108.1 4.8 bitcast_dynamic-update-slice_fusion.4
  115.6 4.9 bitcast_dynamic-update-slice_fusion.4
  123.1 4.8 bitcast_dynamic-update-slice_fusion.4
  130.5 4.8 bitcast_dynamic-update-slice_fusion.4
  138.0 4.8 bitcast_dynamic-update-slice_fusion.4
  145.4 4.9 bitcast_dynamic-update-slice_fusion.4
  152.9 4.9 bitcast_dynamic-update-slice_fusion.4
  157.7 9.0 copy.183
  171.9 5.1 reshape.318
  177.0 238.3 %reduce-scatter.3.cloned.1.call-done = bf16[256,576]{0,1:T(8,128)(2,1)} async-done(((bf16[8192,576]{0,1:T(8,128)(2,1)}), bf16[256,576]{0,1:T(8,128)(2,1)}) %reduce-scatter.3.cloned.1.call-update) | async-done | bytes 294928 | tf_op jit(solution)/shard_map/reduce_scatter | solution.py:263
  423.4 72.7 %all-gather.8.cloned.1.call-done = bf16[576,3072]{0,1:T(8,128)(2,1)} async-done(((bf16[576,96]{0,1:T(8,128)(2,1)}), bf16[576,3072]{0,1:T(8,128)(2,1)}) %all-gather.8.cloned.1.call-update) | async-done | bytes 3538960 | tf_op jit(solution)/shard_map/all_gather | solution.py:240
  503.3 76.5 %all_gather.24 = s32[1,32,3]{2,0,1:T(1,128)S(1)} all-gather(s32[1,1,3]{2,0,1:T(1,128)S(1)} %bitcast.345), channel_id=1, replica_groups=mesh['grp'=4,'wide'=32] {'wide'}, dimensions={1}, use_global_device_ids=true | all-gather | bytes 396 | tf_op jit(solution)/shard_map/all_gather | solution.py:246
  580.7 73.8 %all_gather.30 = s32[1,8192]{1,0:T(1,128)S(1)} all-gather(s32[1,256]{1,0:T(1,128)S(1)} %copy-done.65), channel_id=1, replica_groups=mesh['grp'=4,'wide'=32] {'wide'}, dimensions={1}, use_global_device_ids=true | all-gather | bytes 33792 | tf_op jit(solution)/shard_map/all_gather | solution.py:245
  654.5 13.4 copy.152
  667.9 86.3 %while.51 = (s32[]{:T(128)}, f32[8,1024]{1,0:T(8,128)S(1)}, f32[8,1024]{1,0:T(8,128)S(1)}, f32[8,1024]{1,0:T(8,128)}, s32[8]{0:T(128)S(1)}, /*index=5*/bf16[8192...) while((s32[]{:T(128)}, f32[8,1024]{1,0:T(8,128)S(1)}, ...), condition=%wide.region_13.14_spmd.clone, body=%wide.region_9.13_spmd.clone.sunk | while | flops 1821374464 | bytes 15716547 | solution.py:297
  670.5 4.0 fusion.166
  681.3 4.0 fusion.166
  692.0 4.0 fusion.166
  702.8 4.0 fusion.166
  713.6 4.0 fusion.166
  724.4 4.0 fusion.166
  735.2 4.0 fusion.166
  746.0 4.0 fusion.166
  754.2 150.1 %pmax.7 = f32[8192]{0:T(1024)S(1)} all-reduce(f32[8192]{0:T(1024)S(1)} %bitcast.338), channel_id=1, replica_groups=mesh['grp'=4,'wide'=32] {'wide'}, use_global_device_ids=true, to_apply=%region_14.15 | all-reduce | flops 8192 | bytes 65536 | tf_op jit(solution)/shard_map/pmax | solution.py:301
  904.3 148.3 %psum.84 = f32[8192]{0:T(1024)S(1)} all-reduce(f32[8192]{0:T(1024)S(1)} %bitcast_multiply_fusion.7), channel_id=1, replica_groups=mesh['grp'=4,'wide'=32] {'wide'}, use_global_device_ids=true, to_apply=%region_15.16 | all-reduce | flops 8192 | bytes 65536 | tf_op jit(solution)/shard_map/psum | solution.py:302
  1053.9 147.0 %while.53 = (s32[]{:T(128)}, f32[1536,576]{0,1:T(8,128)}, bf16[8,1024,1536]{2,1,0:T(8,128)(2,1)}, s32[8]{0:T(128)S(1)}, f32[8192]{0:T(1024)}, /*index=5*/bf16[81...) while((s32[]{:T(128)}, f32[1536,576]{0,1:T(8,128)}, ...), condition=%wide.region_20.21_spmd.clone, body=%wide.region_19.20_spmd.clone.sunk | while | flops 3635086336 | bytes 49463580 | solution.py:331
  1060.0 6.6 bitcast_dynamic-update-slice_fusion.5
  1066.7 4.0 select_add_fusion.2
  1078.3 6.7 bitcast_dynamic-update-slice_fusion.5
  1085.0 4.0 select_add_fusion.2
  1096.7 6.7 bitcast_dynamic-update-slice_fusion.5
  1103.4 4.0 select_add_fusion.2
  1115.1 6.7 bitcast_dynamic-update-slice_fusion.5
  1121.8 4.0 select_add_fusion.2
  1133.4 6.7 bitcast_dynamic-update-slice_fusion.5
  1140.1 4.0 select_add_fusion.2
  1151.7 6.7 bitcast_dynamic-update-slice_fusion.5
  1158.4 4.0 select_add_fusion.2
  1170.1 6.7 bitcast_dynamic-update-slice_fusion.5
  1188.3 6.8 bitcast_dynamic-update-slice_fusion.5
  1200.9 23.2 fusion.32
  1225.1 357.0 %reduce-scatter.5.cloned.1.call-done = f32[256,576]{0,1:T(8,128)} async-done(((f32[8192,576]{0,1:T(8,128)}), f32[256,576]{0,1:T(8,128)}) %reduce-scatter.5.cloned.1.call-update) | async-done | bytes 589840 | tf_op jit(solution)/shard_map/reduce_scatter | solution.py:333
  1586.3 4.1 fusion.87
  1597.3 4.6 fusion.77
  1620.0 393.6 %all-reduce.12.cloned.1.call-done = (f32[576,960]{0,1:T(8,128)}, f32[576,3072]{0,1:T(8,128)}, f32[2112,576]{0,1:T(8,128)}) async-done(((f32[576,960]{0,1:T(8,128)}, f32[576,3072]{0,1:T(8,128)}, f32[2112,576]{0,1:T(8,128)}), (f32[576,960]{0,1:T(8,128)}, f32[576,3072]{0,1:T(8,128)}, f32[2112,576]{0,1:T(8,128)})) %all-reduce.12.cloned.1.call-update) | async-done | bytes 14155792 | tf_op jit(solution)/shard_map/psum | solution.py:360
  2018.4 118.4 %all-gather.12.cloned.1.call-done = bf16[8192,576]{0,1:T(8,128)(2,1)} async-done(((bf16[256,576]{0,1:T(8,128)(2,1)}), bf16[8192,576]{0,1:T(8,128)(2,1)}) %all-gather.12.cloned.1.call-update) | async-done | bytes 9437200 | tf_op jit(solution)/shard_map/all_gather | solution.py:342
  2136.7 14.1 copy.178
  2150.8 58.2 %while.52 = (s32[]{:T(128)}, f32[1536,576]{0,1:T(8,128)}, s32[8,1024]{1,0:T(8,128)}, bf16[8,1024,576]{2,1,0:T(8,128)(2,1)}, s32[]{:T(128)}) while((s32[]{:T(128)}, f32[1536,576]{0,1:T(8,128)}, s32[8,1024]{1,0:T(8,128)}, bf16[8,1024,576]{2,1,0:T(8,128)(2,1)}, s32[]{:T(128)}) %tuple.186), condition=%wide.region_27.28_spmd.clone, body=%wide.region_26.27_spmd.clone.sunk | while | flops 1814396928 | bytes 8400973 | solution.py:354
  2151.6 6.5 fusion.168
  2158.9 6.5 fusion.168
  2166.2 6.5 fusion.168
  2173.4 6.5 fusion.168
  2180.7 6.5 fusion.168
  2188.0 6.5 fusion.168
  2195.3 6.5 fusion.168
  2202.6 6.5 fusion.168
  2215.2 153.1 %all-reduce.6 = (f32[8192]{0:T(1024)}, f32[]{:T(128)}, f32[3,576]{1,0:T(4,128)S(1)}) all-reduce(f32[8192]{0:T(1024)} %bitcast.337, f32[]{:T(128)S(6)} %add.304, f32[3,576]{1,0:T(4,128)} %pad_maximum_fusion.6), channel_id=1, replica_groups=mesh['grp'=4,'wide'=32] {'wide'}, use_global_device_ids=true, to_apply=%region_16.17 | all-reduce | flops 9921 | bytes 79368 | tf_op jit(solution)/shard_map/psum | solution.py:302
  2376.9 9.6 fusion.55
  2396.0 40.3 %psum.95 = f32[3,576]{1,0:T(4,128)S(1)} all-reduce(f32[3,576]{1,0:T(4,128)} %get-tuple-element.672), channel_id=1, replica_groups=mesh['grp'=4,'wide'=32] {'grp'}, use_global_device_ids=true, to_apply=%region_45.46 | all-reduce | flops 1728 | bytes 13824 | tf_op jit(solution)/shard_map/psum | solution.py:431
  2439.1 61.6 %all-reduce.14.cloned.1.call-done = (f32[1536,576]{0,1:T(8,128)}, f32[576,30]{0,1:T(8,128)}, f32[576,96]{0,1:T(8,128)}, f32[2112,18]{0,1:T(8,128)}) async-done(((f32[1536,576]{0,1:T(8,128)}, f32[576,30]{0,1:T(8,128)}, f32[576,96]{0,1:T(8,128)}, f32[2112,18]{0,1:T(8,128)}), (f32[1536,576]{0,1:T(8,128)}, f32[576,30]{0,1:T(8,128)}, f32[576,96]{0,1:T(8,128)}, ...) | async-done | bytes 3981328 | tf_op jit(solution)/shard_map/psum | solution.py:431
  2506.5 8.4 multiply_subtract_fusion
  (397 shorter events, 195.0 us)
Async XLA Ops:
  7.2 163.0 %all-gather.14.cloned.1.call-start = ((), (), s32[]{:S(2)}) async-start(), calls=%async_computation.7 | async-start | bytes 1351680 | tf_op jit(solution)/shard_map/all_gather | solution.py:239
  8.8 163.1 %all-gather.16.cloned.1.call-start = ((), (), s32[]{:S(2)}) async-start(), calls=%async_computation.8 | async-start | bytes 3446784 | tf_op jit(solution)/shard_map/all_gather | solution.py:241
  10.4 404.8 %reduce-scatter.3.cloned.1.call-start = ((), (), s32[]{:S(2)}) async-start(), calls=%async_computation.2 | async-start | bytes 9732096 | tf_op jit(solution)/shard_map/reduce_scatter | solution.py:263
  12.7 2.3 copy-start.64
  157.7 9.0 copy-start.43
  166.8 3.3 copy-start.60
  166.8 329.3 %all-gather.8.cloned.1.call-start = ((), (), s32[]{:S(2)}) async-start(), calls=%async_computation.3 | async-start | bytes 4055040 | tf_op jit(solution)/shard_map/all_gather | solution.py:240
  168.4 486.1 %all-gather.10.cloned.1.call-start = ((), (), s32[]{:S(2)}) async-start(), calls=%async_computation.4 | async-start | bytes 9732096 | tf_op jit(solution)/shard_map/all_gather | solution.py:280
  168.5 247.8 %copy-start.48 = (f32[576]{0:T(1024)}, f32[576]{0:T(1024)S(1)}, u32[]{:S(2)}) copy-start(f32[576]{0:T(1024)S(1)} %get-tuple-element.598) | copy-start | bytes 6916
  168.5 327.6 %copy-start.32 = (f32[576]{0:T(1024)}, f32[576]{0:T(1024)S(1)}, u32[]{:S(2)}) copy-start(f32[576]{0:T(1024)S(1)} %get-tuple-element.597) | copy-start | bytes 6916
  168.5 333.2 %copy-start.50 = (f32[576]{0:T(1024)}, f32[576]{0:T(1024)S(1)}, u32[]{:S(2)}) copy-start(f32[576]{0:T(1024)S(1)} %get-tuple-element.596) | copy-start | bytes 6916
  169.4 248.9 %copy-start.25 = (f32[256,64]{0,1:T(8,128)}, f32[256,64]{0,1:T(8,128)S(1)}, u32[]{:S(2)}) copy-start(f32[256,64]{0,1:T(8,128)S(1)} %get-tuple-element.716) | copy-start | bytes 196612
  170.0 248.2 %copy-start.27 = (f32[256,64]{0,1:T(8,128)}, f32[256,64]{0,1:T(8,128)S(1)}, u32[]{:S(2)}) copy-start(f32[256,64]{0,1:T(8,128)S(1)} %get-tuple-element.718) | copy-start | bytes 196612
  171.8 246.1 %copy-start.14 = (bf16[960,576]{1,0:T(8,128)(2,1)}, bf16[960,576]{1,0:T(8,128)(2,1)S(1)}, u32[]{:S(2)}) copy-start(bf16[960,576]{1,0:T(8,128)(2,1)S(1)} %reshape.316) | copy-start | bytes 3317764
  416.3 1.9 copy-start.58
  416.3 1.9 copy-start.54
  418.0 2.0 copy-start.36
  420.0 2.4 copy-start.18
  422.8 77.4 %copy-start.9 = (f32[256,576]{0,1:T(8,128)}, f32[256,576]{0,1:T(8,128)S(1)}, u32[]{:S(2)}) copy-start(f32[256,576]{0,1:T(8,128)S(1)} %get-tuple-element.727) | copy-start | bytes 1769476
  423.4 76.4 %copy-start.46 = (f32[256]{0:T(256)}, f32[256]{0:T(256)S(1)}, u32[]{:S(2)}) copy-start(f32[256]{0:T(256)S(1)} %fusion.121) | copy-start | bytes 3076
  500.3 3.0 copy-start.66
  500.3 80.4 %copy-start.65 = (s32[1,256]{1,0:T(1,128)S(1)}, s32[1,256]{1,0:T(1,128)}, u32[]{:S(2)}) copy-start(s32[1,256]{1,0:T(1,128)} %param.38) | copy-start | bytes 3076
  501.5 166.4 %copy-start.63 = (f32[256]{0:T(256)}, f32[256]{0:T(256)S(1)}, u32[]{:S(2)}) copy-start(f32[256]{0:T(256)S(1)} %get-tuple-element.728) | copy-start | bytes 3076
  503.2 1078.9 %reduce-scatter.5.cloned.1.call-start = ((), (), s32[]{:S(2)}) async-start(), calls=%async_computation.5 | async-start | bytes 19464192 | tf_op jit(solution)/shard_map/reduce_scatter | solution.py:333
  580.7 471.9 %copy-start.40 = (f32[4,2,8,128]{3,1,2,0:T(2,128)}, f32[4,2,8,128]{3,1,2,0:T(2,128)S(1)}, u32[]{:S(2)}) copy-start(f32[4,2,8,128]{3,1,2,0:T(2,128)S(1)} %copy.184) | copy-start | bytes 98308
  654.5 13.4 copy-start.23
  754.1 299.8 %copy-start.44 = (s32[8192]{0:T(1024)}, s32[8192]{0:T(1024)S(1)}, u32[]{:S(2)}) copy-start(s32[8192]{0:T(1024)S(1)} %get-tuple-element.1110) | copy-start | bytes 98308
  1053.9 147.0 %copy-start.3 = (f32[1,1536,576]{1,2,0:T(8,128)S(1)}, f32[1,1536,576]{1,2,0:T(8,128)}, u32[]{:S(2)}) copy-start(f32[1,1536,576]{1,2,0:T(8,128)} %param.41) | copy-start | bytes 10616836
  1060.0 6.6 copy-start.4
  1070.7 1.8 copy-start.5
  1078.3 6.7 copy-start.4
  1096.7 6.7 copy-start.4
  1115.1 6.7 copy-start.4
  1133.4 6.7 copy-start.4
  1144.1 1.8 copy-start.5
  1151.7 6.7 copy-start.4
  1170.1 6.7 copy-start.4
  1180.7 1.8 copy-start.5
  1188.3 6.8 copy-start.4
  1224.1 358.0 %copy-start.51 = (f32[576]{0:T(1024)S(1)}, f32[576]{0:T(1024)}, u32[]{:S(2)}) copy-start(f32[576]{0:T(1024)} %copy-done.50) | copy-start | bytes 6916
  1224.1 789.5 %all-reduce.12.cloned.1.call-start = ((), (), s32[]{:S(2)}) async-start(), calls=%async_computation.9 | async-start | bytes 30670848 | tf_op jit(solution)/shard_map/psum | solution.py:360
  1586.3 4.1 copy-start.2
  1586.3 4.1 copy-start.10
  1586.3 4.1 copy-start.33
  1586.3 4.1 copy-start.47
  1590.5 1.8 copy-start.62
  1592.3 2.2 copy-start.39
  1592.3 2.6 copy-start.1
  1592.5 2.4 copy-start.11
  1592.6 2.9 copy-start.37
  1595.5 11.9 copy-start.34
  1604.0 3.5 copy-start.24
  1604.0 3.4 copy-start.41
  1604.0 4.1 copy-start.16
  1604.0 4.1 copy-start.49
  1604.0 4.1 copy-start.55
  1610.2 8.5 copy-start.56
  1610.2 526.5 %all-gather.12.cloned.1.call-start = ((), (), s32[]{:S(2)}) async-start(), calls=%async_computation.6 | async-start | bytes 9732096 | tf_op jit(solution)/shard_map/all_gather | solution.py:342
  1610.3 3.0 copy-start.59
  1610.3 3.0 copy-start.12
  1610.3 3.0 copy-start.17
  1614.2 886.5 %all-reduce.14.cloned.1.call-start = ((), (), s32[]{:S(2)}) async-start(), calls=%async_computation.10 | async-start | bytes 8151040 | tf_op jit(solution)/shard_map/psum | solution.py:431
  2370.3 6.6 copy-start.6
  2386.6 119.9 %copy-start.7 = (f32[1536,576]{0,1:T(8,128)S(1)}, f32[1536,576]{0,1:T(8,128)}, u32[]{:S(2)}) copy-start(f32[1536,576]{0,1:T(8,128)} %param.44) | copy-start | bytes 10616836
  (26 other events, 32.8 us)
Sparse Core Ops, SparseCore 0:
  11.8 69.5 all-gather.13
  85.1 74.0 all-gather.15
  166.9 248.2 reduce-scatter.2
  419.1 76.8 all-gather.7
  503.3 104.7 all-gather.9
  1224.3 357.7 reduce-scatter.4
  1610.3 403.2 all-reduce.11
  2017.3 119.3 all-gather.11
  2386.7 113.9 all-reduce.13
where the time goes:
time: 2540 us; the launch traced here: 2520 us
  waiting for transfers between devices  1240 us (49%)
  blocking collectives  725 us (29%)
  matrix products  260 us (10%)
  local copies, waits for them, and re-layouts  133 us (5%)
  other arithmetic  92.8 us (4%)
  loops' own time  48.4 us (2%)
    psum x1, waiting for transfers between devices, on_device(): lax.psum((grad_attn, grad_ffn, grad_proj, grad_gains), 'wide')  394 us
    reduce_scatter x1, waiting for transfers between devices, on_device(): lax.psum_scatter(jnp.dot(kept_logits, table_low, preferred_element_type=j...  357 us
    psum x2, blocking collectives, on_device(): lax.psum((expsums * jnp.exp(peaks - peak), pickeds), 'wide')  301 us
    reduce_scatter x1, waiting for transfers between devices, on_device(): lax.psum_scatter(lax.map(one_block, jnp.arange(number) * embed_size).resh...  238 us
    pmax x1, blocking collectives, on_device(): peak = lax.pmax(peaks, 'wide')  150 us
    all_gather x1, waiting for transfers between devices, on_device(): lax.all_gather(grad_hidden0.astype(jnp.bfloat16), 'wide', axis=0, tiled=T...  118 us
    dot_general x16, matrix products, logits_at(): jnp.einsum('td,vd->tv', rows_blk, table_low, preferred_element_type=jnp.f...  85.8 us
    all_gather x1, blocking collectives, on_device(): lax.all_gather(token_ids, 'wide', axis=1, tiled=True)  83.1 us
  transfers between devices with their start and end apart: 9, of which 6 were waited for; matrix products, arithmetic and copies ran while one was open for 4% of the time, Pallas kernels for 0%

commit v1 on v0

v1 whole, which is shorter than its diff:
```python
import functools

import jax
import jax.numpy as jnp
from jax import lax
from jax.experimental import pallas as pl
from jax.experimental.pallas import tpu as pltpu
from jax.sharding import PartitionSpec as P

D = 576
H = 9
KVH = 3
HD = 64
FF = 1536
QKV = 960
STEP = 8
T = 256
SHARD = 1536
NW = 32
NG = 4
CAP = 32
FA_ROWS = 128
WP_ROWS = 320

beta_one = 0.9
beta_two = 0.999
adam_eps = 1e-08
weight_decay = 0.1
inner_rate = 0.02
gain_rate = 0.2
clip_norm = 0.01
penalty_weight = 0.005
outer_rate = 0.7
outer_momentum = 0.9
rope_base = 100000.0
norm_eps = 1e-05
masked_score = -1e30

BF = jnp.bfloat16
F32 = jnp.float32
MESH = pl.DeviceIdType.MESH
VMEM = pl.BlockSpec(memory_space=pltpu.VMEM)
ANY = pl.BlockSpec(memory_space=pl.ANY)
DMA = pltpu.SemaphoreType.DMA
MIB = 1 << 20


def params(collective, mib):
    return pltpu.CompilerParams(
        collective_id=collective, has_side_effects=True, vmem_limit_bytes=mib * MIB
    )


def place():
    me = lax.axis_index("wide")
    return me, me // 8, lax.rem(me // 4, 2), lax.rem(me, 4)


def flat(y, xh, z):
    return y * 8 + xh * 4 + z


def turn4(at, by):
    return lax.rem(at + by, 4)


def remote(src, dst, ssem, rsem, **device):
    return pltpu.make_async_remote_copy(
        src_ref=src,
        dst_ref=dst,
        send_sem=ssem,
        recv_sem=rsem,
        device_id=device,
        device_id_type=MESH,
    )


def greet_wide(me, grp=None):
    barrier = pltpu.get_barrier_semaphore()

    def one(k, carry):
        pl.semaphore_signal(
            barrier, inc=1, device_id={"wide": lax.rem(me + k, NW)}, device_id_type=MESH
        )
        return carry

    lax.fori_loop(1, NW, one, 0)
    count = NW - 1
    if grp is not None:
        for k in range(1, NG):
            pl.semaphore_signal(
                barrier, inc=1, device_id={"grp": lax.rem(grp + k, NG)}, device_id_type=MESH
            )
        count += NG - 1
    pl.semaphore_wait(barrier, count)


class Scatter:
    def __init__(self, src_at, dst_at, ssem, rsem, me):
        self.src_at, self.dst_at, self.ssem, self.rsem, self.me = src_at, dst_at, ssem, rsem, me

    def copy(self, k):
        peer = lax.rem(self.me + k, NW)
        return remote(
            self.src_at(peer), self.dst_at(self.me), self.ssem.at[k], self.rsem.at[self.me], wide=peer
        )

    def start(self):
        def one(k, carry):
            self.copy(k).start()
            return carry

        lax.fori_loop(1, NW, one, 0)

    def wait_recv(self):
        def one(k, carry):
            peer = lax.rem(self.me + k, NW)
            remote(
                self.src_at(peer), self.dst_at(peer), self.ssem.at[k], self.rsem.at[peer], wide=peer
            ).wait_recv()
            return carry

        lax.fori_loop(1, NW, one, 0)

    def wait_send(self):
        def one(k, carry):
            self.copy(k).wait_send()
            return carry

        lax.fori_loop(1, NW, one, 0)


class Gather:
    def __init__(self, x, out, rows, ssem, rsem, lsem):
        self.x, self.out, self.half = x, out, rows // 2
        self.ssem, self.rsem, self.lsem = ssem, rsem, lsem
        self.me, self.y, self.xh, self.z = place()
        self.used = 0
        self.sent = []

    def send(self, src, dst, rsem, peer):
        copy = remote(src, dst, self.ssem.at[self.used], rsem, wide=peer)
        self.used += 1
        copy.start()
        self.sent.append(copy)

    def rows(self, part):
        return pl.ds(part * self.half, self.half)

    def wait(self, block, part=None):
        dst = self.out.at[block] if part is None else self.out.at[block, self.rows(part)]
        remote(
            dst, dst, self.ssem.at[0], self.rsem.at[block, 0 if part is None else part], wide=block
        ).wait_recv()

    def whole(self, src, block):
        y, xh, z = self.y, self.xh, self.z
        for k in (1, 3, 2):
            self.send(src, self.out.at[block], self.rsem.at[block, 0], flat(turn4(y, k), xh, z))
            self.send(src, self.out.at[block], self.rsem.at[block, 0], flat(y, xh, turn4(z, k)))

    def start(self):
        other = flat(self.y, 1 - self.xh, self.z)
        self.send(self.x, self.out.at[self.me], self.rsem.at[self.me, 0], other)
        self.local = pltpu.make_async_copy(self.x, self.out.at[self.me], self.lsem)
        self.local.start()
        self.whole(self.x, self.me)

    def second(self):
        other = flat(self.y, 1 - self.xh, self.z)
        self.wait(other)
        self.whole(self.out.at[other], other)

    def third(self, xh):
        y, z = self.y, self.z
        for k in (1, 3, 2):
            block = flat(turn4(y, k), xh, z)
            self.wait(block)
            for m in (1, 3, 2):
                piece = self.out.at[block, self.rows(0)]
                self.send(piece, piece, self.rsem.at[block, 0], flat(y, self.xh, turn4(z, m)))
            block = flat(y, xh, turn4(z, k))
            self.wait(block)
            for m in (1, 3, 2):
                piece = self.out.at[block, self.rows(1)]
                self.send(piece, piece, self.rsem.at[block, 1], flat(turn4(y, m), self.xh, z))

    def finish(self):
        for xh in (self.xh, 1 - self.xh):
            for k in (1, 2, 3):
                for m in (1, 2, 3):
                    block = flat(turn4(self.y, k), xh, turn4(self.z, m))
                    self.wait(block, 0)
                    self.wait(block, 1)
        for copy in self.sent:
            copy.wait_send()
        self.local.wait()


GATHER_SENDS = 1 + 12 + 36


def look_up(got, table, hot, rows, slot_row):
    asked = got[:, slot_row, :].astype(F32)
    asked = jnp.concatenate([asked, jnp.zeros((128 - NW, 128), F32)], 0).T
    step = 8 * CAP
    for first in range(0, NW, 8):
        for d in range(8):
            column = asked[0:CAP, first + d : first + d + 1]
            lanes = lax.broadcasted_iota(jnp.int32, (CAP, SHARD), 1).astype(F32)
            hot[d * CAP : (d + 1) * CAP, :] = jnp.where(lanes == column, 1.0, 0.0).astype(BF)
        picked = lax.dot_general(
            hot[...], table[...], (((1,), (1,)), ((), ())), preferred_element_type=F32
        )
        rows[first * CAP : first * CAP + step, :] = picked.astype(BF)


def slots(at):
    return pl.ds(pl.multiple_of(at * CAP, CAP), CAP)


def front_kernel(
    msg, table, fa, wp, got, emb, most, table_other, fa_all, wp_all,
    hot, rows, own_most, msg_s, msg_r, emb_s, emb_r, most_s, most_r, swap, fa_s, fa_r, wp_s, wp_r, local,
):
    me, y, xh, z = place()
    grp = lax.axis_index("grp")
    greet_wide(me, grp)
    ask = Scatter(lambda p: msg.at[p], lambda p: got.at[p], msg_s, msg_r, me)
    ask.start()
    got[me] = msg[me]
    gather_fa = Gather(fa, fa_all, FA_ROWS, fa_s, fa_r, local.at[0])
    gather_wp = Gather(wp, wp_all, WP_ROWS, wp_s, wp_r, local.at[1])
    gather_fa.start()
    gather_wp.start()
    trade = remote(table, table_other, swap.at[0], swap.at[1], wide=flat(y, 1 - xh, z))
    trade.start()
    ask.wait_recv()
    look_up(got, table, hot, rows, 0)
    reply = Scatter(lambda p: rows.at[slots(p)], lambda p: emb.at[slots(p)], emb_s, emb_r, me)
    reply.start()
    emb[slots(me), :] = rows[slots(me), :]
    largest = jnp.max(got[:, 4, :], 0, keepdims=True)
    own_most[...] = jnp.broadcast_to(largest, (8, 128))
    most[grp] = own_most[...]
    told = []
    for k in range(1, NG):
        other = lax.rem(grp + k, NG)
        told.append(remote(own_most, most.at[grp], most_s.at[k], most_r.at[grp], grp=other))
        told[-1].start()
    gather_fa.second()
    gather_wp.second()
    for side in (xh, 1 - xh):
        gather_fa.third(side)
        gather_wp.third(side)
    reply.wait_recv()
    for k in range(1, NG):
        other = lax.rem(grp + k, NG)
        remote(own_most, most.at[other], most_s.at[k], most_r.at[other], grp=other).wait_recv()
    ask.wait_send()
    reply.wait_send()
    for copy in told:
        copy.wait_send()
    gather_fa.finish()
    gather_wp.finish()
    trade.wait()


def front(msg, table, fa, wp):
    return pl.pallas_call(
        front_kernel,
        name="front",
        out_shape=(
            jax.ShapeDtypeStruct((NW, 8, 128), jnp.int32),
            jax.ShapeDtypeStruct((NW * CAP, D), BF),
            jax.ShapeDtypeStruct((NG, 8, 128), jnp.int32),
            jax.ShapeDtypeStruct((D, SHARD), BF),
            jax.ShapeDtypeStruct((NW, FA_ROWS, D), BF),
            jax.ShapeDtypeStruct((NW, WP_ROWS, 128), BF),
        ),
        in_specs=[VMEM, VMEM, ANY, ANY],
        out_specs=(VMEM, VMEM, VMEM, ANY, ANY, ANY),
        scratch_shapes=[
            pltpu.VMEM((8 * CAP, SHARD), BF),
            pltpu.VMEM((NW * CAP, D), BF),
            pltpu.VMEM((8, 128), jnp.int32),
            DMA((NW,)),
            DMA((NW,)),
            DMA((NW,)),
            DMA((NW,)),
            DMA((NG,)),
            DMA((NG,)),
            DMA((2,)),
            DMA((GATHER_SENDS,)),
            DMA((NW, 2)),
            DMA((GATHER_SENDS,)),
            DMA((NW, 2)),
            DMA((2,)),
        ],
        compiler_params=params(1, 40),
        cost_estimate=pl.CostEstimate(flops=2 * 10**9, bytes_accessed=3 * 10**7, transcendentals=0),
    )(msg, table, fa, wp)


def more_rows_kernel(msg, table, got, emb, hot, rows, msg_s, msg_r, emb_s, emb_r):
    me = lax.axis_index("wide")
    greet_wide(me)
    ask = Scatter(lambda p: msg.at[p], lambda p: got.at[p], msg_s, msg_r, me)
    ask.start()
    got[me] = msg[me]
    ask.wait_recv()
    look_up(got, table, hot, rows, 0)
    reply = Scatter(lambda p: rows.at[slots(p)], lambda p: emb.at[slots(p)], emb_s, emb_r, me)
    reply.start()
    emb[slots(me), :] = rows[slots(me), :]
    reply.wait_recv()
    ask.wait_send()
    reply.wait_send()


def more_rows(msg, table):
    return pl.pallas_call(
        more_rows_kernel,
        name="more_rows",
        out_shape=(
            jax.ShapeDtypeStruct((NW, 8, 128), jnp.int32),
            jax.ShapeDtypeStruct((NW * CAP, D), BF),
        ),
        in_specs=[VMEM, VMEM],
        out_specs=(VMEM, VMEM),
        scratch_shapes=[pltpu.VMEM((8 * CAP, SHARD), BF), pltpu.VMEM((NW * CAP, D), BF)]
        + [DMA((NW,))] * 4,
        compiler_params=params(2, 40),
    )(msg, table)[1]


def more_grads_kernel(msg, rows, got, out, msg_s, msg_r, row_s, row_r):
    me = lax.axis_index("wide")
    greet_wide(me)
    ask = Scatter(lambda p: msg.at[p], lambda p: got.at[p], msg_s, msg_r, me)
    ask.start()
    give = Scatter(lambda p: rows.at[slots(p)], lambda p: out.at[slots(p)], row_s, row_r, me)
    give.start()
    got[me] = msg[me]
    out[slots(me), :] = rows[slots(me), :]
    ask.wait_recv()
    give.wait_recv()
    ask.wait_send()
    give.wait_send()


def more_grads(msg, rows):
    return pl.pallas_call(
        more_grads_kernel,
        name="more_grads",
        out_shape=(
            jax.ShapeDtypeStruct((NW, 8, 128), jnp.int32),
            jax.ShapeDtypeStruct((NW * CAP, D), BF),
        ),
        in_specs=[VMEM, VMEM],
        out_specs=(VMEM, VMEM),
        scratch_shapes=[DMA((NW,))] * 4,
        compiler_params=params(3, 20),
    )(msg, rows)


VOC = 2 * SHARD
TOK = 16 * T
CH = 512
NCH = VOC // CH
HALF = D // 2


def cols(j):
    return pl.ds(pl.multiple_of(j * T, T), T)


def head_kernel(
    final, rows_t, table, table_other, goal, weights,
    grad_final, head_own, head_other, loss,
    fall, expo, tops, stat, stat_in, coef, coef_in, parts, in_a, in_b, sum_a, sum_b, in_a2, in_b2,
    g_s, g_r, st_s, st_r, co_s, co_r, a_s, a_r, b_s, b_r, a2_s, a2_r, b2_s, b2_r,
):
    me, y, xh, z = place()
    mine = y * 4 + z

    def dev(j):
        return flat(j // 4, xh, lax.rem(j, 4))

    barrier = pltpu.get_barrier_semaphore()

    def greet(k, carry):
        pl.semaphore_signal(
            barrier, inc=1, device_id={"wide": dev(lax.rem(mine + k, 16))}, device_id_type=MESH
        )
        return carry

    lax.fori_loop(1, 16, greet, 0)
    pl.semaphore_wait(barrier, 15)

    upper, lower = pl.ds(0, HALF), pl.ds(HALF, HALF)
    sent = []

    def send(src, dst, ssem, rsem, to):
        copy = remote(src, dst, ssem, rsem, wide=to)
        copy.start()
        sent.append(copy)

    def arrived(dst, rsem):
        remote(dst, dst, g_s.at[0], rsem, wide=dev(mine)).wait_recv()

    fall[:, cols(mine)] = final[...]
    used = 0
    for k in (1, 3, 2):
        for to in (flat(turn4(y, k), xh, z), flat(y, xh, turn4(z, k))):
            send(final, fall.at[:, cols(mine)], g_s.at[used], g_r.at[mine, 0], to)
            used += 1

    def logits(j):
        seen = fall[:, cols(j)]
        goals = goal[j, 0:1, :]
        tip, weight, hit = [], [], jnp.zeros((1, T), F32)
        for c in range(NCH):
            part = jnp.dot(rows_t[c * CH : (c + 1) * CH, :], seen, preferred_element_type=F32)
            top = jnp.max(part, 0, keepdims=True)
            power = jnp.exp(part - top)
            spot = lax.broadcasted_iota(jnp.int32, (CH, T), 0) + c * CH
            hit = hit + jnp.sum(jnp.where(spot == goals, part, 0.0), 0, keepdims=True)
            expo[c * CH : (c + 1) * CH, cols(j)] = power.astype(BF)
            tip.append(top)
            weight.append(jnp.sum(power, 0, keepdims=True))
        top = functools.reduce(jnp.maximum, tip)
        total = sum(w * jnp.exp(t - top) for w, t in zip(weight, tip))
        zero = jnp.zeros((1, T), F32)
        tops[j] = jnp.concatenate(tip + [zero] * (8 - NCH), 0)
        stat[j] = jnp.concatenate([top, total, hit] + [zero] * 5, 0)

    logits(mine)
    for k in (1, 3, 2):
        row, column = turn4(y, k), turn4(z, k)
        block = row * 4 + z
        arrived(fall.at[:, cols(block)], g_r.at[block, 0])
        for m in (1, 3, 2):
            piece = fall.at[upper, cols(block)]
            send(piece, piece, g_s.at[used], g_r.at[block, 0], flat(y, xh, turn4(z, m)))
            used += 1
        block = y * 4 + column
        arrived(fall.at[:, cols(block)], g_r.at[block, 0])
        for m in (1, 3, 2):
            piece = fall.at[lower, cols(block)]
            send(piece, piece, g_s.at[used], g_r.at[block, 1], flat(turn4(y, m), xh, z))
            used += 1

    def tell(j):
        return remote(stat.at[j], stat_in.at[mine], st_s.at[j], st_r.at[mine], wide=dev(j))

    def block_at(k):
        return turn4(y, k // 4) * 4 + turn4(z, lax.rem(k, 4))

    def forward(k, carry):
        j = block_at(k)
        dy, dz = k // 4, lax.rem(k, 4)

        @pl.when((dy > 0) & (dz > 0))
        def _():
            arrived(fall.at[upper, cols(j)], g_r.at[j, 0])
            arrived(fall.at[lower, cols(j)], g_r.at[j, 1])

        logits(j)
        tell(j).start()
        return carry

    stat_in[mine] = stat[mine]
    lax.fori_loop(1, 16, forward, 0)

    def hear(k, carry):
        j = lax.rem(mine + k, 16)
        arrived(stat_in.at[j], st_r.at[j])
        return carry

    lax.fori_loop(1, 16, hear, 0)
    tip, weight, hit = stat_in[:, 0, :], stat_in[:, 1, :], stat_in[:, 2, :]
    top = jnp.max(tip, 0, keepdims=True)
    lse = top + jnp.log(jnp.sum(weight * jnp.exp(tip - top), 0, keepdims=True))
    picked = jnp.sum(hit, 0, keepdims=True)
    share, plain = weights[0:1, :], weights[1:2, :]
    zero = jnp.zeros((1, T), F32)
    coef[...] = jnp.concatenate(
        [lse, share * (1.0 + 2.0 * penalty_weight * lse), share] + [zero] * 5, 0
    )
    loss[...] = jnp.concatenate(
        [plain * (lse - picked + penalty_weight * lse * lse)] + [zero] * 7, 0
    )
    coef_in[mine] = coef[...]

    def spread(k):
        j = lax.rem(mine + k, 16)
        return remote(coef, coef_in.at[mine], co_s.at[k], co_r.at[mine], wide=dev(j))

    def spread_start(k, carry):
        spread(k).start()
        return carry

    lax.fori_loop(1, 16, spread_start, 0)

    def piece_a(dz, row):
        return remote(
            parts.at[row * 4 + turn4(z, dz), upper],
            in_a.at[dz - 1, row],
            a_s.at[dz - 1, row],
            a_r.at[dz - 1, row],
            wide=flat(y, xh, turn4(z, dz)),
        )

    def piece_b(dy, column):
        return remote(
            parts.at[turn4(y, dy) * 4 + column, lower],
            in_b.at[dy - 1, column],
            b_s.at[dy - 1, column],
            b_r.at[dy - 1, column],
            wide=flat(turn4(y, dy), xh, z),
        )

    def backward(k, carry):
        j = block_at(15 - k)
        dy, dz = (15 - k) // 4, lax.rem(15 - k, 4)

        @pl.when(k < 15)
        def _():
            arrived(coef_in.at[j], co_r.at[j])

        lse, soft, pick = coef_in[j, 0:1, :], coef_in[j, 1:2, :], coef_in[j, 2:3, :]
        goals = goal[j, 0:1, :]
        for c in range(NCH):
            scale = soft * jnp.exp(tops[j, c : c + 1, :] - lse)
            power = expo[c * CH : (c + 1) * CH, cols(j)].astype(F32)
            spot = lax.broadcasted_iota(jnp.int32, (CH, T), 0) + c * CH
            grad = power * scale - jnp.where(spot == goals, pick, 0.0)
            expo[c * CH : (c + 1) * CH, cols(j)] = grad.astype(BF)
        product = jnp.dot(table[...], expo[0:SHARD, cols(j)], preferred_element_type=F32)
        product += jnp.dot(table_other[...], expo[SHARD:VOC, cols(j)], preferred_element_type=F32)
        parts[j] = product.astype(BF)

        @pl.when(dz > 0)
        def _():
            piece_a(dz, j // 4).start()

        @pl.when(dy > 0)
        def _():
            piece_b(dy, lax.rem(j, 4)).start()

        return carry

    lax.fori_loop(0, 16, backward, 0)

    def head_chunk(c):
        return lax.dot_general(
            fall[...],
            expo[pl.ds(pl.multiple_of(c * 256, 256), 256), :],
            (((1,), (1,)), ((), ())),
            preferred_element_type=F32,
        )

    def other_chunk(c, carry):
        head_other[:, cols(c)] = head_chunk(c + SHARD // 256).astype(BF)
        return carry

    lax.fori_loop(0, SHARD // 256, other_chunk, 0)

    keep_a = keep_b = None
    for d in (3, 2, 1, 0):
        row = turn4(y, d)
        acc = parts[row * 4 + z, 0:HALF, :].astype(F32)
        for m in (1, 2, 3):
            arrived(in_a.at[m - 1, row], a_r.at[m - 1, row])
            acc = acc + in_a[m - 1, row].astype(F32)
        if d:
            sum_a[d - 1] = acc.astype(BF)
            send(sum_a.at[d - 1], in_a2.at[d - 1], a2_s.at[d - 1], a2_r.at[d - 1], flat(row, xh, z))
        else:
            keep_a = acc
        column = turn4(z, d)
        acc = parts[y * 4 + column, HALF:D, :].astype(F32)
        for m in (1, 2, 3):
            arrived(in_b.at[m - 1, column], b_r.at[m - 1, column])
            acc = acc + in_b[m - 1, column].astype(F32)
        if d:
            sum_b[d - 1] = acc.astype(BF)
            send(sum_b.at[d - 1], in_b2.at[d - 1], b2_s.at[d - 1], b2_r.at[d - 1], flat(y, xh, column))
        else:
            keep_b = acc
    grad_final[0:HALF, :] = keep_a
    grad_final[HALF:D, :] = keep_b

    def own_chunk(c, carry):
        head_own[:, cols(c)] = head_chunk(c)
        return carry

    lax.fori_loop(0, SHARD // 256, own_chunk, 0)
    for d in (1, 2, 3):
        arrived(in_a2.at[d - 1], a2_r.at[d - 1])
        arrived(in_b2.at[d - 1], b2_r.at[d - 1])
    grad_final[0:HALF, :] += sum(in_a2[d].astype(F32) for d in range(3))
    grad_final[HALF:D, :] += sum(in_b2[d].astype(F32) for d in range(3))

    def finish(k, carry):
        tell(block_at(k)).wait_send()
        spread(k).wait_send()
        return carry

    lax.fori_loop(1, 16, finish, 0)
    for copy in sent:
        copy.wait_send()

    def finish_pieces(k, carry):
        piece_a(k // 4 + 1, lax.rem(k, 4)).wait_send()
        piece_b(k // 4 + 1, lax.rem(k, 4)).wait_send()
        return carry

    lax.fori_loop(0, 12, finish_pieces, 0)


def head(final, rows_t, table, table_other, goal, weights):
    return pl.pallas_call(
        head_kernel,
        name="head",
        out_shape=(
            jax.ShapeDtypeStruct((D, T), F32),
            jax.ShapeDtypeStruct((D, SHARD), F32),
            jax.ShapeDtypeStruct((D, SHARD), BF),
            jax.ShapeDtypeStruct((8, T), F32),
        ),
        in_specs=[VMEM] * 6,
        out_specs=(VMEM,) * 4,
        scratch_shapes=[
            pltpu.VMEM((D, TOK), BF),
            pltpu.VMEM((VOC, TOK), BF),
            pltpu.VMEM((16, 8, T), F32),
            pltpu.VMEM((16, 8, T), F32),
            pltpu.VMEM((16, 8, T), F32),
            pltpu.VMEM((8, T), F32),
            pltpu.VMEM((16, 8, T), F32),
            pltpu.VMEM((16, D, T), BF),
            pltpu.VMEM((3, 4, HALF, T), BF),
            pltpu.VMEM((3, 4, HALF, T), BF),
            pltpu.VMEM((3, HALF, T), BF),
            pltpu.VMEM((3, HALF, T), BF),
            pltpu.VMEM((3, HALF, T), BF),
            pltpu.VMEM((3, HALF, T), BF),
            DMA((24,)),
            DMA((16, 2)),
            DMA((16,)),
            DMA((16,)),
            DMA((16,)),
            DMA((16,)),
            DMA((3, 4)),
            DMA((3, 4)),
            DMA((3, 4)),
            DMA((3, 4)),
            DMA((3,)),
            DMA((3,)),
            DMA((3,)),
            DMA((3,)),
        ],
        compiler_params=params(4, 61),
        cost_estimate=pl.CostEstimate(
            flops=6 * VOC * TOK * D, bytes_accessed=2 * 10**7, transcendentals=VOC * TOK
        ),
    )(final, rows_t, table, table_other, goal, weights)


class Reduce:
    def __init__(self, parts, first, first_in, second, second_in, third, third_in, rows, along_z, sems):
        self.parts, self.first, self.first_in = parts, first, first_in
        self.second, self.second_in = second, second_in
        self.third, self.third_in = third, third_in
        self.rows, self.along_z = rows, along_z
        self.s, self.r = sems
        self.me, self.y, self.xh, self.z = place()
        self.sent = []

    def send(self, src, dst, at, to):
        copy = remote(src, dst, self.s.at[at], self.r.at[at], wide=to)
        copy.start()
        self.sent.append(copy)

    def wait(self, dst, at):
        remote(dst, dst, self.s.at[at], self.r.at[at], wide=self.me).wait_recv()

    def one(self, d):
        if self.along_z:
            at = turn4(self.z, d)
            return flat(self.y, self.xh, at), (slice(None), slice(None), at, self.rows)
        at = turn4(self.y, d)
        return flat(at, self.xh, self.z), (at, slice(None), slice(None), self.rows)

    def start(self):
        for d in (2, 1, 3):
            to, index = self.one(d)
            self.send(self.parts.at[index], self.first_in.at[d - 1], d - 1, to)

    def middle(self):
        _, index = self.one(0)
        for d in (1, 2, 3):
            self.wait(self.first_in.at[d - 1], d - 1)
        acc = self.parts[index].astype(F32)
        for d in (1, 2, 3):
            acc = acc + self.first_in[d - 1].astype(F32)
        self.first[...] = acc.astype(BF)
        for d in (2, 1, 3):
            if self.along_z:
                at = turn4(self.y, d)
                src, to = self.first.at[at], flat(at, self.xh, self.z)
            else:
                at = turn4(self.z, d)
                src, to = self.first.at[:, at], flat(self.y, self.xh, at)
            self.send(src, self.second_in.at[d - 1], 2 + d, to)

    def last(self):
        for d in (1, 2, 3):
            self.wait(self.second_in.at[d - 1], 2 + d)
        own = self.first[self.y] if self.along_z else self.first[:, self.z]
        acc = own.astype(F32)
        for d in (1, 2, 3):
            acc = acc + self.second_in[d - 1].astype(F32)
        self.second[...] = acc
        self.third[...] = self.second[1 - self.xh].astype(BF)
        self.send(self.third, self.third_in, 6, flat(self.y, 1 - self.xh, self.z))

    def total(self):
        self.wait(self.third_in, 6)
        return self.second[self.xh] + self.third_in[...].astype(F32)

    def finish(self):
        for copy in self.sent:
            copy.wait_send()


def reduce_scratch(half, lanes):
    shapes = []
    for group in ((4, 2), (2, 4)):
        shapes += [
            pltpu.VMEM(group + (half, lanes), BF),
            pltpu.VMEM((3,) + group + (half, lanes), BF),
            pltpu.VMEM((2, half, lanes), F32),
            pltpu.VMEM((3, 2, half, lanes), BF),
            pltpu.VMEM((half, lanes), BF),
            pltpu.VMEM((half, lanes), BF),
            DMA((7,)),
            DMA((7,)),
        ]
    return shapes


def back_kernel(fa, wp, rows, head_other, extra, fa_sum, wp_sum, rows_in, head_in, extra_sum, *scratch):
    me, y, xh, z = place()
    greet_wide(me)
    streams = []
    for parts, rows_of, at in ((fa, FA_ROWS, 0), (wp, WP_ROWS, 16)):
        for half in range(2):
            base = at + half * 8
            f, f_in, s, s_in, t, t_in, sends, recvs = scratch[base : base + 8]
            streams.append(
                Reduce(
                    parts, f, f_in, s, s_in, t, t_in,
                    pl.ds(half * rows_of // 2, rows_of // 2), half == 0, (sends, recvs),
                )
            )
    extra_in, row_s, row_r, extra_s, extra_r, swap = scratch[32:]
    for stream in streams:
        stream.start()
    give = Scatter(lambda p: rows.at[slots(p)], lambda p: rows_in.at[slots(p)], row_s, row_r, me)
    give.start()
    share = Scatter(lambda p: extra, lambda p: extra_in.at[p], extra_s, extra_r, me)
    share.start()
    trade = remote(head_other, head_in, swap.at[0], swap.at[1], wide=flat(y, 1 - xh, z))
    trade.start()
    rows_in[slots(me), :] = rows[slots(me), :]
    extra_in[me] = extra[...]
    for stream in streams:
        stream.middle()
    for stream in streams:
        stream.last()
    share.wait_recv()
    total = extra_in[0]
    for w in range(1, NW):
        total = total + extra_in[w]
    extra_sum[...] = total
    for out, pair, half in ((fa_sum, streams[:2], FA_ROWS // 2), (wp_sum, streams[2:], WP_ROWS // 2)):
        out[0:half, :] = pair[0].total()
        out[half : 2 * half, :] = pair[1].total()
    give.wait_recv()
    for stream in streams:
        stream.finish()
    give.wait_send()
    share.wait_send()
    trade.wait()


def back(fa, wp, rows, head_other, extra):
    return pl.pallas_call(
        back_kernel,
        name="back",
        out_shape=(
            jax.ShapeDtypeStruct((FA_ROWS, D), F32),
            jax.ShapeDtypeStruct((WP_ROWS, 128), F32),
            jax.ShapeDtypeStruct((NW * CAP, D), BF),
            jax.ShapeDtypeStruct((D, SHARD), BF),
            jax.ShapeDtypeStruct((8, 640), F32),
        ),
        in_specs=[VMEM, VMEM, VMEM, ANY, VMEM],
        out_specs=(VMEM, VMEM, VMEM, ANY, VMEM),
        scratch_shapes=reduce_scratch(FA_ROWS // 2, D)
        + reduce_scratch(WP_ROWS // 2, 128)
        + [pltpu.VMEM((NW, 8, 640), F32)]
        + [DMA((NW,))] * 4
        + [DMA((2,))],
        compiler_params=params(5, 48),
        cost_estimate=pl.CostEstimate(flops=10**8, bytes_accessed=3 * 10**7, transcendentals=0),
    )(fa, wp, rows, head_other, extra)


def norm_kernel(value, out, landing, s, r):
    me = lax.axis_index("wide")
    greet_wide(me)
    share = Scatter(lambda p: value, lambda p: landing.at[p], s, r, me)
    share.start()
    landing[me] = value[...]
    share.wait_recv()
    total = landing[0]
    for w in range(1, NW):
        total = total + landing[w]
    out[...] = total
    share.wait_send()


def norm_sum(value):
    return pl.pallas_call(
        norm_kernel,
        name="norm_sum",
        out_shape=jax.ShapeDtypeStruct((8, 128), F32),
        in_specs=[VMEM],
        out_specs=VMEM,
        scratch_shapes=[pltpu.VMEM((NW, 8, 128), F32), DMA((NW,)), DMA((NW,))],
        compiler_params=params(6, 16),
    )(value)


GRP_PARTS = ((D, SHARD), (FA_ROWS, D), (WP_ROWS, 128))


def group_kernel(*refs):
    values, gains = refs[0:3], refs[3]
    outs, gains_out = refs[4:7], refs[7]
    scratch = refs[8:]
    grp = lax.axis_index("grp")
    core, x = lax.rem(grp, 2), grp // 2
    near, far = x * 2 + 1 - core, (1 - x) * 2 + core
    barrier = pltpu.get_barrier_semaphore()
    for k in range(1, NG):
        pl.semaphore_signal(
            barrier, inc=1, device_id={"grp": lax.rem(grp + k, NG)}, device_id_type=MESH
        )
    pl.semaphore_wait(barrier, NG - 1)
    gains_in, gains_s, gains_r = scratch[15:18]
    told = []
    for k in range(1, NG):
        to = lax.rem(grp + k, NG)
        told.append(remote(gains, gains_in.at[grp], gains_s.at[k], gains_r.at[grp], grp=to))
        told[-1].start()
    gains_in[grp] = gains[...]
    sent = []
    for i, value in enumerate(values):
        half = value.shape[0] // 2
        one, one_in, two, two_in, sems = scratch[5 * i : 5 * i + 5]
        away = pl.ds(pl.multiple_of((1 - core) * half, 16), half)
        one[...] = value[away, :].astype(BF)
        copy = remote(one, one_in, sems.at[0], sems.at[1], grp=near)
        copy.start()
        sent.append(copy)
    for i, value in enumerate(values):
        half = value.shape[0] // 2
        one, one_in, two, two_in, sems = scratch[5 * i : 5 * i + 5]
        kept = pl.ds(pl.multiple_of(core * half, 16), half)
        sent[i].wait_recv()
        two[...] = (value[kept, :] + one_in[...].astype(F32)).astype(BF)
        copy = remote(two, two_in, sems.at[2], sems.at[3], grp=far)
        copy.start()
        sent.append(copy)
    for i, value in enumerate(values):
        half = value.shape[0] // 2
        one, one_in, two, two_in, sems = scratch[5 * i : 5 * i + 5]
        kept = pl.ds(pl.multiple_of(core * half, 16), half)
        sent[3 + i].wait_recv()
        outs[i][kept, :] = two[...].astype(F32) + two_in[...].astype(F32)
        piece = outs[i].at[kept]
        copy = remote(piece, piece, sems.at[4], sems.at[5], grp=near)
        copy.start()
        sent.append(copy)
    for k in range(1, NG):
        other = lax.rem(grp + k, NG)
        remote(gains, gains_in.at[other], gains_s.at[k], gains_r.at[other], grp=other).wait_recv()
    gains_out[...] = (gains_in[0] + gains_in[1]) + (gains_in[2] + gains_in[3])
    for i, value in enumerate(values):
        half = value.shape[0] // 2
        sems = scratch[5 * i + 4]
        away = outs[i].at[pl.ds(pl.multiple_of((1 - core) * half, 16), half)]
        remote(away, away, sems.at[4], sems.at[5], grp=near).wait_recv()
    for copy in sent + told:
        copy.wait_send()


def group_sum(*values):
    scratch = []
    for rows, lanes in GRP_PARTS:
        scratch += [pltpu.VMEM((rows // 2, lanes), BF)] * 4 + [DMA((6,))]
    shapes = GRP_PARTS + ((8, 640),)
    return pl.pallas_call(
        group_kernel,
        name="group_sum",
        out_shape=tuple(jax.ShapeDtypeStruct(shape, F32) for shape in shapes),
        in_specs=[VMEM] * 4,
        out_specs=(VMEM,) * 4,
        scratch_shapes=scratch + [pltpu.VMEM((NG, 8, 640), F32), DMA((NG,)), DMA((NG,))],
        compiler_params=params(7, 40),
        cost_estimate=pl.CostEstimate(flops=10**7, bytes_accessed=2 * 10**7, transcendentals=0),
    )(*values)


def dot(spec, a, b):
    return jnp.einsum(spec, a, b, preferred_element_type=F32)


def rms_normed(values, gain):
    scale = lax.rsqrt(jnp.mean(values * values, 0, keepdims=True) + norm_eps)
    return values * scale * gain[:, None]


def norm_back(values, gain, grad):
    scale = lax.rsqrt(jnp.mean(values * values, 0, keepdims=True) + norm_eps)
    pulled = grad * gain[:, None]
    middle = jnp.mean(values * pulled, 0, keepdims=True)
    return (
        scale * pulled - values * (scale * scale * scale) * middle,
        jnp.sum(grad * values * scale, 1),
    )


def rotary():
    half = HD // 2
    freqs = rope_base ** (-(jnp.arange(half, dtype=F32) * 2.0) / HD)
    angles = freqs[:, None] * jnp.arange(T, dtype=F32)[None, :]
    return (jnp.concatenate([jnp.cos(angles)] * 2, 0), jnp.concatenate([jnp.sin(angles)] * 2, 0))


def rotate(values, cosine, sine):
    half = HD // 2
    turned = jnp.concatenate([-values[..., half:, :], values[..., :half, :]], -2)
    return values * cosine + turned * sine


def unrotate(grad, cosine, sine):
    half = HD // 2
    part = grad * sine
    return grad * cosine + jnp.concatenate([part[..., half:, :], -part[..., :half, :]], -2)


def layer_forward(hidden0, gains, wa, wf, wp, allowed, cosine, sine):
    kv = KVH * HD
    group = H // KVH
    normed1 = rms_normed(hidden0, gains[0]).astype(BF)
    mixed = dot("ed,dt->et", wa, normed1)
    queries = rotate(mixed[:D].reshape(KVH, group, HD, T), cosine, sine).astype(BF)
    keys = rotate(mixed[D : D + kv].reshape(KVH, HD, T), cosine, sine).astype(BF)
    values = mixed[D + kv :].reshape(KVH, HD, T).astype(BF)
    scores = dot("kct,kgcq->kgtq", keys, queries) * HD ** (-0.5)
    scores = jnp.where(allowed, scores, masked_score)
    expo = jnp.exp(scores - jnp.max(scores, -2, keepdims=True))
    soft = expo / jnp.sum(expo, -2, keepdims=True)
    probs = soft.astype(BF)
    attended = dot("kct,kgtq->kgcq", values, probs).reshape(D, T).astype(BF)
    hidden1 = hidden0 + dot("de,et->dt", wp[:, :D], attended)
    normed2 = rms_normed(hidden1, gains[1]).astype(BF)
    gate_up = dot("ed,dt->et", wf, normed2)
    inner = (jax.nn.silu(gate_up[:FF]) * gate_up[FF:]).astype(BF)
    hidden2 = hidden1 + dot("df,ft->dt", wp[:, D:], inner)
    final = rms_normed(hidden2, gains[2]).astype(BF)
    kept = (
        hidden0, normed1, queries, keys, values, soft, probs,
        attended, hidden1, normed2, gate_up, inner, hidden2,
    )
    return final, kept


def layer_backward(grad_final, kept, gains, wa, wf, wp, cosine, sine):
    (
        hidden0, normed1, queries, keys, values, soft, probs,
        attended, hidden1, normed2, gate_up, inner, hidden2,
    ) = kept
    group = H // KVH
    grad_h2, grad_g3 = norm_back(hidden2, gains[2], grad_final)
    branch = grad_h2.astype(BF)
    grad_down = dot("dt,ft->df", branch, inner)
    grad_inner = dot("df,dt->ft", wp[:, D:], branch)
    gate, up = gate_up[:FF], gate_up[FF:]
    sigmoid = jax.nn.sigmoid(gate)
    slope = sigmoid * (1.0 + gate * (1.0 - sigmoid))
    grad_gate_up = jnp.concatenate(
        [grad_inner * up * slope, grad_inner * (gate * sigmoid)], 0
    ).astype(BF)
    grad_ffn = dot("et,dt->ed", grad_gate_up, normed2)
    grad_normed2 = dot("ed,et->dt", wf, grad_gate_up)
    grad_part, grad_g2 = norm_back(hidden1, gains[1], grad_normed2)
    grad_h1 = grad_h2 + grad_part
    branch = grad_h1.astype(BF)
    grad_wo = dot("dt,et->de", branch, attended)
    grad_att = dot("de,dt->et", wp[:, :D], branch).astype(BF).reshape(KVH, group, HD, T)
    grad_probs = dot("kct,kgcq->kgtq", values, grad_att)
    grad_scores = (
        soft * (grad_probs - jnp.sum(soft * grad_probs, -2, keepdims=True))
    ).astype(BF)
    grad_q = dot("kct,kgtq->kgcq", keys, grad_scores) * HD ** (-0.5)
    grad_k = dot("kgcq,kgtq->kct", queries, grad_scores) * HD ** (-0.5)
    grad_v = dot("kgcq,kgtq->kct", grad_att, probs)
    grad_q = unrotate(grad_q, cosine, sine).reshape(D, T)
    grad_k = unrotate(grad_k, cosine, sine).reshape(KVH * HD, T)
    grad_mixed = jnp.concatenate([grad_q, grad_k, grad_v.reshape(KVH * HD, T)], 0).astype(BF)
    grad_attn = dot("et,dt->ed", grad_mixed, normed1)
    grad_normed1 = dot("ed,et->dt", wa, grad_mixed)
    grad_part, grad_g1 = norm_back(hidden0, gains[0], grad_normed1)
    grad_proj = jnp.concatenate([grad_wo, grad_down], 1)
    return (
        (grad_h1 + grad_part).astype(BF),
        grad_attn,
        grad_ffn,
        grad_proj,
        jnp.stack([grad_g1, grad_g2, grad_g3]),
    )


def adam_update(weight, grad, first, second, rate, decay):
    first = beta_one * first + (1.0 - beta_one) * grad
    second = beta_two * second + (1.0 - beta_two) * grad * grad
    ratio = first / (1.0 - beta_one**STEP) / (jnp.sqrt(second / (1.0 - beta_two**STEP)) + adam_eps)
    return (weight - rate * (ratio + decay * weight), first, second)


def pack_fa(attn, ffn):
    pad = [(0, 0)] * (attn.ndim - 2) + [(0, FA_ROWS - 126), (0, 0)]
    return jnp.pad(jnp.concatenate([ffn, attn], -2), pad)


def pack_wp(proj):
    lead = proj.shape[:-2]
    pad = [(0, 0)] * len(lead) + [(0, WP_ROWS - 297), (0, 0)]
    return jnp.pad(proj.reshape(lead + (297, 128)), pad)


def on_device(
    token_ids,
    targets,
    segment_ids,
    row_counts,
    embed_table_master,
    embed_table_first,
    embed_table_second,
    embed_table_anchor,
    embed_table_momentum,
    attn_in_master,
    attn_in_first,
    attn_in_second,
    attn_in_anchor,
    attn_in_momentum,
    ffn_in_master,
    ffn_in_first,
    ffn_in_second,
    ffn_in_anchor,
    ffn_in_momentum,
    proj_out_master,
    proj_out_first,
    proj_out_second,
    proj_out_anchor,
    proj_out_momentum,
    norm_gains_master,
    norm_gains_first,
    norm_gains_second,
    norm_gains_anchor,
    norm_gains_momentum,
):
    me = lax.axis_index("wide")
    xh = lax.rem(me // 4, 2)
    other = flat(me // 8, 1 - xh, lax.rem(me, 4))
    ids = token_ids[0]
    gains = norm_gains_master[0]
    table = embed_table_master[0].T.astype(BF)
    weight = jnp.sum(row_counts[0, 0] * jnp.arange(1, 4))

    owner = ids // SHARD
    local = ids - owner * SHARD
    place_of = jnp.arange(T)
    same = ids[:, None] == ids[None, :]
    first_seen = ~jnp.any(same & (place_of[None, :] < place_of[:, None]), 1)
    rank = jnp.sum(
        (first_seen[None, :] & (owner[None, :] == owner[:, None]) & (ids[None, :] < ids[:, None])),
        1,
        dtype=jnp.int32,
    )
    most = jnp.max(rank) + 1
    slot_place = jnp.arange(NW * CAP)

    def slot_picks(turn):
        at = rank - turn * CAP
        slot = jnp.where((at >= 0) & (at < CAP), owner * CAP + at, -1)
        return slot_place[:, None] == slot[None, :]

    def message(picks):
        asked = jnp.max(jnp.where(picks, local[None, :], -1), 1).reshape(NW, 1, CAP)
        asked = jnp.pad(asked, ((0, 0), (0, 0), (0, 128 - CAP)), constant_values=-1)
        rest = jnp.concatenate(
            [
                targets[0].reshape(2, 128),
                jnp.broadcast_to(weight, (1, 128)),
                jnp.broadcast_to(most, (1, 128)),
                jnp.zeros((3, 128), jnp.int32),
            ],
            0,
        )
        return jnp.concatenate([asked, jnp.broadcast_to(rest[None], (NW, 7, 128))], 1)

    picks = slot_picks(0)
    fa = pack_fa(attn_in_master[0].T, ffn_in_master[0].T).astype(BF)
    wp = pack_wp(proj_out_master[0].T).astype(BF)
    got, rows, most_all, table_other, fa_all, wp_all = front(message(picks), table, fa, wp)
    turns = (jnp.max(most_all) + CAP - 1) // CAP

    def to_tokens(rows, picks):
        return dot("sd,st->dt", rows, picks.astype(BF))

    def more_tokens(carry):
        turn, hidden = carry
        picks = slot_picks(turn)
        return turn + 1, hidden + to_tokens(more_rows(message(picks), table), picks)

    hidden0 = lax.while_loop(
        lambda carry: carry[0] < turns, more_tokens, (jnp.int32(1), to_tokens(rows, picks))
    )[1]

    wf_full = fa_all[:, :96].reshape(2 * FF, D)
    wa_full = fa_all[:, 96:126].reshape(QKV, D)
    wp_full = wp_all[:, :297].reshape(D, D + FF)
    segments = segment_ids[0]
    allowed = (place_of[:, None] <= place_of[None, :]) & (segments[:, None] == segments[None, :])
    cosine, sine = rotary()
    final, kept = layer_forward(hidden0, gains, wa_full, wf_full, wp_full, allowed, cosine, sine)

    total = jnp.sum(got[:, 3, 0]).astype(F32) * T
    goals = got[:, 1:3, :].reshape(4, 2, 4, T)
    goals = jnp.where(xh == 0, goals[:, 0], goals[:, 1]).reshape(16, 1, T)
    near, far = goals - me * SHARD, goals - other * SHARD
    goals = jnp.where(
        (near >= 0) & (near < SHARD), near, jnp.where((far >= 0) & (far < SHARD), far + SHARD, -1)
    )
    goals = jnp.broadcast_to(goals, (16, 8, T))
    plain = weight.astype(F32)
    weights = jnp.concatenate(
        [jnp.full((1, T), plain / total, F32), jnp.full((1, T), plain, F32), jnp.zeros((6, T), F32)], 0
    )
    rows_t = jnp.concatenate([table, table_other], 1).T
    grad_final, head_own, head_other, loss = head(final, rows_t, table, table_other, goals, weights)

    grad_embedded, grad_attn, grad_ffn, grad_proj, grad_gains = layer_backward(
        grad_final, kept, gains, wa_full, wf_full, wp_full, cosine, sine
    )
    fa_parts = pack_fa(
        grad_attn.astype(BF).reshape(NW, 30, D), grad_ffn.astype(BF).reshape(NW, 96, D)
    ).reshape(4, 2, 4, FA_ROWS, D)
    wp_parts = pack_wp(grad_proj.astype(BF).reshape(NW, 18, D + FF)).reshape(4, 2, 4, WP_ROWS, 128)
    extra = jnp.zeros((8, 640), F32).at[:3, :D].set(grad_gains).at[3, 0].set(jnp.sum(loss[0]))

    def to_slots(picks):
        return dot("st,dt->sd", picks.astype(BF), grad_embedded).astype(BF)

    fa_sum, wp_sum, rows_in, head_in, extra_sum = back(
        fa_parts, wp_parts, to_slots(picks), head_other, extra
    )

    def to_table(got, rows):
        asked = got[:, 0, :CAP].reshape(NW * CAP)
        hot = (asked[:, None] == jnp.arange(SHARD)[None, :]).astype(BF)
        return dot("sd,sv->dv", rows, hot)

    def more_table(carry):
        turn, grad = carry
        picks = slot_picks(turn)
        return turn + 1, grad + to_table(*more_grads(message(picks), to_slots(picks)))

    table_grad = lax.while_loop(
        lambda carry: carry[0] < turns,
        more_table,
        (jnp.int32(1), head_own + head_in.astype(F32) + to_table(got, rows_in)),
    )[1]

    sum_gains = extra_sum[:3, :D]
    loss_total = extra_sum[3, 0]
    squares = jnp.sum(table_grad * table_grad) + jnp.sum(fa_sum * fa_sum) + jnp.sum(wp_sum * wp_sum)
    squares = norm_sum(jnp.broadcast_to(squares, (8, 128)))[0, 0]
    norm = jnp.sqrt(squares + jnp.sum(sum_gains * sum_gains))
    factor = jnp.minimum(1.0, clip_norm / norm)

    sum_ffn, sum_attn = fa_sum[:96], fa_sum[96:126]
    sum_proj = wp_sum[:297].reshape(18, D + FF)
    kinds = (
        (
            embed_table_master[0].T,
            table_grad,
            embed_table_first[0].T,
            embed_table_second[0].T,
            embed_table_anchor.T,
            embed_table_momentum.T,
            inner_rate,
            weight_decay,
        ),
        (
            attn_in_master[0].T,
            sum_attn,
            attn_in_first[0].T,
            attn_in_second[0].T,
            attn_in_anchor.T,
            attn_in_momentum.T,
            inner_rate,
            weight_decay,
        ),
        (
            ffn_in_master[0].T,
            sum_ffn,
            ffn_in_first[0].T,
            ffn_in_second[0].T,
            ffn_in_anchor.T,
            ffn_in_momentum.T,
            inner_rate,
            weight_decay,
        ),
        (
            proj_out_master[0].T,
            sum_proj,
            proj_out_first[0].T,
            proj_out_second[0].T,
            proj_out_anchor.T,
            proj_out_momentum.T,
            inner_rate,
            weight_decay,
        ),
        (
            gains,
            sum_gains,
            norm_gains_first[0],
            norm_gains_second[0],
            norm_gains_anchor,
            norm_gains_momentum,
            gain_rate,
            0.0,
        ),
    )
    updated = [
        adam_update(kind[0], kind[1] * factor, kind[2], kind[3], kind[6], kind[7]) for kind in kinds
    ]
    diffs = [kinds[index][4] - updated[index][0] for index in range(5)]
    summed = group_sum(
        diffs[0],
        pack_fa(diffs[1], diffs[2]),
        pack_wp(diffs[3]),
        jnp.zeros((8, 640), F32).at[:3, :D].set(diffs[4]),
    )
    sums = (
        summed[0],
        summed[1][96:126],
        summed[1][:96],
        summed[2][:297].reshape(18, D + FF),
        summed[3][:3, :D],
    )
    results = [loss_total.reshape(1), total.reshape(1), norm.reshape(1)]
    for index in range(5):
        average = sums[index] / NG
        outer = outer_momentum * kinds[index][5] + average
        weight = kinds[index][4] - outer_rate * (average + outer_momentum * outer)
        values = [average, outer, weight, updated[index][1], updated[index][2]]
        if index < 4:
            values = [value.T for value in values]
        results += values[:3] + [values[3][None], values[4][None]]
    return tuple(results)


def solution(mesh):
    in_specs = (
        P("grp", "wide"),
        P("grp", "wide"),
        P("grp", "wide"),
        P("grp", "wide", None),
        P("grp", "wide", None),
        P("grp", "wide", None),
        P("grp", "wide", None),
        P("wide", None),
        P("wide", None),
        P("grp", None, "wide"),
        P("grp", None, "wide"),
        P("grp", None, "wide"),
        P(None, "wide"),
        P(None, "wide"),
        P("grp", None, "wide"),
        P("grp", None, "wide"),
        P("grp", None, "wide"),
        P(None, "wide"),
        P(None, "wide"),
        P("grp", None, "wide"),
        P("grp", None, "wide"),
        P("grp", None, "wide"),
        P(None, "wide"),
        P(None, "wide"),
        P("grp", None, None),
        P("grp", None, None),
        P("grp", None, None),
        P(),
        P(),
    )
    out_specs = (
        P("grp"),
        P("grp"),
        P("grp"),
        P("wide", None),
        P("wide", None),
        P("wide", None),
        P("grp", "wide", None),
        P("grp", "wide", None),
        P(None, "wide"),
        P(None, "wide"),
        P(None, "wide"),
        P("grp", None, "wide"),
        P("grp", None, "wide"),
        P(None, "wide"),
        P(None, "wide"),
        P(None, "wide"),
        P("grp", None, "wide"),
        P("grp", None, "wide"),
        P(None, "wide"),
        P(None, "wide"),
        P(None, "wide"),
        P("grp", None, "wide"),
        P("grp", None, "wide"),
        P(),
        P(),
        P(),
        P("grp", None, None),
        P("grp", None, None),
    )
    return jax.shard_map(
        on_device, mesh=mesh, in_specs=in_specs, out_specs=out_specs, check_vma=False
    )
```

time: 2540 us -> 506 us (0.20)
  waiting for transfers between devices: 1240 us -> 0 us
  blocking collectives: 725 us -> 0 us
  Pallas kernels: 0 us -> 324 us
  matrix products: 260 us -> 28.6 us
  local copies, waits for them, and re-layouts: 133 us -> 68.9 us
  loops' own time: 48.4 us -> 0.23 us
  other arithmetic: 92.8 us -> 63.9 us
    reduce_scatter x2 -> x0, waiting for transfers between devices: 595 us -> none  [the longest x1 357 us: on_device(): lax.psum_scatter(jnp.dot(kept_logits, table_low, preferred_element_type=j...]
    psum x2 -> x0, waiting for transfers between devices: 455 us -> none  [the longest x1 394 us: on_device(): lax.psum((grad_attn, grad_ffn, grad_proj, grad_gains), 'wide')]
    psum x3 -> x0, blocking collectives: 342 us -> none  [the longest x2 301 us: on_device(): lax.psum((expsums * jnp.exp(peaks - peak), pickeds), 'wide')]
    pallas_call x0 -> x5, Pallas kernels: none -> 324 us  [the longest x1 108 us: head(): pl.pallas_call(head_kernel, name='head', out_shape=(jax.ShapeDtypeStruct(...]
    dot_general x59 -> x20, matrix products: 260 us -> 26.3 us  [dot(): return jnp.einsum(spec, a, b, preferred_element_type=F32)]
    all_gather x3 -> x0, blocking collectives: 233 us -> none  [the longest x1 83.1 us: on_device(): lax.all_gather(token_ids, 'wide', axis=1, tiled=True)]
    all_gather x5 -> x0, waiting for transfers between devices: 191 us -> none  [the longest x1 118 us: on_device(): lax.all_gather(grad_hidden0.astype(jnp.bfloat16), 'wide', axis=0, tiled=T...]
    pmax x1 -> x0, blocking collectives: 150 us -> none  [on_device(): peak = lax.pmax(peaks, 'wide')]
  transfers between devices with their start and end apart: 9 -> 0, of which waited for: 6 -> 0; matrix products, arithmetic and copies ran while one was open for 4% -> 0% of each run, Pallas kernels for 0% -> 0%
where the time goes in v1:
time: 506 us; the launch traced here: 496 us
  Pallas kernels  324 us (64%)
  local copies, waits for them, and re-layouts  68.9 us (14%)
  other arithmetic  63.9 us (13%)
  matrix products  28.6 us (6%)
  between operations  10.3 us (2%)
    pallas_call x1, Pallas kernels, head(): pl.pallas_call(head_kernel, name='head', out_shape=(jax.ShapeDtypeStruct(...  108 us
    pallas_call x1, Pallas kernels, back(): pl.pallas_call(back_kernel, name='back', out_shape=(jax.ShapeDtypeStruct(...  88.9 us
    pallas_call x1, Pallas kernels, front(): pl.pallas_call(front_kernel, name='front', out_shape=(jax.ShapeDtypeStruc...  83.7 us
    pallas_call x1, Pallas kernels, group_sum(): pl.pallas_call(group_kernel, name='group_sum', out_shape=tuple((jax.Shape...  32.1 us
    dot_general x20, matrix products, dot(): return jnp.einsum(spec, a, b, preferred_element_type=F32)  26.3 us
    transpose x5, other arithmetic, on_device(): values = [value.T for value in values]  16.5 us
    unnamed x158, local copies, waits for them, and re-layouts  15.2 us
    pallas_call x1, Pallas kernels, norm_sum(): pl.pallas_call(norm_kernel, name='norm_sum', out_shape=jax.ShapeDtypeStru...  11.5 us

profile of v1, /device:TPU:1, one launch (start us, length us, event | category | flops | bytes accessed | tf_op | source)
XLA Modules:
  0.0 496.1 jit_solution(13727048020209132950)
XLA Ops:
  0.7 1.3 fusion.103
  3.4 0.9 fusion.57
  4.4 1.3 multiply_subtract_fusion.2
  6.4 1.0 convert_reduce_fusion
  8.7 0.8 add_add_fusion.3
  9.8 1.3 slice_reduce_fusion.3
  11.1 0.9 copy.190
  12.3 1.5 fusion.58
  13.7 0.9 copy.189
  14.8 1.0 bitcast_convert_fusion.1
  16.6 2.2 bitcast_convert_fusion.table
  18.8 83.7 %front.1 = (s32[32,8,128]{2,1,0:T(8,128)S(1)}, bf16[1024,576]{1,0:T(8,128)(2,1)S(1)}, s32[4,8,128]{2,1,0:T(8,128)S(1)}, bf16[576,1536]{1,0:T(8,128)(2,1)S(1)}, b...) custom-call(s32[32,8,128]{2,1,0:T(8,128)S(1)} %select_add_fusion.2.msg, ...), custom_call_target="tpu_custom_call" | custom-call | flops 2000000000 | bytes 30000000 | tf_op jit(solution)/shard_map/front/pallas_call | solution.py:270
  102.5 2.3 copy-done
  104.9 1.2 copy-done.1
  106.1 1.1 copy-done.6
  109.9 1.6 slice.184
  112.2 5.1 %reshape.442 = bf16[576,2112]{1,0:T(8,128)(2,1)} reshape(bf16[32,297,128]{2,1,0:T(8,128)(2,1)} %slice.184) | data formatting | bytes 4866048 | tf_op jit(solution)/shard_map/reshape | solution.py:1150
  118.8 1.3 fusion.41
  120.2 1.2 multiply_reduce_fusion.9
  121.4 2.5 slice.187
  123.9 4.5 slice.196
  128.3 2.7 reshape.443
  131.0 2.0 fusion.112
  134.5 2.3 fusion.116
  136.8 2.2 convolution_convert_fusion.6
  140.4 1.5 fusion.113
  142.4 0.8 multiply_reduce_fusion.7
  144.4 0.8 multiply_convert_fusion.3.final
  145.2 2.3 maximum_bitcast_fusion
  147.6 6.1 %copy.103.rows_t = bf16[3072,576]{1,0:T(8,128)(2,1)} copy(bf16[3072,576]{0,1:T(8,128)(2,1)} %maximum_bitcast_fusion) | data formatting | bytes 7077888 | tf_op jit(solution)/shard_map/transpose | solution.py:1168
  153.7 108.0 %head.1 = (f32[576,256]{1,0:T(8,128)}, f32[576,1536]{1,0:T(8,128)}, bf16[576,1536]{1,0:T(8,128)(2,1)}, f32[8,256]{1,0:T(8,128)}) custom-call(bf16[576,256]{1,0:T(8,128)(2,1)} %multiply_convert_fusion.3.final, bf16[3072,576]{1,0:T(8,128)(2,1)} %copy.103.rows_t, bf16[576,1536]{1,0:T(8,128)(2,1)S(1)} %get-tuple-element.714, bf16[576,1536]{1,0:T(8,128)(2,1)} %copy-done.1, ...), custom_call_target="tpu_custom_call" | custom-call | flops 43486543872 | bytes 20000000 | tf_op jit(solution)/shard_map/head/pallas_call | solution.py:624
  261.7 1.5 slice_reduce_fusion.6
  263.1 1.5 multiply_reduce_fusion.1
  264.7 1.4 multiply_subtract_fusion
  266.1 4.0 multiply_convert_fusion.1
  270.2 1.3 multiply_reduce_fusion.2
  272.2 1.3 copy-done.28
  273.5 1.2 fusion.40
  275.8 0.8 pad_maximum_fusion
  276.6 3.8 convert_element_type.122
  280.4 3.7 pad.54
  284.1 2.9 convolution_convert_fusion.1
  287.0 6.3 %copy.104 = bf16[3072,576]{1,0:T(8,128)(2,1)} copy(bf16[3072,576]{0,1:T(8,128)(2,1)} %convolution_convert_fusion.1) | data formatting | bytes 7077888 | tf_op jit(solution)/shard_map/convert_element_type | solution.py:1175
  298.8 1.1 copy.105
  300.4 5.2 %fusion.17 = bf16[32,128,576]{2,1,0:T(8,128)(2,1)} fusion(bf16[32,30,576]{2,1,0:T(8,128)(2,1)S(1)} %reshape.453, bf16[32,96,576]{2,1,0:T(8,128)(2,1)} %bitcast.369), kind=kLoop, calls=%fused_computation.32 | loop fusion | flops 16515072 | bytes 9363456 | tf_op jit(solution)/shard_map/concatenate | solution.py:1050
  306.9 88.9 %back.1 = (f32[128,576]{1,0:T(8,128)S(1)}, f32[320,128]{1,0:T(8,128)S(1)}, bf16[1024,576]{1,0:T(8,128)(2,1)S(1)}, bf16[576,1536]{1,0:T(8,128)(2,1)S(1)}, f32[8,640]{1,0:T(8,128)S(1)}) custom-call(bf16[4,2,4,128,576]{4,3,2,1,0:T(8,128)(2,1)} %bitcast.366, bf16[4,2,4,320,128]{4,3,2,1,0:T(8,128)(2,1)} %bitcast.370, bf16[1024,576]{1,0:T(8,128)(2,1)S(1)} %copy.106.rows, ...), custom_call_target="tpu_custom_call" | custom-call | flops 100000000 | bytes 30000000 | tf_op jit(solution)/shard_map/back/pallas_call | solution.py:801
  398.3 4.1 add_add_fusion.2
  402.8 3.7 multiply_reduce_fusion
  408.4 11.5 %norm_sum.1 = f32[8,128]{1,0:T(8,128)S(1)} custom-call(f32[8,128]{1,0:T(8,128)S(1)} %broadcast_in_dim.191.value), custom_call_target="tpu_custom_call" | custom-call | tf_op jit(solution)/shard_map/norm_sum/pallas_call | solution.py:838
  423.8 0.8 mul.920
  426.1 1.0 fusion.94
  427.1 0.8 select_maximum_fusion.refs_1_
  427.8 2.5 fusion.91
  430.3 0.8 broadcast_in_dim.199
  431.1 1.7 reshape.459
  432.8 0.9 pad.56.refs_2_
  433.7 1.7 broadcast_in_dim.198
  435.4 8.3 %fusion.44 = (f32[1,1536,576]{1,2,0:T(8,128)}, f32[576,1536]{1,0:T(8,128)S(1)}, f32[1,1536,576]{1,2,0:T(8,128)}) fusion(f32[576,1536]{1,0:T(8,128)} %get-tuple-element.216, f32[]{:T(128)S(6)} %min.3, f32[1,1536,576]{1,2,0:T(8,128)} %param.45, f32[1,1536,576]{1,2,0:T(8,128)} %param.44, f32[1,1536,576]{1,2,0:T(8,128)S(1)} %copy-done.15, f32[1536,576]{0,1:T(8,128)} %param.46), kind=kLoop, calls=%fused_computation.91 | loop fusion | flops 15040512 | bytes 28311556 | tf_op jit(solution)/shard_map/broadcast_in_dim | solution.py:1289
  443.8 32.1 %group_sum.1 = (f32[576,1536]{1,0:T(8,128)S(1)}, f32[128,576]{1,0:T(8,128)S(1)}, f32[320,128]{1,0:T(8,128)S(1)}, f32[8,640]{1,0:T(8,128)S(1)}) custom-call(f32[576,1536]{1,0:T(8,128)S(1)} %get-tuple-element.441.refs_0_, f32[128,576]{1,0:T(8,128)S(1)} %copy-done.3, f32[320,128]{1,0:T(8,128)S(1)} %pad.56.refs_2_, f32[8,640]{1,0:T(8,128)S(1)} %copy-done.5), custom_call_target="tpu_custom_call" | custom-call | flops 10000000 | bytes 20000000 | tf_op jit(solution)/shard_map/group_sum/pallas_call | solution.py:918
  477.9 1.7 div.253
  479.6 1.7 fusion.88
  481.3 2.1 fusion.63
  483.4 1.9 fusion.71
  485.3 8.4 %fusion.22 = (f32[1536,576]{0,1:T(8,128)}, f32[1536,576]{0,1:T(8,128)}, f32[1536,576]{0,1:T(8,128)}) fusion(f32[1536,576]{0,1:T(8,128)} %param.46, f32[1536,576]{0,1:T(8,128)} %param.47, f32[576,1536]{1,0:T(8,128)S(1)} %get-tuple-element.219), kind=kLoop, calls=%fused_computation.45 | loop fusion | flops 6193152 | bytes 21233664 | tf_op jit(solution)/shard_map/transpose | solution.py:1288
  (236 shorter events, 29.2 us)
Async XLA Ops:
  7.3 4.9 copy-start.43
  8.7 3.6 copy-start.64
  18.8 83.7 %copy-start.8 = (bf16[576,1536]{1,0:T(8,128)(2,1)}, bf16[576,1536]{1,0:T(8,128)(2,1)S(1)}, u32[]{:S(2)}) copy-start(bf16[576,1536]{1,0:T(8,128)(2,1)S(1)} %bitcast_convert_fusion.table) | copy-start | bytes 5308420
  102.5 2.3 copy-start
  112.2 6.6 %copy-start.7 = (bf16[1024,576]{1,0:T(8,128)(2,1)S(1)}, bf16[1024,576]{1,0:T(8,128)(2,1)}, u32[]{:S(2)}) copy-start(bf16[1024,576]{1,0:T(8,128)(2,1)} %copy-done.6) | copy-start | bytes 3538948
  112.2 6.6 %copy-start.65 = (s32[1,256]{1,0:T(1,128)S(1)}, s32[1,256]{1,0:T(1,128)}, u32[]{:S(2)}) copy-start(s32[1,256]{1,0:T(1,128)} %copy-done.64) | copy-start | bytes 3076
  117.3 2.9 copy-start.9
  117.3 2.9 copy-start.44
  117.3 2.9 copy-start.47
  117.3 2.9 copy-start.49
  117.3 2.9 copy-start.51
  128.3 2.7 copy-start.16
  128.3 2.7 copy-start.60
  131.0 2.8 copy-start.36
  131.0 2.8 copy-start.37
  134.5 4.5 copy-start.30
  134.5 2.3 copy-start.53
  136.8 2.4 copy-start.24
  136.8 3.6 copy-start.10
  136.8 3.6 copy-start.61
  139.6 2.8 copy-start.17
  141.9 1.7 copy-start.12
  142.4 1.4 copy-start.26
  142.4 2.0 copy-start.57
  142.4 2.8 copy-start.2
  261.7 4.4 copy-start.25
  266.1 4.0 copy-start.11
  266.1 4.0 copy-start.18
  270.1 1.4 copy-start.73
  270.1 1.4 copy-start.75
  271.5 2.0 copy-start.28
  271.7 3.6 copy-start.20
  272.2 2.5 copy-start.70
  280.4 3.7 copy-start.19
  280.4 3.7 copy-start.74
  280.4 3.7 copy-start.76
  287.0 6.3 %copy-start.29 = (f32[3,3,256,256]{3,2,1,0:T(8,128)S(1)}, f32[3,3,256,256]{3,2,1,0:T(8,128)}, u32[]{:S(2)}) copy-start(f32[3,3,256,256]{3,2,1,0:T(8,128)} %get-tuple-element.491) | copy-start | bytes 7077892
  287.0 6.3 %copy-start.54 = (bf16[192,256]{1,0:T(8,128)(2,1)S(1)}, bf16[192,256]{1,0:T(8,128)(2,1)}, u32[]{:S(2)}) copy-start(bf16[192,256]{1,0:T(8,128)(2,1)} %slice.333) | copy-start | bytes 294916
  287.0 6.3 %copy-start.71 = (bf16[576,256]{1,0:T(8,128)(2,1)S(1)}, bf16[576,256]{1,0:T(8,128)(2,1)}, u32[]{:S(2)}) copy-start(bf16[576,256]{1,0:T(8,128)(2,1)} %copy-done.70) | copy-start | bytes 884740
  296.0 1.4 copy-start.21
  300.4 5.3 %copy-start.66 = (s32[1,256]{1,0:T(1,128)S(1)}, s32[1,256]{1,0:T(1,128)}, u32[]{:S(2)}) copy-start(s32[1,256]{1,0:T(1,128)} %copy-done.64) | copy-start | bytes 3076
  306.9 91.4 %copy-start.69 = (s32[1024]{0:T(1024)S(1)}, s32[1024]{0:T(1024)}, u32[]{:S(2)}) copy-start(s32[1024]{0:T(1024)} %eq.136) | copy-start | bytes 12292
  306.9 91.4 %copy-start.77 = (f32[576,1536]{1,0:T(8,128)S(1)}, f32[576,1536]{1,0:T(8,128)}, u32[]{:S(2)}) copy-start(f32[576,1536]{1,0:T(8,128)} %get-tuple-element.213) | copy-start | bytes 10616836
  398.3 4.1 copy-start.45
  398.3 4.1 copy-start.48
  398.3 4.1 copy-start.50
  398.3 4.1 copy-start.52
  402.7 19.2 %copy-start.59 = (f32[3,576]{1,0:T(4,128)S(1)}, f32[3,576]{1,0:T(4,128)}, u32[]{:S(2)}) copy-start(f32[3,576]{1,0:T(4,128)} %param.66) | copy-start | bytes 20740
  402.7 19.2 %copy-start.62 = (f32[1,3,576]{2,0,1:T(1,128)S(1)}, f32[1,3,576]{2,0,1:T(1,128)}, u32[]{:S(2)}) copy-start(f32[1,3,576]{2,0,1:T(1,128)} %param.63) | copy-start | bytes 20740
  402.7 19.2 %copy-start.67 = (f32[1,3,576]{2,0,1:T(1,128)S(1)}, f32[1,3,576]{2,0,1:T(1,128)}, u32[]{:S(2)}) copy-start(f32[1,3,576]{2,0,1:T(1,128)} %param.65) | copy-start | bytes 20740
  402.7 19.2 %copy-start.68 = (f32[1,3,576]{2,0,1:T(1,128)S(1)}, f32[1,3,576]{2,0,1:T(1,128)}, u32[]{:S(2)}) copy-start(f32[1,3,576]{2,0,1:T(1,128)} %param.64) | copy-start | bytes 20740
  402.7 21.8 %copy-start.39 = (f32[576,30]{0,1:T(8,128)S(1)}, f32[576,30]{0,1:T(8,128)}, u32[]{:S(2)}) copy-start(f32[576,30]{0,1:T(8,128)} %param.51) | copy-start | bytes 207364
  402.7 21.8 %copy-start.40 = (f32[1,576,30]{1,0,2:T(1,128)S(1)}, f32[1,576,30]{1,0,2:T(1,128)}, u32[]{:S(2)}) copy-start(f32[1,576,30]{1,0,2:T(1,128)} %param.48) | copy-start | bytes 207364
  402.7 21.8 %copy-start.55 = (f32[1,576,30]{1,0,2:T(1,128)S(1)}, f32[1,576,30]{1,0,2:T(1,128)}, u32[]{:S(2)}) copy-start(f32[1,576,30]{1,0,2:T(1,128)} %param.50) | copy-start | bytes 207364
  402.8 21.8 %copy-start.56 = (f32[1,576,30]{1,0,2:T(1,128)S(1)}, f32[1,576,30]{1,0,2:T(1,128)}, u32[]{:S(2)}) copy-start(f32[1,576,30]{1,0,2:T(1,128)} %param.49) | copy-start | bytes 207364
  402.8 23.3 %copy-start.32 = (f32[1,576,96]{1,2,0:T(8,128)S(1)}, f32[1,576,96]{1,2,0:T(8,128)}, u32[]{:S(2)}) copy-start(f32[1,576,96]{1,2,0:T(8,128)} %param.53) | copy-start | bytes 663556
  402.8 23.3 %copy-start.33 = (f32[576,96]{0,1:T(8,128)S(1)}, f32[576,96]{0,1:T(8,128)}, u32[]{:S(2)}) copy-start(f32[576,96]{0,1:T(8,128)} %param.56) | copy-start | bytes 663556
  402.8 23.3 %copy-start.41 = (f32[1,576,96]{1,2,0:T(8,128)S(1)}, f32[1,576,96]{1,2,0:T(8,128)}, u32[]{:S(2)}) copy-start(f32[1,576,96]{1,2,0:T(8,128)} %param.55) | copy-start | bytes 663556
  402.8 23.3 %copy-start.42 = (f32[1,576,96]{1,2,0:T(8,128)S(1)}, f32[1,576,96]{1,2,0:T(8,128)}, u32[]{:S(2)}) copy-start(f32[1,576,96]{1,2,0:T(8,128)} %param.54) | copy-start | bytes 663556
  424.6 3.3 copy-start.34
  427.1 8.4 %copy-start.15 = (f32[1,1536,576]{1,2,0:T(8,128)S(1)}, f32[1,1536,576]{1,2,0:T(8,128)}, u32[]{:S(2)}) copy-start(f32[1,1536,576]{1,2,0:T(8,128)} %param.43) | copy-start | bytes 10616836
  435.4 8.4 %copy-start.3 = (f32[128,576]{1,0:T(8,128)S(1)}, f32[128,576]{1,0:T(8,128)}, u32[]{:S(2)}) copy-start(f32[128,576]{1,0:T(8,128)} %select_maximum_fusion.refs_1_) | copy-start | bytes 884740
  435.4 8.4 %copy-start.5 = (f32[8,640]{1,0:T(8,128)S(1)}, f32[8,640]{1,0:T(8,128)}, u32[]{:S(2)}) copy-start(f32[8,640]{1,0:T(8,128)} %scatter.14.refs_3_) | copy-start | bytes 61444
  443.8 32.8 %copy-start.63 = (f32[3,576]{1,0:T(4,128)S(1)}, f32[3,576]{1,0:T(4,128)}, u32[]{:S(2)}) copy-start(f32[3,576]{1,0:T(4,128)} %param.67) | copy-start | bytes 20740
  (12 other events, 11.9 us)

commit v2 on v1

--- a/solution.py
+++ b/solution.py
@@ -75,7 +75,7 @@
     )
 
 
-def greet_wide(me, grp=None):
+def greet_wide(me, grp=None, sides=False):
     barrier = pltpu.get_barrier_semaphore()
 
     def one(k, carry):
@@ -92,6 +92,10 @@
                 barrier, inc=1, device_id={"grp": lax.rem(grp + k, NG)}, device_id_type=MESH
             )
         count += NG - 1
+    if sides:
+        for step in (1, 3):
+            pl.semaphore_signal(barrier, inc=1, device_id=beside(step), device_id_type=MESH)
+        count += 2
     pl.semaphore_wait(barrier, count)
 
 
@@ -130,74 +134,126 @@
         lax.fori_loop(1, NW, one, 0)
 
 
-class Gather:
-    def __init__(self, x, out, rows, ssem, rsem, lsem):
-        self.x, self.out, self.half = x, out, rows // 2
-        self.ssem, self.rsem, self.lsem = ssem, rsem, lsem
+class Ring:
+    def __init__(self, view, sem, quarter, ssem, at):
+        self.view, self.sem, self.q = view, sem, quarter
+        self.ssem, self.used, self.sent = ssem, at, []
         self.me, self.y, self.xh, self.z = place()
-        self.used = 0
-        self.sent = []
-
-    def send(self, src, dst, rsem, peer):
-        copy = remote(src, dst, self.ssem.at[self.used], rsem, wide=peer)
+
+    def send(self, src, dst, rsem, to):
+        copy = remote(src, dst, self.ssem.at[self.used], rsem, wide=flat(to[0], self.xh, to[1]))
         self.used += 1
         copy.start()
         self.sent.append(copy)
 
-    def rows(self, part):
-        return pl.ds(part * self.half, self.half)
-
-    def wait(self, block, part=None):
-        dst = self.out.at[block] if part is None else self.out.at[block, self.rows(part)]
-        remote(
-            dst, dst, self.ssem.at[0], self.rsem.at[block, 0 if part is None else part], wide=block
-        ).wait_recv()
-
-    def whole(self, src, block):
-        y, xh, z = self.y, self.xh, self.z
+    def pass_on(self, y, z, first, count, index, *to):
+        piece = self.view(y, z, first * self.q, count * self.q)
+        for one in to:
+            self.send(piece, piece, self.sem(y, z, index), one)
+
+    def wait(self, y, z, first, count, index):
+        piece = self.view(y, z, first * self.q, count * self.q)
+        remote(piece, piece, self.ssem.at[0], self.sem(y, z, index), wide=self.me).wait_recv()
+
+    def around(self):
+        y, z = self.y, self.z
+        return y, z, (turn4(y, 1), z), (turn4(y, 3), z), (y, turn4(z, 1)), (y, turn4(z, 3))
+
+    def own(self, src):
+        y, z, y_up, y_down, z_up, z_down = self.around()
+        for to in (y_up, y_down, z_up, z_down):
+            self.send(src, self.view(y, z, 0, 4 * self.q), self.sem(y, z, 0), to)
+
+    def near(self):
+        y, z, y_up, y_down, z_up, z_down = self.around()
+        for at, far, turn, half, sides in (
+            (y_down, y_up, 0, 0, (z_up, z_down)),
+            (y_up, y_down, 1, 0, (z_up, z_down)),
+            (z_down, z_up, 0, 2, (y_up, y_down)),
+            (z_up, z_down, 1, 2, (y_up, y_down)),
+        ):
+            self.wait(*at, 0, 4, 0)
+            self.pass_on(*at, turn, 1, turn, far)
+            self.pass_on(*at, 2 + turn, 1, 2 + turn, far)
+            self.pass_on(*at, half, 2, half, *sides)
+
+    def far(self):
+        y, z, y_up, y_down, z_up, z_down = self.around()
+        for at, half, sides in (
+            ((turn4(y, 2), z), 0, (z_up, z_down)),
+            ((y, turn4(z, 2)), 2, (y_up, y_down)),
+        ):
+            for index in range(4):
+                self.wait(*at, index, 1, index)
+            self.pass_on(*at, half, 2, half, *sides)
+
+    def cross(self):
+        y, z, y_up, y_down, z_up, z_down = self.around()
         for k in (1, 3, 2):
-            self.send(src, self.out.at[block], self.rsem.at[block, 0], flat(turn4(y, k), xh, z))
-            self.send(src, self.out.at[block], self.rsem.at[block, 0], flat(y, xh, turn4(z, k)))
-
-    def start(self):
-        other = flat(self.y, 1 - self.xh, self.z)
-        self.send(self.x, self.out.at[self.me], self.rsem.at[self.me, 0], other)
-        self.local = pltpu.make_async_copy(self.x, self.out.at[self.me], self.lsem)
-        self.local.start()
-        self.whole(self.x, self.me)
-
-    def second(self):
-        other = flat(self.y, 1 - self.xh, self.z)
-        self.wait(other)
-        self.whole(self.out.at[other], other)
-
-    def third(self, xh):
+            row, column = turn4(y, k), turn4(z, k)
+            self.wait(row, z_down[1], 0, 2, 0)
+            self.pass_on(row, z_down[1], 0, 1, 0, z_up)
+            self.wait(row, z_up[1], 0, 2, 0)
+            self.pass_on(row, z_up[1], 1, 1, 1, z_down)
+            self.wait(y_down[0], column, 2, 2, 2)
+            self.pass_on(y_down[0], column, 2, 1, 2, y_up)
+            self.wait(y_up[0], column, 2, 2, 2)
+            self.pass_on(y_up[0], column, 3, 1, 3, y_down)
+
+    def last(self):
         y, z = self.y, self.z
         for k in (1, 3, 2):
-            block = flat(turn4(y, k), xh, z)
-            self.wait(block)
-            for m in (1, 3, 2):
-                piece = self.out.at[block, self.rows(0)]
-                self.send(piece, piece, self.rsem.at[block, 0], flat(y, self.xh, turn4(z, m)))
-            block = flat(y, xh, turn4(z, k))
-            self.wait(block)
-            for m in (1, 3, 2):
-                piece = self.out.at[block, self.rows(1)]
-                self.send(piece, piece, self.rsem.at[block, 1], flat(turn4(y, m), self.xh, z))
+            row, column = turn4(y, k), turn4(z, k)
+            for index in range(2):
+                self.wait(row, turn4(z, 2), index, 1, index)
+                self.wait(turn4(y, 2), column, 2 + index, 1, 2 + index)
 
     def finish(self):
-        for xh in (self.xh, 1 - self.xh):
-            for k in (1, 2, 3):
-                for m in (1, 2, 3):
-                    block = flat(turn4(self.y, k), xh, turn4(self.z, m))
-                    self.wait(block, 0)
-                    self.wait(block, 1)
         for copy in self.sent:
             copy.wait_send()
-        self.local.wait()
-
-
-GATHER_SENDS = 1 + 12 + 36
+
+
+RING_SENDS = 36
+
+
+def beside(step):
+    me, y, xh, z = place()
+    grp = lax.axis_index("grp")
+    low = grp // 2
+    side = lax.rem(xh + low + (0 if step == 1 else 1), 2)
+    return {"grp": (1 - low) * 2 + lax.rem(grp, 2), "wide": flat(y, side, z)}
+
+
+class Relay:
+    def __init__(self, sources, stops, ends, ssem, rsem):
+        self.sources, self.stops, self.ends, self.ssem, self.rsem = sources, stops, ends, ssem, rsem
+
+    def copy(self, src, dst, at, step):
+        return remote(src, dst, self.ssem.at[at], self.rsem.at[at], **beside(step))
+
+    def legs(self, hop):
+        for i, step in enumerate((1, 3)):
+            src = self.sources[i] if hop == 0 else self.stops[i]
+            dst = self.stops[i] if hop == 0 else self.ends[i]
+            yield self.copy(src, dst, 2 * hop + i, step)
+
+    def start(self):
+        for copy in self.legs(0):
+            copy.start()
+
+    def forward(self):
+        for first, second in zip(self.legs(0), self.legs(1)):
+            first.wait_recv()
+            second.start()
+
+    def wait(self):
+        for copy in self.legs(1):
+            copy.wait_recv()
+
+    def finish(self):
+        for hop in (0, 1):
+            for copy in self.legs(hop):
+                copy.wait_send()
 
 
 def look_up(got, table, hot, rows, slot_row):
@@ -219,21 +275,54 @@
     return pl.ds(pl.multiple_of(at * CAP, CAP), CAP)
 
 
+def turn_over(table, rows, first):
+    for c in range(0, SHARD, 256):
+        rows[first + c : first + c + 256, :] = table[:, c : c + 256].T
+
+
 def front_kernel(
-    msg, table, fa, wp, got, emb, most, table_other, fa_all, wp_all,
-    hot, rows, own_most, msg_s, msg_r, emb_s, emb_r, most_s, most_r, swap, fa_s, fa_r, wp_s, wp_r, local,
+    msg, table, fa, wp, got, emb, most, table_other, rows_t, fa_all, wp_all,
+    hot, rows, own_most, stops, msg_s, msg_r, emb_s, emb_r, most_s, most_r, swap_s, swap_r,
+    fa_s, fa_r, wp_s, wp_r, x_s, x_r, local,
 ):
     me, y, xh, z = place()
     grp = lax.axis_index("grp")
-    greet_wide(me, grp)
+    greet_wide(me, grp, sides=True)
     ask = Scatter(lambda p: msg.at[p], lambda p: got.at[p], msg_s, msg_r, me)
     ask.start()
     got[me] = msg[me]
-    gather_fa = Gather(fa, fa_all, FA_ROWS, fa_s, fa_r, local.at[0])
-    gather_wp = Gather(wp, wp_all, WP_ROWS, wp_s, wp_r, local.at[1])
-    gather_fa.start()
-    gather_wp.start()
-    trade = remote(table, table_other, swap.at[0], swap.at[1], wide=flat(y, 1 - xh, z))
+    other = flat(y, 1 - xh, z)
+    over, own, rings = [], [], []
+    for i, (x, out, size, ssem, rsem) in enumerate(
+        ((fa, fa_all, FA_ROWS, fa_s, fa_r), (wp, wp_all, WP_ROWS, wp_s, wp_r))
+    ):
+        over.append(remote(x, out.at[me], x_s.at[i], x_r.at[i], wide=other))
+        over[-1].start()
+        own.append(pltpu.make_async_copy(x, out.at[me], local.at[i]))
+        own[-1].start()
+        pair = []
+        for k, side in enumerate((xh, 1 - xh)):
+            pair.append(
+                Ring(
+                    lambda Y, Z, first, count, out=out, side=side: out.at[
+                        flat(Y, side, Z), pl.ds(first, count)
+                    ],
+                    lambda Y, Z, index, rsem=rsem, side=side: rsem.at[flat(Y, side, Z), index],
+                    size // 4,
+                    ssem,
+                    k * RING_SENDS,
+                )
+            )
+        rings.append(pair)
+        pair[0].own(x)
+    halves = (pl.ds(0, D // 2), pl.ds(D // 2, D // 2))
+    trade = Relay(
+        [table.at[half] for half in halves],
+        [stops.at[i] for i in range(2)],
+        [table_other.at[half] for half in halves],
+        swap_s,
+        swap_r,
+    )
     trade.start()
     ask.wait_recv()
     look_up(got, table, hot, rows, 0)
@@ -245,25 +334,45 @@
     most[grp] = own_most[...]
     told = []
     for k in range(1, NG):
-        other = lax.rem(grp + k, NG)
-        told.append(remote(own_most, most.at[grp], most_s.at[k], most_r.at[grp], grp=other))
+        to = lax.rem(grp + k, NG)
+        told.append(remote(own_most, most.at[grp], most_s.at[k], most_r.at[grp], grp=to))
         told[-1].start()
-    gather_fa.second()
-    gather_wp.second()
-    for side in (xh, 1 - xh):
-        gather_fa.third(side)
-        gather_wp.third(side)
+    for i in range(2):
+        rings[i][0].near()
+    for i, out in enumerate((fa_all, wp_all)):
+        over[i].wait_recv()
+        rings[i][1].own(out.at[other])
+    for i in range(2):
+        rings[i][0].far()
+    for i in range(2):
+        rings[i][1].near()
+    for i in range(2):
+        rings[i][0].cross()
+    turn_over(table, rows_t, 0)
+    trade.forward()
+    for i in range(2):
+        rings[i][1].far()
+    for i in range(2):
+        rings[i][1].cross()
     reply.wait_recv()
     for k in range(1, NG):
-        other = lax.rem(grp + k, NG)
-        remote(own_most, most.at[other], most_s.at[k], most_r.at[other], grp=other).wait_recv()
+        to = lax.rem(grp + k, NG)
+        remote(own_most, most.at[to], most_s.at[k], most_r.at[to], grp=to).wait_recv()
+    trade.wait()
+    turn_over(table_other, rows_t, SHARD)
+    for pair in rings:
+        for ring in pair:
+            ring.last()
     ask.wait_send()
     reply.wait_send()
-    for copy in told:
+    trade.finish()
+    for copy in told + over:
         copy.wait_send()
-    gather_fa.finish()
-    gather_wp.finish()
-    trade.wait()
+    for copy in own:
+        copy.wait()
+    for pair in rings:
+        for ring in pair:
+            ring.finish()
 
 
 def front(msg, table, fa, wp):
@@ -275,29 +384,34 @@
             jax.ShapeDtypeStruct((NW * CAP, D), BF),
             jax.ShapeDtypeStruct((NG, 8, 128), jnp.int32),
             jax.ShapeDtypeStruct((D, SHARD), BF),
+            jax.ShapeDtypeStruct((2 * SHARD, D), BF),
             jax.ShapeDtypeStruct((NW, FA_ROWS, D), BF),
             jax.ShapeDtypeStruct((NW, WP_ROWS, 128), BF),
         ),
         in_specs=[VMEM, VMEM, ANY, ANY],
-        out_specs=(VMEM, VMEM, VMEM, ANY, ANY, ANY),
+        out_specs=(VMEM, VMEM, VMEM, VMEM, VMEM, ANY, ANY),
         scratch_shapes=[
             pltpu.VMEM((8 * CAP, SHARD), BF),
             pltpu.VMEM((NW * CAP, D), BF),
             pltpu.VMEM((8, 128), jnp.int32),
+            pltpu.VMEM((2, D // 2, SHARD), BF),
             DMA((NW,)),
             DMA((NW,)),
             DMA((NW,)),
             DMA((NW,)),
             DMA((NG,)),
             DMA((NG,)),
+            DMA((4,)),
+            DMA((4,)),
+            DMA((2 * RING_SENDS,)),
+            DMA((NW, 4)),
+            DMA((2 * RING_SENDS,)),
+            DMA((NW, 4)),
             DMA((2,)),
-            DMA((GATHER_SENDS,)),
-            DMA((NW, 2)),
-            DMA((GATHER_SENDS,)),
-            DMA((NW, 2)),
+            DMA((2,)),
             DMA((2,)),
         ],
-        compiler_params=params(1, 40),
+        compiler_params=params(1, 48),
         cost_estimate=pl.CostEstimate(flops=2 * 10**9, bytes_accessed=3 * 10**7, transcendentals=0),
     )(msg, table, fa, wp)
 
@@ -368,7 +482,7 @@
 TOK = 16 * T
 CH = 512
 NCH = VOC // CH
-HALF = D // 2
+QUART = D // 4
 
 
 def cols(j):
@@ -378,8 +492,9 @@
 def head_kernel(
     final, rows_t, table, table_other, goal, weights,
     grad_final, head_own, head_other, loss,
-    fall, expo, tops, stat, stat_in, coef, coef_in, parts, in_a, in_b, sum_a, sum_b, in_a2, in_b2,
-    g_s, g_r, st_s, st_r, co_s, co_r, a_s, a_r, b_s, b_r, a2_s, a2_r, b2_s, b2_r,
+    fall, expo, tops, stat, stat_in, coef, coef_in, parts,
+    part_a, part_b, whole_a, whole_b, sum_a, sum_b, part_a2, part_b2, whole_a2, whole_b2,
+    g_s, g_r, st_s, st_r, co_s, co_r, a_s, b_s, pa_r, pb_r, wa_r, wb_r, a2_s, b2_s, a2_r, b2_r,
 ):
     me, y, xh, z = place()
     mine = y * 4 + z
@@ -398,7 +513,6 @@
     lax.fori_loop(1, 16, greet, 0)
     pl.semaphore_wait(barrier, 15)
 
-    upper, lower = pl.ds(0, HALF), pl.ds(HALF, HALF)
     sent = []
 
     def send(src, dst, ssem, rsem, to):
@@ -409,12 +523,15 @@
     def arrived(dst, rsem):
         remote(dst, dst, g_s.at[0], rsem, wide=dev(mine)).wait_recv()
 
+    ring = Ring(
+        lambda Y, Z, first, count: fall.at[pl.ds(first, count), cols(Y * 4 + Z)],
+        lambda Y, Z, index: g_r.at[Y * 4 + Z, index],
+        QUART,
+        g_s,
+        0,
+    )
+    ring.own(final)
     fall[:, cols(mine)] = final[...]
-    used = 0
-    for k in (1, 3, 2):
-        for to in (flat(turn4(y, k), xh, z), flat(y, xh, turn4(z, k))):
-            send(final, fall.at[:, cols(mine)], g_s.at[used], g_r.at[mine, 0], to)
-            used += 1
 
     def logits(j):
         seen = fall[:, cols(j)]
@@ -435,43 +552,40 @@
         tops[j] = jnp.concatenate(tip + [zero] * (8 - NCH), 0)
         stat[j] = jnp.concatenate([top, total, hit] + [zero] * 5, 0)
 
-    logits(mine)
-    for k in (1, 3, 2):
-        row, column = turn4(y, k), turn4(z, k)
-        block = row * 4 + z
-        arrived(fall.at[:, cols(block)], g_r.at[block, 0])
-        for m in (1, 3, 2):
-            piece = fall.at[upper, cols(block)]
-            send(piece, piece, g_s.at[used], g_r.at[block, 0], flat(y, xh, turn4(z, m)))
-            used += 1
-        block = y * 4 + column
-        arrived(fall.at[:, cols(block)], g_r.at[block, 0])
-        for m in (1, 3, 2):
-            piece = fall.at[lower, cols(block)]
-            send(piece, piece, g_s.at[used], g_r.at[block, 1], flat(turn4(y, m), xh, z))
-            used += 1
-
     def tell(j):
         return remote(stat.at[j], stat_in.at[mine], st_s.at[j], st_r.at[mine], wide=dev(j))
 
-    def block_at(k):
-        return turn4(y, k // 4) * 4 + turn4(z, lax.rem(k, 4))
-
-    def forward(k, carry):
-        j = block_at(k)
-        dy, dz = k // 4, lax.rem(k, 4)
-
-        @pl.when((dy > 0) & (dz > 0))
-        def _():
-            arrived(fall.at[upper, cols(j)], g_r.at[j, 0])
-            arrived(fall.at[lower, cols(j)], g_r.at[j, 1])
-
-        logits(j)
-        tell(j).start()
-        return carry
-
+    def block(dy, dz):
+        return turn4(y, dy) * 4 + turn4(z, dz)
+
+    def forward(offsets):
+        def one(k, carry):
+            j = block(*offsets(k))
+            logits(j)
+            tell(j).start()
+            return carry
+
+        return one
+
+    def odd(k):
+        return 1 + 2 * lax.rem(k, 2)
+
+    logits(mine)
     stat_in[mine] = stat[mine]
-    lax.fori_loop(1, 16, forward, 0)
+    ring.near()
+    lax.fori_loop(0, 4, forward(lambda k: ((1 - k // 2) * odd(k), (k // 2) * odd(k))), 0)
+    ring.far()
+    lax.fori_loop(0, 2, forward(lambda k: (2 * (1 - k), 2 * k)), 0)
+    ring.cross()
+    lax.fori_loop(0, 4, forward(lambda k: (odd(k // 2), odd(k))), 0)
+    ring.last()
+    lax.fori_loop(
+        0,
+        4,
+        forward(lambda k: (2 * (1 - k // 2) + odd(k) * (k // 2), odd(k) * (1 - k // 2) + 2 * (k // 2))),
+        0,
+    )
+    forward(lambda k: (2, 2))(0, 0)
 
     def hear(k, carry):
         j = lax.rem(mine + k, 16)
@@ -503,29 +617,79 @@
 
     lax.fori_loop(1, 16, spread_start, 0)
 
-    def piece_a(dz, row):
+    up, down = 1, 3
+    z_to = {step: flat(y, xh, turn4(z, step)) for step in (up, down)}
+    y_to = {step: flat(turn4(y, step), xh, z) for step in (up, down)}
+
+    def piece_a(j, index):
+        row = j // 4
         return remote(
-            parts.at[row * 4 + turn4(z, dz), upper],
-            in_a.at[dz - 1, row],
-            a_s.at[dz - 1, row],
-            a_r.at[dz - 1, row],
-            wide=flat(y, xh, turn4(z, dz)),
+            parts.at[j, pl.ds(index * QUART, QUART)], part_a.at[index, row],
+            a_s.at[j, index], pa_r.at[index, row], wide=z_to[(up, down)[index]],
         )
 
-    def piece_b(dy, column):
+    def piece_b(j, index):
+        column = lax.rem(j, 4)
         return remote(
-            parts.at[turn4(y, dy) * 4 + column, lower],
-            in_b.at[dy - 1, column],
-            b_s.at[dy - 1, column],
-            b_r.at[dy - 1, column],
-            wide=flat(turn4(y, dy), xh, z),
+            parts.at[j, pl.ds((2 + index) * QUART, QUART)], part_b.at[index, column],
+            b_s.at[j, index], pb_r.at[index, column], wide=y_to[(up, down)[index]],
         )
 
+    def half_a(j, index):
+        row = j // 4
+        return remote(
+            parts.at[j, pl.ds(0, 2 * QUART)], whole_a.at[index, row],
+            a_s.at[j, 0], wa_r.at[index, row], wide=z_to[(up, down)[index]],
+        )
+
+    def half_b(j, index):
+        column = lax.rem(j, 4)
+        return remote(
+            parts.at[j, pl.ds(2 * QUART, 2 * QUART)], whole_b.at[index, column],
+            b_s.at[j, 0], wb_r.at[index, column], wide=y_to[(up, down)[index]],
+        )
+
+    def offsets(k):
+        return lax.rem(2 + k // 4, 4), lax.rem(2 + k, 4)
+
+    def post(k):
+        dy, dz = offsets(k)
+        j = block(dy, dz)
+
+        @pl.when(dz == 2)
+        def _():
+            piece_a(j, 0).start()
+            piece_a(j, 1).start()
+
+        @pl.when(dy == 2)
+        def _():
+            piece_b(j, 0).start()
+            piece_b(j, 1).start()
+
+        for index, step in enumerate((up, down)):
+
+            @pl.when(dz == step)
+            def _():
+                row = j // 4
+                arrived(part_a.at[index, row], pa_r.at[index, row])
+                rows = pl.ds(index * QUART, QUART)
+                total = parts[j, rows, :].astype(F32) + part_a[index, row].astype(F32)
+                parts[j, rows, :] = total.astype(BF)
+                half_a(j, index).start()
+
+            @pl.when(dy == step)
+            def _():
+                column = lax.rem(j, 4)
+                arrived(part_b.at[index, column], pb_r.at[index, column])
+                rows = pl.ds((2 + index) * QUART, QUART)
+                total = parts[j, rows, :].astype(F32) + part_b[index, column].astype(F32)
+                parts[j, rows, :] = total.astype(BF)
+                half_b(j, index).start()
+
     def backward(k, carry):
-        j = block_at(15 - k)
-        dy, dz = (15 - k) // 4, lax.rem(15 - k, 4)
-
-        @pl.when(k < 15)
+        j = block(*offsets(k))
+
+        @pl.when(k != 10)
         def _():
             arrived(coef_in.at[j], co_r.at[j])
 
@@ -541,17 +705,14 @@
         product += jnp.dot(table_other[...], expo[SHARD:VOC, cols(j)], preferred_element_type=F32)
         parts[j] = product.astype(BF)
 
-        @pl.when(dz > 0)
+        @pl.when(k > 0)
         def _():
-            piece_a(dz, j // 4).start()
-
-        @pl.when(dy > 0)
-        def _():
-            piece_b(dy, lax.rem(j, 4)).start()
+            post(k - 1)
 
         return carry
 
     lax.fori_loop(0, 16, backward, 0)
+    post(15)
 
     def head_chunk(c):
         return lax.dot_general(
@@ -565,59 +726,69 @@
         head_other[:, cols(c)] = head_chunk(c + SHARD // 256).astype(BF)
         return carry
 
-    lax.fori_loop(0, SHARD // 256, other_chunk, 0)
-
-    keep_a = keep_b = None
-    for d in (3, 2, 1, 0):
-        row = turn4(y, d)
-        acc = parts[row * 4 + z, 0:HALF, :].astype(F32)
-        for m in (1, 2, 3):
-            arrived(in_a.at[m - 1, row], a_r.at[m - 1, row])
-            acc = acc + in_a[m - 1, row].astype(F32)
-        if d:
-            sum_a[d - 1] = acc.astype(BF)
-            send(sum_a.at[d - 1], in_a2.at[d - 1], a2_s.at[d - 1], a2_r.at[d - 1], flat(row, xh, z))
-        else:
-            keep_a = acc
-        column = turn4(z, d)
-        acc = parts[y * 4 + column, HALF:D, :].astype(F32)
-        for m in (1, 2, 3):
-            arrived(in_b.at[m - 1, column], b_r.at[m - 1, column])
-            acc = acc + in_b[m - 1, column].astype(F32)
-        if d:
-            sum_b[d - 1] = acc.astype(BF)
-            send(sum_b.at[d - 1], in_b2.at[d - 1], b2_s.at[d - 1], b2_r.at[d - 1], flat(y, xh, column))
-        else:
-            keep_b = acc
-    grad_final[0:HALF, :] = keep_a
-    grad_final[HALF:D, :] = keep_b
-
     def own_chunk(c, carry):
         head_own[:, cols(c)] = head_chunk(c)
         return carry
 
-    lax.fori_loop(0, SHARD // 256, own_chunk, 0)
-    for d in (1, 2, 3):
-        arrived(in_a2.at[d - 1], a2_r.at[d - 1])
-        arrived(in_b2.at[d - 1], b2_r.at[d - 1])
-    grad_final[0:HALF, :] += sum(in_a2[d].astype(F32) for d in range(3))
-    grad_final[HALF:D, :] += sum(in_b2[d].astype(F32) for d in range(3))
+    lax.fori_loop(0, SHARD // 256, other_chunk, 0)
+
+    kinds = (
+        (whole_a, wa_r, sum_a, part_a2, whole_a2, a2_s, a2_r, y_to, 0),
+        (whole_b, wb_r, sum_b, part_b2, whole_b2, b2_s, b2_r, z_to, 2 * QUART),
+    )
+    for d in (2, 1, 3, 0):
+        for kind, (whole, w_r, total, part2, whole2, s2, r2, to, base) in enumerate(kinds):
+            at = turn4(y if kind == 0 else z, d)
+            j = at * 4 + z if kind == 0 else y * 4 + at
+            acc = parts[j, base : base + 2 * QUART, :].astype(F32)
+            for index in range(2):
+                arrived(whole.at[index, at], w_r.at[index, at])
+                acc = acc + whole[index, at].astype(F32)
+            if d == 0:
+                grad_final[base : base + 2 * QUART, :] = acc
+            else:
+                total[d - 1] = acc.astype(BF)
+            if d == 2:
+                for index, step in enumerate((up, down)):
+                    piece = total.at[1, pl.ds(index * QUART, QUART)]
+                    send(piece, part2.at[index], s2.at[index], r2.at[index], to[step])
+    lax.fori_loop(0, SHARD // 512, own_chunk, 0)
+    for kind, (whole, w_r, total, part2, whole2, s2, r2, to, base) in enumerate(kinds):
+        for index, step in enumerate((up, down)):
+            arrived(part2.at[index], r2.at[index])
+            rows = pl.ds(index * QUART, QUART)
+            added = total[step - 1, rows, :].astype(F32) + part2[index].astype(F32)
+            total[step - 1, rows, :] = added.astype(BF)
+            send(total.at[step - 1], whole2.at[index], s2.at[2 + index], r2.at[2 + index], to[step])
+    lax.fori_loop(SHARD // 512, SHARD // 256, own_chunk, 0)
+    for kind, (whole, w_r, total, part2, whole2, s2, r2, to, base) in enumerate(kinds):
+        for index in range(2):
+            arrived(whole2.at[index], r2.at[2 + index])
+        grad_final[base : base + 2 * QUART, :] += whole2[0].astype(F32) + whole2[1].astype(F32)
 
     def finish(k, carry):
-        tell(block_at(k)).wait_send()
+        j = lax.rem(mine + k, 16)
+        tell(j).wait_send()
         spread(k).wait_send()
         return carry
 
     lax.fori_loop(1, 16, finish, 0)
     for copy in sent:
         copy.wait_send()
+    ring.finish()
 
     def finish_pieces(k, carry):
-        piece_a(k // 4 + 1, lax.rem(k, 4)).wait_send()
-        piece_b(k // 4 + 1, lax.rem(k, 4)).wait_send()
+        row, column = block(k, 2), block(2, k)
+        piece_a(row, 0).wait_send()
+        piece_a(row, 1).wait_send()
+        piece_b(column, 0).wait_send()
+        piece_b(column, 1).wait_send()
+        for index, step in enumerate((up, down)):
+            half_a(block(k, step), index).wait_send()
+            half_b(block(step, k), index).wait_send()
         return carry
 
-    lax.fori_loop(0, 12, finish_pieces, 0)
+    lax.fori_loop(0, 4, finish_pieces, 0)
 
 
 def head(final, rows_t, table, table_other, goal, weights):
@@ -641,26 +812,32 @@
             pltpu.VMEM((8, T), F32),
             pltpu.VMEM((16, 8, T), F32),
             pltpu.VMEM((16, D, T), BF),
-            pltpu.VMEM((3, 4, HALF, T), BF),
-            pltpu.VMEM((3, 4, HALF, T), BF),
-            pltpu.VMEM((3, HALF, T), BF),
-            pltpu.VMEM((3, HALF, T), BF),
-            pltpu.VMEM((3, HALF, T), BF),
-            pltpu.VMEM((3, HALF, T), BF),
-            DMA((24,)),
-            DMA((16, 2)),
+            pltpu.VMEM((2, 4, QUART, T), BF),
+            pltpu.VMEM((2, 4, QUART, T), BF),
+            pltpu.VMEM((2, 4, 2 * QUART, T), BF),
+            pltpu.VMEM((2, 4, 2 * QUART, T), BF),
+            pltpu.VMEM((3, 2 * QUART, T), BF),
+            pltpu.VMEM((3, 2 * QUART, T), BF),
+            pltpu.VMEM((2, QUART, T), BF),
+            pltpu.VMEM((2, QUART, T), BF),
+            pltpu.VMEM((2, 2 * QUART, T), BF),
+            pltpu.VMEM((2, 2 * QUART, T), BF),
+            DMA((RING_SENDS,)),
+            DMA((16, 4)),
             DMA((16,)),
             DMA((16,)),
             DMA((16,)),
             DMA((16,)),
-            DMA((3, 4)),
-            DMA((3, 4)),
-            DMA((3, 4)),
-            DMA((3, 4)),
-            DMA((3,)),
-            DMA((3,)),
-            DMA((3,)),
-            DMA((3,)),
+            DMA((16, 2)),
+            DMA((16, 2)),
+            DMA((2, 4)),
+            DMA((2, 4)),
+            DMA((2, 4)),
+            DMA((2, 4)),
+            DMA((4,)),
+            DMA((4,)),
+            DMA((4,)),
+            DMA((4,)),
         ],
         compiler_params=params(4, 61),
         cost_estimate=pl.CostEstimate(
@@ -670,65 +847,84 @@
 
 
 class Reduce:
-    def __init__(self, parts, first, first_in, second, second_in, third, third_in, rows, along_z, sems):
-        self.parts, self.first, self.first_in = parts, first, first_in
-        self.second, self.second_in = second, second_in
-        self.third, self.third_in = third, third_in
-        self.rows, self.along_z = rows, along_z
-        self.s, self.r = sems
+    def __init__(self, parts, base, quarter, along_z, refs):
+        (
+            self.first, self.part1, self.whole1, self.second, self.part2, self.whole2,
+            self.third, self.stop, self.third_in, self.s, self.r,
+        ) = refs
+        self.parts, self.base, self.q, self.along_z = parts, base, quarter, along_z
         self.me, self.y, self.xh, self.z = place()
         self.sent = []
 
-    def send(self, src, dst, at, to):
-        copy = remote(src, dst, self.s.at[at], self.r.at[at], wide=to)
+    def send(self, src, dst, at, **to):
+        copy = remote(src, dst, self.s.at[at], self.r.at[at], **to)
         copy.start()
         self.sent.append(copy)
 
     def wait(self, dst, at):
         remote(dst, dst, self.s.at[at], self.r.at[at], wide=self.me).wait_recv()
 
-    def one(self, d):
+    def item1(self, step, first, count):
+        rows = pl.ds(self.base + first * self.q, count * self.q)
         if self.along_z:
-            at = turn4(self.z, d)
-            return flat(self.y, self.xh, at), (slice(None), slice(None), at, self.rows)
-        at = turn4(self.y, d)
-        return flat(at, self.xh, self.z), (at, slice(None), slice(None), self.rows)
-
-    def start(self):
-        for d in (2, 1, 3):
-            to, index = self.one(d)
-            self.send(self.parts.at[index], self.first_in.at[d - 1], d - 1, to)
-
-    def middle(self):
-        _, index = self.one(0)
-        for d in (1, 2, 3):
-            self.wait(self.first_in.at[d - 1], d - 1)
-        acc = self.parts[index].astype(F32)
-        for d in (1, 2, 3):
-            acc = acc + self.first_in[d - 1].astype(F32)
-        self.first[...] = acc.astype(BF)
-        for d in (2, 1, 3):
-            if self.along_z:
-                at = turn4(self.y, d)
-                src, to = self.first.at[at], flat(at, self.xh, self.z)
-            else:
-                at = turn4(self.z, d)
-                src, to = self.first.at[:, at], flat(self.y, self.xh, at)
-            self.send(src, self.second_in.at[d - 1], 2 + d, to)
-
-    def last(self):
-        for d in (1, 2, 3):
-            self.wait(self.second_in.at[d - 1], 2 + d)
-        own = self.first[self.y] if self.along_z else self.first[:, self.z]
-        acc = own.astype(F32)
-        for d in (1, 2, 3):
-            acc = acc + self.second_in[d - 1].astype(F32)
-        self.second[...] = acc
+            return (slice(None), slice(None), turn4(self.z, step), rows)
+        return (turn4(self.y, step), slice(None), slice(None), rows)
+
+    def item2(self, step, first, count):
+        rows = pl.ds(first * self.q, count * self.q)
+        if self.along_z:
+            return (turn4(self.y, step), slice(None), rows)
+        return (slice(None), turn4(self.z, step), rows)
+
+    def to(self, stage, step):
+        if self.along_z == (stage == 1):
+            return flat(self.y, self.xh, turn4(self.z, step))
+        return flat(turn4(self.y, step), self.xh, self.z)
+
+    def split(self, stage, ref, item, part, base):
+        for index, step in enumerate((1, 3)):
+            self.send(ref.at[item(2, index, 1)], part.at[index], base + index, wide=self.to(stage, step))
+
+    def join(self, stage, ref, item, part, whole, base):
+        for index, step in enumerate((1, 3)):
+            self.wait(part.at[index], base + index)
+            at = item(step, index, 1)
+            ref[at] = (ref[at].astype(F32) + part[index].astype(F32)).astype(BF)
+            self.send(
+                ref.at[item(step, 0, 2)], whole.at[index], base + 2 + index, wide=self.to(stage, step)
+            )
+
+    def add(self, ref, item, whole, base):
+        acc = ref[item(0, 0, 2)].astype(F32)
+        for index in range(2):
+            self.wait(whole.at[index], base + 2 + index)
+            acc = acc + whole[index].astype(F32)
+        return acc
+
+    def one(self):
+        self.split(1, self.parts, self.item1, self.part1, 0)
+
+    def two(self):
+        self.join(1, self.parts, self.item1, self.part1, self.whole1, 0)
+
+    def three(self):
+        self.first[...] = self.add(self.parts, self.item1, self.whole1, 0).astype(BF)
+        self.split(2, self.first, self.item2, self.part2, 4)
+
+    def four(self):
+        self.join(2, self.first, self.item2, self.part2, self.whole2, 4)
+
+    def five(self):
+        self.second[...] = self.add(self.first, self.item2, self.whole2, 4)
         self.third[...] = self.second[1 - self.xh].astype(BF)
-        self.send(self.third, self.third_in, 6, flat(self.y, 1 - self.xh, self.z))
+        self.send(self.third, self.stop, 8, **beside(1 if self.along_z else 3))
+
+    def six(self):
+        self.wait(self.stop, 8)
+        self.send(self.stop, self.third_in, 9, **beside(1 if self.along_z else 3))
 
     def total(self):
-        self.wait(self.third_in, 6)
+        self.wait(self.third_in, 9)
         return self.second[self.xh] + self.third_in[...].astype(F32)
 
     def finish(self):
@@ -739,62 +935,83 @@
 def reduce_scratch(half, lanes):
     shapes = []
     for group in ((4, 2), (2, 4)):
+        quarter = half // 2
         shapes += [
             pltpu.VMEM(group + (half, lanes), BF),
-            pltpu.VMEM((3,) + group + (half, lanes), BF),
+            pltpu.VMEM((2,) + group + (quarter, lanes), BF),
+            pltpu.VMEM((2,) + group + (half, lanes), BF),
             pltpu.VMEM((2, half, lanes), F32),
-            pltpu.VMEM((3, 2, half, lanes), BF),
+            pltpu.VMEM((2, 2, quarter, lanes), BF),
+            pltpu.VMEM((2, 2, half, lanes), BF),
             pltpu.VMEM((half, lanes), BF),
             pltpu.VMEM((half, lanes), BF),
-            DMA((7,)),
-            DMA((7,)),
+            pltpu.VMEM((half, lanes), BF),
+            DMA((10,)),
+            DMA((10,)),
         ]
     return shapes
 
 
-def back_kernel(fa, wp, rows, head_other, extra, fa_sum, wp_sum, rows_in, head_in, extra_sum, *scratch):
+def back_kernel(fa_in, wp_in, rows, head_other, extra, fa_sum, wp_sum, rows_in, head_in, extra_sum, *scratch):
     me, y, xh, z = place()
-    greet_wide(me)
+    greet_wide(me, sides=True)
+    fa, wp, extra_in, stops, row_s, row_r, extra_s, extra_r, swap_s, swap_r, local = scratch[44:]
+    loads = [
+        pltpu.make_async_copy(fa_in, fa, local.at[0]),
+        pltpu.make_async_copy(wp_in, wp, local.at[1]),
+    ]
+    for load in loads:
+        load.start()
+    halves = (pl.ds(0, D // 2), pl.ds(D // 2, D // 2))
+    trade = Relay(
+        [head_other.at[half] for half in halves],
+        [stops.at[i] for i in range(2)],
+        [head_in.at[half] for half in halves],
+        swap_s,
+        swap_r,
+    )
+    for load in loads:
+        load.wait()
     streams = []
-    for parts, rows_of, at in ((fa, FA_ROWS, 0), (wp, WP_ROWS, 16)):
+    for parts, rows_of, at in ((fa, FA_ROWS, 0), (wp, WP_ROWS, 22)):
         for half in range(2):
-            base = at + half * 8
-            f, f_in, s, s_in, t, t_in, sends, recvs = scratch[base : base + 8]
-            streams.append(
-                Reduce(
-                    parts, f, f_in, s, s_in, t, t_in,
-                    pl.ds(half * rows_of // 2, rows_of // 2), half == 0, (sends, recvs),
-                )
-            )
-    extra_in, row_s, row_r, extra_s, extra_r, swap = scratch[32:]
+            refs = scratch[at + 11 * half : at + 11 * half + 11]
+            streams.append(Reduce(parts, half * rows_of // 2, rows_of // 4, half == 0, refs))
     for stream in streams:
-        stream.start()
+        stream.one()
+    trade.start()
     give = Scatter(lambda p: rows.at[slots(p)], lambda p: rows_in.at[slots(p)], row_s, row_r, me)
     give.start()
     share = Scatter(lambda p: extra, lambda p: extra_in.at[p], extra_s, extra_r, me)
     share.start()
-    trade = remote(head_other, head_in, swap.at[0], swap.at[1], wide=flat(y, 1 - xh, z))
-    trade.start()
     rows_in[slots(me), :] = rows[slots(me), :]
     extra_in[me] = extra[...]
     for stream in streams:
-        stream.middle()
+        stream.two()
+    trade.forward()
     for stream in streams:
-        stream.last()
+        stream.three()
+    for stream in streams:
+        stream.four()
+    for stream in streams:
+        stream.five()
     share.wait_recv()
     total = extra_in[0]
     for w in range(1, NW):
         total = total + extra_in[w]
     extra_sum[...] = total
+    for stream in streams:
+        stream.six()
     for out, pair, half in ((fa_sum, streams[:2], FA_ROWS // 2), (wp_sum, streams[2:], WP_ROWS // 2)):
         out[0:half, :] = pair[0].total()
         out[half : 2 * half, :] = pair[1].total()
     give.wait_recv()
+    trade.wait()
     for stream in streams:
         stream.finish()
     give.wait_send()
     share.wait_send()
-    trade.wait()
+    trade.finish()
 
 
 def back(fa, wp, rows, head_other, extra):
@@ -808,13 +1025,18 @@
             jax.ShapeDtypeStruct((D, SHARD), BF),
             jax.ShapeDtypeStruct((8, 640), F32),
         ),
-        in_specs=[VMEM, VMEM, VMEM, ANY, VMEM],
+        in_specs=[ANY, ANY, VMEM, ANY, VMEM],
         out_specs=(VMEM, VMEM, VMEM, ANY, VMEM),
         scratch_shapes=reduce_scratch(FA_ROWS // 2, D)
         + reduce_scratch(WP_ROWS // 2, 128)
-        + [pltpu.VMEM((NW, 8, 640), F32)]
+        + [
+            pltpu.VMEM((4, 2, 4, FA_ROWS, D), BF),
+            pltpu.VMEM((4, 2, 4, WP_ROWS, 128), BF),
+            pltpu.VMEM((NW, 8, 640), F32),
+            pltpu.VMEM((2, D // 2, SHARD), BF),
+        ]
         + [DMA((NW,))] * 4
-        + [DMA((2,))],
+        + [DMA((4,)), DMA((4,)), DMA((2,))],
         compiler_params=params(5, 48),
         cost_estimate=pl.CostEstimate(flops=10**8, bytes_accessed=3 * 10**7, transcendentals=0),
     )(fa, wp, rows, head_other, extra)
@@ -1130,7 +1352,7 @@
     picks = slot_picks(0)
     fa = pack_fa(attn_in_master[0].T, ffn_in_master[0].T).astype(BF)
     wp = pack_wp(proj_out_master[0].T).astype(BF)
-    got, rows, most_all, table_other, fa_all, wp_all = front(message(picks), table, fa, wp)
+    got, rows, most_all, table_other, rows_t, fa_all, wp_all = front(message(picks), table, fa, wp)
     turns = (jnp.max(most_all) + CAP - 1) // CAP
 
     def to_tokens(rows, picks):
@@ -1165,7 +1387,6 @@
     weights = jnp.concatenate(
         [jnp.full((1, T), plain / total, F32), jnp.full((1, T), plain, F32), jnp.zeros((6, T), F32)], 0
     )
-    rows_t = jnp.concatenate([table, table_other], 1).T
     grad_final, head_own, head_other, loss = head(final, rows_t, table, table_other, goals, weights)
 
     grad_embedded, grad_attn, grad_ffn, grad_proj, grad_gains = layer_backward(

time: 506 us -> 476 us (0.941)
  Pallas kernels: 324 us -> 306 us
  local copies, waits for them, and re-layouts: 68.9 us -> 60.6 us
    pallas_call x1, Pallas kernels: 88.9 us -> 77.1 us  [back(): pl.pallas_call(back_kernel, name='back', out_shape=(jax.ShapeDtypeStruct(...]
    pallas_call x1, Pallas kernels: 83.7 us -> 75.1 us  [front(): pl.pallas_call(front_kernel, name='front', out_shape=(jax.ShapeDtypeStruc...]
    pallas_call x1, Pallas kernels: 32.1 us -> 39 us  [group_sum(): pl.pallas_call(group_kernel, name='group_sum', out_shape=tuple((jax.Shape...]
    transpose x1 -> x0, local copies, waits for them, and re-layouts: 6.09 us -> none  [on_device(): rows_t = jnp.concatenate([table, table_other], 1).T]
    unnamed x158 -> x154, local copies, waits for them, and re-layouts: 15.2 us -> 12.9 us
where the time goes in v2:
time: 476 us; the launch traced here: 468 us
  Pallas kernels  306 us (64%)
  other arithmetic  61.7 us (13%)
  local copies, waits for them, and re-layouts  60.6 us (13%)
  matrix products  28.6 us (6%)
  between operations  10.5 us (2%)
    pallas_call x1, Pallas kernels, head(): pl.pallas_call(head_kernel, name='head', out_shape=(jax.ShapeDtypeStruct(...  105 us
    pallas_call x1, Pallas kernels, back(): pl.pallas_call(back_kernel, name='back', out_shape=(jax.ShapeDtypeStruct(...  77.1 us
    pallas_call x1, Pallas kernels, front(): pl.pallas_call(front_kernel, name='front', out_shape=(jax.ShapeDtypeStruc...  75.1 us
    pallas_call x1, Pallas kernels, group_sum(): pl.pallas_call(group_kernel, name='group_sum', out_shape=tuple((jax.Shape...  39 us
    dot_general x20, matrix products, dot(): return jnp.einsum(spec, a, b, preferred_element_type=F32)  26.3 us
    transpose x5, other arithmetic, on_device(): values = [value.T for value in values]  16.5 us
    unnamed x154, local copies, waits for them, and re-layouts  12.9 us
    pallas_call x1, Pallas kernels, norm_sum(): pl.pallas_call(norm_kernel, name='norm_sum', out_shape=jax.ShapeDtypeStru...  10.2 us

profile of v2, /device:TPU:1, one launch (start us, length us, event | category | flops | bytes accessed | tf_op | source)
XLA Modules:
  0.0 468.0 jit_solution(10659357204518608817)
XLA Ops:
  0.7 1.3 fusion.103
  3.4 0.9 fusion.57
  4.4 1.3 multiply_subtract_fusion.2
  6.4 1.0 convert_reduce_fusion
  8.7 0.8 add_add_fusion.3
  9.8 1.3 slice_reduce_fusion.3
  11.1 0.9 copy.186
  12.3 1.5 fusion.58
  13.7 0.9 copy.185
  14.8 1.0 bitcast_convert_fusion.1
  16.6 2.2 bitcast_convert_fusion.table
  18.8 75.1 %front.1 = (s32[32,8,128]{2,1,0:T(8,128)S(1)}, bf16[1024,576]{1,0:T(8,128)(2,1)S(1)}, s32[4,8,128]{2,1,0:T(8,128)S(1)}, bf16[576,1536]{1,0:T(8,128)(2,1)S(1)}, b...) custom-call(s32[32,8,128]{2,1,0:T(8,128)S(1)} %select_add_fusion.2.msg, ...), custom_call_target="tpu_custom_call" | custom-call | flops 2000000000 | bytes 30000000 | tf_op jit(solution)/shard_map/front/pallas_call | solution.py:379
  94.0 1.0 copy-done.3
  95.0 1.2 copy-done.5
  99.0 1.6 slice.184
  101.3 5.1 %reshape.442 = bf16[576,2112]{1,0:T(8,128)(2,1)} reshape(bf16[32,297,128]{2,1,0:T(8,128)(2,1)} %slice.184) | data formatting | bytes 4866048 | tf_op jit(solution)/shard_map/reshape | solution.py:1372
  107.9 1.4 fusion.41
  109.5 1.2 multiply_reduce_fusion.9
  110.7 2.5 slice.187
  113.2 4.4 slice.196
  117.6 2.5 reshape.443
  120.2 2.0 fusion.112
  123.7 2.3 fusion.116
  126.0 2.2 convolution_convert_fusion.6
  128.8 0.7 copy-done.8
  129.6 1.5 fusion.113
  131.6 0.8 multiply_reduce_fusion.7
  133.6 0.9 multiply_convert_fusion.3.final
  134.4 104.7 %head.1 = (f32[576,256]{1,0:T(8,128)}, f32[576,1536]{1,0:T(8,128)}, bf16[576,1536]{1,0:T(8,128)(2,1)}, f32[8,256]{1,0:T(8,128)}) custom-call(bf16[576,256]{1,0:T(8,128)(2,1)} %multiply_convert_fusion.3.final, bf16[3072,576]{1,0:T(8,128)(2,1)} %get-tuple-element.208.rows_t, bf16[576,1536]{1,0:T(8,128)(2,1)S(1)} %get-tuple-element.716, ...), custom_call_target="tpu_custom_call" | custom-call | flops 43486543872 | bytes 20000000 | tf_op jit(solution)/shard_map/head/pallas_call | solution.py:795
  239.2 1.5 slice_reduce_fusion.6
  240.6 1.5 multiply_reduce_fusion.1
  242.2 1.4 multiply_subtract_fusion
  243.6 4.0 multiply_convert_fusion.1
  247.7 1.3 multiply_reduce_fusion.2
  249.7 1.3 copy-done.26
  251.0 1.2 fusion.40
  253.3 0.8 pad_maximum_fusion
  254.1 3.8 convert_element_type.122
  257.9 3.7 pad.54
  261.6 2.9 convolution_convert_fusion.1
  264.5 6.3 %copy.100 = bf16[3072,576]{1,0:T(8,128)(2,1)} copy(bf16[3072,576]{0,1:T(8,128)(2,1)} %convolution_convert_fusion.1) | data formatting | bytes 7077888 | tf_op jit(solution)/shard_map/convert_element_type | solution.py:1396
  275.1 0.9 scatter.11.extra
  276.5 1.1 copy.101
  278.1 5.3 %fusion.17 = bf16[32,128,576]{2,1,0:T(8,128)(2,1)} fusion(bf16[32,30,576]{2,1,0:T(8,128)(2,1)S(1)} %reshape.453, bf16[32,96,576]{2,1,0:T(8,128)(2,1)} %bitcast.367), kind=kLoop, calls=%fused_computation.32 | loop fusion | flops 16515072 | bytes 9363456 | tf_op jit(solution)/shard_map/concatenate | solution.py:1272
  284.0 0.7 copy.102.rows
  284.7 77.1 %back.1 = (f32[128,576]{1,0:T(8,128)S(1)}, f32[320,128]{1,0:T(8,128)S(1)}, bf16[1024,576]{1,0:T(8,128)(2,1)S(1)}, bf16[576,1536]{1,0:T(8,128)(2,1)S(1)}, f32[8,640]{1,0:T(8,128)S(1)}) custom-call(bf16[4,2,4,128,576]{4,3,2,1,0:T(8,128)(2,1)} %bitcast.364, bf16[4,2,4,320,128]{4,3,2,1,0:T(8,128)(2,1)} %bitcast.368, bf16[1024,576]{1,0:T(8,128)(2,1)S(1)} %copy.102.rows, ...), custom_call_target="tpu_custom_call" | custom-call | flops 100000000 | bytes 30000000 | tf_op jit(solution)/shard_map/back/pallas_call | solution.py:1018
  364.3 4.1 add_add_fusion.2
  368.8 3.7 multiply_reduce_fusion
  374.5 10.2 %norm_sum.1 = f32[8,128]{1,0:T(8,128)S(1)} custom-call(f32[8,128]{1,0:T(8,128)S(1)} %broadcast_in_dim.191.value), custom_call_target="tpu_custom_call" | custom-call | tf_op jit(solution)/shard_map/norm_sum/pallas_call | solution.py:1060
  388.5 0.8 mul.920
  390.8 1.0 fusion.94
  391.8 0.8 select_maximum_fusion.refs_1_
  392.6 2.5 fusion.91
  395.1 0.8 broadcast_in_dim.199
  395.8 1.7 reshape.459
  397.5 0.9 pad.56.refs_2_
  398.5 1.7 broadcast_in_dim.198
  400.2 8.3 %fusion.44 = (f32[1,1536,576]{1,2,0:T(8,128)}, f32[576,1536]{1,0:T(8,128)S(1)}, f32[1,1536,576]{1,2,0:T(8,128)}) fusion(f32[576,1536]{1,0:T(8,128)} %get-tuple-element.218, f32[]{:T(128)S(6)} %min.3, f32[1,1536,576]{1,2,0:T(8,128)} %param.45, f32[1,1536,576]{1,2,0:T(8,128)} %param.44, f32[1,1536,576]{1,2,0:T(8,128)S(1)} %copy-done.13, f32[1536,576]{0,1:T(8,128)} %param.46), kind=kLoop, calls=%fused_computation.90 | loop fusion | flops 15040512 | bytes 28311556 | tf_op jit(solution)/shard_map/broadcast_in_dim | solution.py:1510
  408.5 39.0 %group_sum.1 = (f32[576,1536]{1,0:T(8,128)S(1)}, f32[128,576]{1,0:T(8,128)S(1)}, f32[320,128]{1,0:T(8,128)S(1)}, f32[8,640]{1,0:T(8,128)S(1)}) custom-call(f32[576,1536]{1,0:T(8,128)S(1)} %get-tuple-element.443.refs_0_, f32[128,576]{1,0:T(8,128)S(1)} %copy-done, f32[320,128]{1,0:T(8,128)S(1)} %pad.56.refs_2_, f32[8,640]{1,0:T(8,128)S(1)} %copy-done.2), custom_call_target="tpu_custom_call" | custom-call | flops 10000000 | bytes 20000000 | tf_op jit(solution)/shard_map/group_sum/pallas_call | solution.py:1140
  449.5 1.7 div.253
  451.2 1.7 fusion.88
  452.9 2.1 fusion.63
  455.0 1.9 fusion.71
  456.9 8.4 %fusion.22 = (f32[1536,576]{0,1:T(8,128)}, f32[1536,576]{0,1:T(8,128)}, f32[1536,576]{0,1:T(8,128)}) fusion(f32[1536,576]{0,1:T(8,128)} %param.46, f32[1536,576]{0,1:T(8,128)} %param.47, f32[576,1536]{1,0:T(8,128)S(1)} %get-tuple-element.221), kind=kLoop, calls=%fused_computation.44 | loop fusion | flops 6193152 | bytes 21233664 | tf_op jit(solution)/shard_map/transpose | solution.py:1509
  (230 shorter events, 27.3 us)
Async XLA Ops:
  7.3 4.9 %copy-start.41 = (s32[256]{0:T(256)}, s32[256]{0:T(256)S(1)}, u32[]{:S(2)}) copy-start(s32[256]{0:T(256)S(1)} %convert_reduce_fusion) | copy-start | bytes 3076
  8.7 3.6 copy-start.62
  18.8 75.2 %copy-start.6 = (bf16[576,1536]{1,0:T(8,128)(2,1)}, bf16[576,1536]{1,0:T(8,128)(2,1)S(1)}, u32[]{:S(2)}) copy-start(bf16[576,1536]{1,0:T(8,128)(2,1)S(1)} %bitcast_convert_fusion.table) | copy-start | bytes 5308420
  101.3 6.6 %copy-start.4 = (bf16[1024,576]{1,0:T(8,128)(2,1)S(1)}, bf16[1024,576]{1,0:T(8,128)(2,1)}, u32[]{:S(2)}) copy-start(bf16[1024,576]{1,0:T(8,128)(2,1)} %copy-done.3) | copy-start | bytes 3538948
  101.3 6.6 %copy-start.63 = (s32[1,256]{1,0:T(1,128)S(1)}, s32[1,256]{1,0:T(1,128)}, u32[]{:S(2)}) copy-start(s32[1,256]{1,0:T(1,128)} %copy-done.62) | copy-start | bytes 3076
  106.4 2.9 copy-start.7
  106.4 2.9 copy-start.42
  106.4 2.9 copy-start.45
  106.4 2.9 copy-start.47
  106.4 2.9 copy-start.49
  117.6 2.5 copy-start.14
  117.6 2.5 copy-start.58
  120.2 2.8 copy-start.34
  120.2 2.8 copy-start.35
  123.7 4.5 copy-start.28
  123.7 2.3 copy-start.51
  126.0 2.4 copy-start.22
  126.0 3.6 copy-start.8
  126.0 3.6 copy-start.59
  128.8 2.8 copy-start.15
  131.1 1.7 copy-start.10
  131.6 1.4 copy-start.24
  131.6 2.0 copy-start.55
  239.2 4.4 copy-start.23
  243.6 4.0 copy-start.9
  243.6 4.0 copy-start.16
  247.6 1.4 copy-start.71
  247.6 1.4 copy-start.73
  249.0 2.0 copy-start.26
  249.2 3.6 copy-start.18
  249.7 2.5 copy-start.68
  257.9 3.7 copy-start.17
  257.9 3.7 copy-start.72
  257.9 3.7 copy-start.74
  264.5 6.3 %copy-start.27 = (f32[3,3,256,256]{3,2,1,0:T(8,128)S(1)}, f32[3,3,256,256]{3,2,1,0:T(8,128)}, u32[]{:S(2)}) copy-start(f32[3,3,256,256]{3,2,1,0:T(8,128)} %get-tuple-element.493) | copy-start | bytes 7077892
  264.5 6.3 %copy-start.52 = (bf16[192,256]{1,0:T(8,128)(2,1)S(1)}, bf16[192,256]{1,0:T(8,128)(2,1)}, u32[]{:S(2)}) copy-start(bf16[192,256]{1,0:T(8,128)(2,1)} %slice.333) | copy-start | bytes 294916
  264.5 6.3 %copy-start.69 = (bf16[576,256]{1,0:T(8,128)(2,1)S(1)}, bf16[576,256]{1,0:T(8,128)(2,1)}, u32[]{:S(2)}) copy-start(bf16[576,256]{1,0:T(8,128)(2,1)} %copy-done.68) | copy-start | bytes 884740
  272.9 1.3 copy-start.21
  272.9 1.3 copy-start.70
  273.5 1.4 copy-start.19
  278.1 5.3 %copy-start.64 = (s32[1,256]{1,0:T(1,128)S(1)}, s32[1,256]{1,0:T(1,128)}, u32[]{:S(2)}) copy-start(s32[1,256]{1,0:T(1,128)} %copy-done.62) | copy-start | bytes 3076
  284.7 79.6 %copy-start.67 = (s32[1024]{0:T(1024)S(1)}, s32[1024]{0:T(1024)}, u32[]{:S(2)}) copy-start(s32[1024]{0:T(1024)} %eq.136) | copy-start | bytes 12292
  284.7 79.6 %copy-start.75 = (f32[576,1536]{1,0:T(8,128)S(1)}, f32[576,1536]{1,0:T(8,128)}, u32[]{:S(2)}) copy-start(f32[576,1536]{1,0:T(8,128)} %get-tuple-element.215) | copy-start | bytes 10616836
  364.3 4.1 copy-start.43
  364.3 4.1 copy-start.46
  364.3 4.1 copy-start.48
  364.3 4.1 copy-start.50
  368.7 17.9 %copy-start.57 = (f32[3,576]{1,0:T(4,128)S(1)}, f32[3,576]{1,0:T(4,128)}, u32[]{:S(2)}) copy-start(f32[3,576]{1,0:T(4,128)} %param.66) | copy-start | bytes 20740
  368.7 17.9 %copy-start.60 = (f32[1,3,576]{2,0,1:T(1,128)S(1)}, f32[1,3,576]{2,0,1:T(1,128)}, u32[]{:S(2)}) copy-start(f32[1,3,576]{2,0,1:T(1,128)} %param.63) | copy-start | bytes 20740
  368.7 17.9 %copy-start.65 = (f32[1,3,576]{2,0,1:T(1,128)S(1)}, f32[1,3,576]{2,0,1:T(1,128)}, u32[]{:S(2)}) copy-start(f32[1,3,576]{2,0,1:T(1,128)} %param.65) | copy-start | bytes 20740
  368.7 17.9 %copy-start.66 = (f32[1,3,576]{2,0,1:T(1,128)S(1)}, f32[1,3,576]{2,0,1:T(1,128)}, u32[]{:S(2)}) copy-start(f32[1,3,576]{2,0,1:T(1,128)} %param.64) | copy-start | bytes 20740
  368.7 20.5 %copy-start.37 = (f32[576,30]{0,1:T(8,128)S(1)}, f32[576,30]{0,1:T(8,128)}, u32[]{:S(2)}) copy-start(f32[576,30]{0,1:T(8,128)} %param.51) | copy-start | bytes 207364
  368.8 20.5 %copy-start.38 = (f32[1,576,30]{1,0,2:T(1,128)S(1)}, f32[1,576,30]{1,0,2:T(1,128)}, u32[]{:S(2)}) copy-start(f32[1,576,30]{1,0,2:T(1,128)} %param.48) | copy-start | bytes 207364
  368.8 20.5 %copy-start.53 = (f32[1,576,30]{1,0,2:T(1,128)S(1)}, f32[1,576,30]{1,0,2:T(1,128)}, u32[]{:S(2)}) copy-start(f32[1,576,30]{1,0,2:T(1,128)} %param.50) | copy-start | bytes 207364
  368.8 20.5 %copy-start.54 = (f32[1,576,30]{1,0,2:T(1,128)S(1)}, f32[1,576,30]{1,0,2:T(1,128)}, u32[]{:S(2)}) copy-start(f32[1,576,30]{1,0,2:T(1,128)} %param.49) | copy-start | bytes 207364
  368.8 22.0 %copy-start.30 = (f32[1,576,96]{1,2,0:T(8,128)S(1)}, f32[1,576,96]{1,2,0:T(8,128)}, u32[]{:S(2)}) copy-start(f32[1,576,96]{1,2,0:T(8,128)} %param.53) | copy-start | bytes 663556
  368.8 22.0 %copy-start.31 = (f32[576,96]{0,1:T(8,128)S(1)}, f32[576,96]{0,1:T(8,128)}, u32[]{:S(2)}) copy-start(f32[576,96]{0,1:T(8,128)} %param.56) | copy-start | bytes 663556
  368.8 22.0 %copy-start.39 = (f32[1,576,96]{1,2,0:T(8,128)S(1)}, f32[1,576,96]{1,2,0:T(8,128)}, u32[]{:S(2)}) copy-start(f32[1,576,96]{1,2,0:T(8,128)} %param.55) | copy-start | bytes 663556
  368.8 22.0 %copy-start.40 = (f32[1,576,96]{1,2,0:T(8,128)S(1)}, f32[1,576,96]{1,2,0:T(8,128)}, u32[]{:S(2)}) copy-start(f32[1,576,96]{1,2,0:T(8,128)} %param.54) | copy-start | bytes 663556
  389.3 3.3 copy-start.32
  391.8 8.4 %copy-start.13 = (f32[1,1536,576]{1,2,0:T(8,128)S(1)}, f32[1,1536,576]{1,2,0:T(8,128)}, u32[]{:S(2)}) copy-start(f32[1,1536,576]{1,2,0:T(8,128)} %param.43) | copy-start | bytes 10616836
  400.2 8.4 %copy-start = (f32[128,576]{1,0:T(8,128)S(1)}, f32[128,576]{1,0:T(8,128)}, u32[]{:S(2)}) copy-start(f32[128,576]{1,0:T(8,128)} %select_maximum_fusion.refs_1_) | copy-start | bytes 884740
  400.2 8.4 %copy-start.2 = (f32[8,640]{1,0:T(8,128)S(1)}, f32[8,640]{1,0:T(8,128)}, u32[]{:S(2)}) copy-start(f32[8,640]{1,0:T(8,128)} %scatter.14.refs_3_) | copy-start | bytes 61444
  408.5 39.7 %copy-start.61 = (f32[3,576]{1,0:T(4,128)S(1)}, f32[3,576]{1,0:T(4,128)}, u32[]{:S(2)}) copy-start(f32[3,576]{1,0:T(4,128)} %param.67) | copy-start | bytes 20740
  (10 other events, 9.3 us)

commit v3 on v2

--- a/solution.py
+++ b/solution.py
@@ -2,6 +2,7 @@
 
 import jax
 import jax.numpy as jnp
+import numpy as np
 from jax import lax
 from jax.experimental import pallas as pl
 from jax.experimental.pallas import tpu as pltpu
@@ -21,6 +22,8 @@
 CAP = 32
 FA_ROWS = 128
 WP_ROWS = 320
+FFN_AT, DOWN_AT, ATTN_AT, PACKED = 0, 96, 160, 208
+SUMMED = 224
 
 beta_one = 0.9
 beta_two = 0.999
@@ -75,7 +78,7 @@
     )
 
 
-def greet_wide(me, grp=None, sides=False):
+def greet_wide(me, grp=None, sides=False, meanwhile=None):
     barrier = pltpu.get_barrier_semaphore()
 
     def one(k, carry):
@@ -96,6 +99,8 @@
         for step in (1, 3):
             pl.semaphore_signal(barrier, inc=1, device_id=beside(step), device_id_type=MESH)
         count += 2
+    if meanwhile is not None:
+        meanwhile()
     pl.semaphore_wait(barrier, count)
 
 
@@ -135,9 +140,9 @@
 
 
 class Ring:
-    def __init__(self, view, sem, quarter, ssem, at):
-        self.view, self.sem, self.q = view, sem, quarter
-        self.ssem, self.used, self.sent = ssem, at, []
+    def __init__(self, view, sem, bounds, ssem):
+        self.view, self.sem, self.bounds = view, sem, bounds
+        self.ssem, self.used, self.sent = ssem, 0, []
         self.me, self.y, self.xh, self.z = place()
 
     def send(self, src, dst, rsem, to):
@@ -146,25 +151,30 @@
         copy.start()
         self.sent.append(copy)
 
+    def piece(self, y, z, first, count):
+        return self.view(y, z, self.bounds[first], self.bounds[first + count] - self.bounds[first])
+
     def pass_on(self, y, z, first, count, index, *to):
-        piece = self.view(y, z, first * self.q, count * self.q)
+        piece = self.piece(y, z, first, count)
         for one in to:
             self.send(piece, piece, self.sem(y, z, index), one)
 
+    def landed(self, piece, sem):
+        remote(piece, piece, self.ssem.at[0], sem, wide=self.me).wait_recv()
+
     def wait(self, y, z, first, count, index):
-        piece = self.view(y, z, first * self.q, count * self.q)
-        remote(piece, piece, self.ssem.at[0], self.sem(y, z, index), wide=self.me).wait_recv()
+        self.landed(self.piece(y, z, first, count), self.sem(y, z, index))
 
     def around(self):
         y, z = self.y, self.z
         return y, z, (turn4(y, 1), z), (turn4(y, 3), z), (y, turn4(z, 1)), (y, turn4(z, 3))
 
-    def own(self, src):
+    def own(self, src, dst, index):
         y, z, y_up, y_down, z_up, z_down = self.around()
         for to in (y_up, y_down, z_up, z_down):
-            self.send(src, self.view(y, z, 0, 4 * self.q), self.sem(y, z, 0), to)
-
-    def near(self):
+            self.send(src, dst, self.sem(y, z, index), to)
+
+    def near(self, parts=None):
         y, z, y_up, y_down, z_up, z_down = self.around()
         for at, far, turn, half, sides in (
             (y_down, y_up, 0, 0, (z_up, z_down)),
@@ -172,7 +182,11 @@
             (z_down, z_up, 0, 2, (y_up, y_down)),
             (z_up, z_down, 1, 2, (y_up, y_down)),
         ):
-            self.wait(*at, 0, 4, 0)
+            if parts is None:
+                self.wait(*at, 0, 4, 0)
+            else:
+                for part, index in parts:
+                    self.landed(part(*at), self.sem(*at, index))
             self.pass_on(*at, turn, 1, turn, far)
             self.pass_on(*at, 2 + turn, 1, 2 + turn, far)
             self.pass_on(*at, half, 2, half, *sides)
@@ -280,41 +294,92 @@
         rows[first + c : first + c + 256, :] = table[:, c : c + 256].T
 
 
+def owner_of(ids):
+    return (((ids >> 9) * 171) >> 9).astype(jnp.int32)
+
+
+def ask_rows(tok, msg, picks, slot_out):
+    row = tok[0:1, :]
+    column = jnp.broadcast_to(row.astype(F32), (128, T)).T[:, 0:1].astype(jnp.int32)
+    row_owner, column_owner = owner_of(row), owner_of(column)
+    down = lax.broadcasted_iota(jnp.int32, (T, T), 0)
+    across = lax.broadcasted_iota(jnp.int32, (T, T), 1)
+    same = row == column
+
+    def count(which, axis):
+        return jnp.sum(jnp.where(which, 1.0, 0.0), axis, keepdims=True)
+
+    first_row = count(same & (down < across), 0) == 0.0
+    first_column = count(same & (across < down), 1) == 0.0
+    near = row_owner == column_owner
+    rank_row = count(near & (column < row) & first_column, 0)
+    rank_column = count(near & (row < column) & first_row, 1)
+    slot_row = jnp.where(rank_row < CAP, row_owner.astype(F32) * CAP + rank_row, -1.0)
+    slot_column = jnp.where(rank_column < CAP, column_owner.astype(F32) * CAP + rank_column, -1.0)
+    lanes = lax.broadcasted_iota(jnp.int32, (T, NW * CAP), 1).astype(F32)
+    hit = lanes == slot_column
+    picks[...] = jnp.where(hit, 1.0, 0.0).astype(BF)
+    slot_out[...] = jnp.broadcast_to(slot_row, (8, T)).astype(jnp.int32)
+    local = (column - column_owner * SHARD).astype(F32)
+    asked = jnp.max(jnp.where(hit, local, -1.0), 0, keepdims=True).astype(jnp.int32)
+    most = (jnp.max(rank_row, 1, keepdims=True) + 1.0).astype(jnp.int32)
+    rest = [
+        tok[1:2, 0:128], tok[1:2, 128:256], tok[3:4, 0:128], jnp.broadcast_to(most, (1, 128)),
+    ] + [jnp.zeros((1, 128), jnp.int32)] * 3
+    for g in range(8):
+        msg[g] = jnp.concatenate([asked[:, g * 128 : (g + 1) * 128]] + rest, 0)
+
+
+def find_rows(got, table, asked_t, hot, rows, part):
+    asked = got[:, 0, :].astype(F32)
+    asked_t[...] = jnp.concatenate([asked, jnp.full((128 - NW, 128), -1.0, F32)], 0).T
+    mine = asked_t[pl.ds(pl.multiple_of(part * CAP, CAP), CAP), :]
+    lanes = lax.broadcasted_iota(jnp.int32, (CAP, SHARD), 1).astype(F32)
+    for d in range(NW):
+        hot[d * CAP : (d + 1) * CAP, :] = jnp.where(lanes == mine[:, d : d + 1], 1.0, 0.0).astype(BF)
+    step = 8 * CAP
+    for first in range(0, NW * CAP, step):
+        picked = lax.dot_general(
+            hot[first : first + step, :], table[...], (((1,), (1,)), ((), ())), preferred_element_type=F32
+        )
+        rows[first : first + step, :] = picked.astype(BF)
+
+
+def turn_over(table, rows, first):
+    for c in range(0, SHARD, 256):
+        rows[first + c : first + c + 256, :] = table[:, c : c + 256].T
+
+
 def front_kernel(
-    msg, table, fa, wp, got, emb, most, table_other, rows_t, fa_all, wp_all,
-    hot, rows, own_most, stops, msg_s, msg_r, emb_s, emb_r, most_s, most_r, swap_s, swap_r,
-    fa_s, fa_r, wp_s, wp_r, x_s, x_r, local,
+    tok, table, packed, got, emb, most, table_other, rows_t, packed_all, picks, slot_out, hot, goal, weights,
+    msg, asked_t, rows, own_most, stops, msg_s, msg_r, emb_s, emb_r, most_s, most_r, swap_s, swap_r,
+    ring_s, ring_r, x_sem, local,
 ):
     me, y, xh, z = place()
     grp = lax.axis_index("grp")
-    greet_wide(me, grp, sides=True)
-    ask = Scatter(lambda p: msg.at[p], lambda p: got.at[p], msg_s, msg_r, me)
+    other = flat(y, 1 - xh, z)
+    greet_wide(me, grp, sides=True, meanwhile=lambda: ask_rows(tok, msg, picks, slot_out))
+    over = remote(packed, packed_all.at[y, z, xh], x_sem.at[0], x_sem.at[1], wide=other)
+    over.start()
+    ask = Scatter(lambda p: msg.at[p // 4], lambda p: got.at[p], msg_s, msg_r, me)
     ask.start()
-    got[me] = msg[me]
-    other = flat(y, 1 - xh, z)
-    over, own, rings = [], [], []
-    for i, (x, out, size, ssem, rsem) in enumerate(
-        ((fa, fa_all, FA_ROWS, fa_s, fa_r), (wp, wp_all, WP_ROWS, wp_s, wp_r))
-    ):
-        over.append(remote(x, out.at[me], x_s.at[i], x_r.at[i], wide=other))
-        over[-1].start()
-        own.append(pltpu.make_async_copy(x, out.at[me], local.at[i]))
-        own[-1].start()
-        pair = []
-        for k, side in enumerate((xh, 1 - xh)):
-            pair.append(
-                Ring(
-                    lambda Y, Z, first, count, out=out, side=side: out.at[
-                        flat(Y, side, Z), pl.ds(first, count)
-                    ],
-                    lambda Y, Z, index, rsem=rsem, side=side: rsem.at[flat(Y, side, Z), index],
-                    size // 4,
-                    ssem,
-                    k * RING_SENDS,
-                )
-            )
-        rings.append(pair)
-        pair[0].own(x)
+    got[me] = msg[me // 4]
+    ring = Ring(
+        lambda Y, Z, first, count: packed_all.at[Y, Z, :, pl.ds(first, count)],
+        lambda Y, Z, index: ring_r.at[Y, Z, index],
+        (0, 48, 96, 144, 208),
+        ring_s,
+    )
+    ring.own(packed, packed_all.at[y, z, xh], 0)
+    keep = pltpu.make_async_copy(packed, packed_all.at[y, z, xh], local.at[0])
+    keep.start()
+    ask.wait_recv()
+    find_rows(got, table, asked_t, hot, rows, lax.rem(me, 4))
+    reply = Scatter(lambda p: rows.at[slots(p)], lambda p: emb.at[slots(p)], emb_s, emb_r, me)
+    reply.start()
+    over.wait_recv()
+    ring.own(packed_all.at[y, z, 1 - xh], packed_all.at[y, z, 1 - xh], 4)
+    emb[slots(me), :] = rows[slots(me), :]
     halves = (pl.ds(0, D // 2), pl.ds(D // 2, D // 2))
     trade = Relay(
         [table.at[half] for half in halves],
@@ -324,11 +389,12 @@
         swap_r,
     )
     trade.start()
-    ask.wait_recv()
-    look_up(got, table, hot, rows, 0)
-    reply = Scatter(lambda p: rows.at[slots(p)], lambda p: emb.at[slots(p)], emb_s, emb_r, me)
-    reply.start()
-    emb[slots(me), :] = rows[slots(me), :]
+    ring.near(
+        [
+            (lambda Y, Z: packed_all.at[Y, Z, xh], 0),
+            (lambda Y, Z: packed_all.at[Y, Z, 1 - xh], 4),
+        ]
+    )
     largest = jnp.max(got[:, 4, :], 0, keepdims=True)
     own_most[...] = jnp.broadcast_to(largest, (8, 128))
     most[grp] = own_most[...]
@@ -337,45 +403,43 @@
         to = lax.rem(grp + k, NG)
         told.append(remote(own_most, most.at[grp], most_s.at[k], most_r.at[grp], grp=to))
         told[-1].start()
-    for i in range(2):
-        rings[i][0].near()
-    for i, out in enumerate((fa_all, wp_all)):
-        over[i].wait_recv()
-        rings[i][1].own(out.at[other])
-    for i in range(2):
-        rings[i][0].far()
-    for i in range(2):
-        rings[i][1].near()
-    for i in range(2):
-        rings[i][0].cross()
+    total = jnp.sum(got[:, 3, :].astype(F32), 0, keepdims=True)
+    total = jnp.concatenate([total, total], 1) * T
+    plain = tok[3:4, :].astype(F32)
+    weights[...] = jnp.concatenate([plain / total, plain, total] + [jnp.zeros((1, T), F32)] * 5, 0)
+
+    def place_goal(j, carry):
+        from_dev = flat(j // 4, xh, lax.rem(j, 4))
+        goals = jnp.concatenate([got[from_dev, 1:2, :], got[from_dev, 2:3, :]], 1)
+        near, far = goals - me * SHARD, goals - other * SHARD
+        at = jnp.where((far >= 0) & (far < SHARD), far + SHARD, -1)
+        at = jnp.where((near >= 0) & (near < SHARD), near, at)
+        goal[j] = jnp.broadcast_to(at, (8, T))
+        return carry
+
+    lax.fori_loop(0, 16, place_goal, 0)
+    ring.far()
     turn_over(table, rows_t, 0)
+    ring.cross()
     trade.forward()
-    for i in range(2):
-        rings[i][1].far()
-    for i in range(2):
-        rings[i][1].cross()
     reply.wait_recv()
     for k in range(1, NG):
         to = lax.rem(grp + k, NG)
         remote(own_most, most.at[to], most_s.at[k], most_r.at[to], grp=to).wait_recv()
     trade.wait()
     turn_over(table_other, rows_t, SHARD)
-    for pair in rings:
-        for ring in pair:
-            ring.last()
+    ring.last()
+    keep.wait()
+    over.wait_send()
     ask.wait_send()
     reply.wait_send()
     trade.finish()
-    for copy in told + over:
+    for copy in told:
         copy.wait_send()
-    for copy in own:
-        copy.wait()
-    for pair in rings:
-        for ring in pair:
-            ring.finish()
-
-
-def front(msg, table, fa, wp):
+    ring.finish()
+
+
+def front(tok, table, packed):
     return pl.pallas_call(
         front_kernel,
         name="front",
@@ -385,13 +449,18 @@
             jax.ShapeDtypeStruct((NG, 8, 128), jnp.int32),
             jax.ShapeDtypeStruct((D, SHARD), BF),
             jax.ShapeDtypeStruct((2 * SHARD, D), BF),
-            jax.ShapeDtypeStruct((NW, FA_ROWS, D), BF),
-            jax.ShapeDtypeStruct((NW, WP_ROWS, 128), BF),
+            jax.ShapeDtypeStruct((4, 4, 2, PACKED, D), BF),
+            jax.ShapeDtypeStruct((T, NW * CAP), BF),
+            jax.ShapeDtypeStruct((8, T), jnp.int32),
+            jax.ShapeDtypeStruct((NW * CAP, SHARD), BF),
+            jax.ShapeDtypeStruct((16, 8, T), jnp.int32),
+            jax.ShapeDtypeStruct((8, T), F32),
         ),
-        in_specs=[VMEM, VMEM, ANY, ANY],
-        out_specs=(VMEM, VMEM, VMEM, VMEM, VMEM, ANY, ANY),
+        in_specs=[VMEM, VMEM, ANY],
+        out_specs=(VMEM, VMEM, VMEM, VMEM, VMEM, ANY) + (VMEM,) * 5,
         scratch_shapes=[
-            pltpu.VMEM((8 * CAP, SHARD), BF),
+            pltpu.VMEM((8, 8, 128), jnp.int32),
+            pltpu.VMEM((128, 128), F32),
             pltpu.VMEM((NW * CAP, D), BF),
             pltpu.VMEM((8, 128), jnp.int32),
             pltpu.VMEM((2, D // 2, SHARD), BF),
@@ -403,17 +472,190 @@
             DMA((NG,)),
             DMA((4,)),
             DMA((4,)),
-            DMA((2 * RING_SENDS,)),
-            DMA((NW, 4)),
-            DMA((2 * RING_SENDS,)),
-            DMA((NW, 4)),
+            DMA((RING_SENDS + 4,)),
+            DMA((4, 4, 5)),
             DMA((2,)),
-            DMA((2,)),
-            DMA((2,)),
+            DMA((1,)),
         ],
         compiler_params=params(1, 48),
         cost_estimate=pl.CostEstimate(flops=2 * 10**9, bytes_accessed=3 * 10**7, transcendentals=0),
-    )(msg, table, fa, wp)
+    )(tok, table, packed)
+
+
+ORDER = tuple((i // 8) * 8 + (i % 2) * 4 + (i // 2) % 4 for i in range(NW))
+
+
+def spread_rows(used, stride, at, repeat=1):
+    picks = np.zeros((NW * stride, NW * used), np.float32)
+    for i, w in enumerate(ORDER):
+        for j in range(repeat):
+            for r in range(used):
+                picks[i * stride + at + j * used + r, w * used + r] = 1.0
+    return picks
+
+
+def rope():
+    half = HD // 2
+    freqs = np.float32(rope_base) ** (-(np.arange(half, dtype=np.float32) * np.float32(2.0)) / np.float32(HD))
+    angles = freqs.astype(np.float32)[:, None] * np.arange(T, dtype=np.float32)[None, :]
+    return np.concatenate([np.cos(angles), np.sin(angles)], 0).astype(np.float32)
+
+
+def turned(values):
+    return values.T
+
+
+def gain_columns(gains):
+    return jnp.concatenate([gains[...], jnp.zeros((120, D), F32)], 0).T
+
+
+def rms(values, gain):
+    scale = lax.rsqrt(jnp.mean(values * values, 0, keepdims=True) + norm_eps)
+    return values * scale * gain
+
+
+def rms_back(values, gain, grad):
+    scale = lax.rsqrt(jnp.mean(values * values, 0, keepdims=True) + norm_eps)
+    pulled = grad * gain
+    middle = jnp.mean(values * pulled, 0, keepdims=True)
+    back = scale * pulled - values * (scale * scale * scale) * middle
+    return back, jnp.sum(grad * values * scale, 1, keepdims=True)
+
+
+def mask_of(tok):
+    row = tok[2:3, :]
+    column = jnp.broadcast_to(row.astype(F32), (128, T)).T[:, 0:1].astype(jnp.int32)
+    down = lax.broadcasted_iota(jnp.int32, (T, T), 0)
+    across = lax.broadcasted_iota(jnp.int32, (T, T), 1)
+    return (down <= across) & (row == column)
+
+
+def mm(a, b):
+    return jnp.dot(a, b, preferred_element_type=F32)
+
+
+def mm_nt(a, b):
+    return lax.dot_general(a, b, (((1,), (1,)), ((), ())), preferred_element_type=F32)
+
+
+def mm_tn(a, b):
+    return lax.dot_general(a, b, (((0,), (0,)), ((), ())), preferred_element_type=F32)
+
+
+def rotated(x, rot):
+    cosine, sine = rot[0:32, :], rot[32:64, :]
+    one, two = x[0:32, :], x[32:64, :]
+    return jnp.concatenate([one * cosine - two * sine, two * cosine + one * sine], 0)
+
+
+def unrotated(x, rot):
+    cosine, sine = rot[0:32, :], rot[32:64, :]
+    one, two = x[0:32, :], x[32:64, :]
+    return jnp.concatenate([one * cosine + two * sine, two * cosine - one * sine], 0)
+
+
+def load_trunk(packed, ffn, down, attn, sem):
+    loads = [
+        pltpu.make_async_copy(packed.at[:, :, :, ATTN_AT:PACKED], attn, sem.at[0]),
+        pltpu.make_async_copy(packed.at[:, :, :, FFN_AT:DOWN_AT], ffn, sem.at[1]),
+        pltpu.make_async_copy(packed.at[:, :, :, DOWN_AT:ATTN_AT, 0:512], down, sem.at[2]),
+    ]
+    for load in loads:
+        load.start()
+    return loads
+
+
+TRUNK_SCRATCH = [
+    pltpu.VMEM((4, 4, 2, 96, D), BF),
+    pltpu.VMEM((4, 4, 2, 64, 512), BF),
+    pltpu.VMEM((4, 4, 2, 48, D), BF),
+    DMA((3,)),
+]
+
+
+def forward_kernel(
+    hidden, packed, gains, rot, tok,
+    final, h0, n1, q, k, v, lse, att, h1, n2, gate_up, inner, h2,
+    ffn, down, attn, sem, mixed,
+):
+    loads = load_trunk(packed, ffn, down, attn, sem)
+    columns = gain_columns(gains)
+    allowed = mask_of(tok)
+    start = turned(hidden[...])
+    h0[...] = start
+    normed = rms(start, columns[:, 0:1]).astype(BF)
+    n1[...] = normed
+    loads[0].wait()
+    rows48 = attn[...].reshape(NW * 48, D)
+    product = mm(rows48, normed)
+    for i, w in enumerate(ORDER):
+        mixed[w * 30 : w * 30 + 30, :] = product[i * 48 : i * 48 + 30, :]
+    for kv in range(KVH):
+        k[kv * HD : (kv + 1) * HD, :] = rotated(
+            mixed[D + kv * HD : D + (kv + 1) * HD, :], rot[...]
+        ).astype(BF)
+        at = D + (KVH + kv) * HD
+        v[kv * HD : (kv + 1) * HD, :] = mixed[at : at + HD, :].astype(BF)
+    logs = []
+    for h in range(H):
+        kv = h // (H // KVH)
+        query = rotated(mixed[h * HD : (h + 1) * HD, :], rot[...]).astype(BF)
+        q[h * HD : (h + 1) * HD, :] = query
+        scores = mm_tn(k[kv * HD : (kv + 1) * HD, :], query) * HD ** (-0.5)
+        scores = jnp.where(allowed, scores, masked_score)
+        top = jnp.max(scores, 0, keepdims=True)
+        power = jnp.exp(scores - top)
+        total = jnp.sum(power, 0, keepdims=True)
+        probs = (power / total).astype(BF)
+        att[h * HD : (h + 1) * HD, :] = mm(v[kv * HD : (kv + 1) * HD, :], probs).astype(BF)
+        logs.append(top + jnp.log(total))
+    lse[...] = jnp.concatenate(logs + [jnp.zeros((16 - H, T), F32)], 0)
+    product = mm(rows48, att[...])
+    for i, w in enumerate(ORDER):
+        mixed[w * 18 : w * 18 + 18, :] = product[i * 48 + 30 : i * 48 + 48, :]
+    middle = start + mixed[0:D, :]
+    h1[...] = middle
+    normed = rms(middle, columns[:, 1:2]).astype(BF)
+    n2[...] = normed
+    loads[1].wait()
+    gate_up[...] = mm(ffn[...].reshape(NW * 96, D), normed)
+    for i in range(NW // 2):
+        gate = gate_up[i * 96 : (i + 1) * 96, :]
+        up = gate_up[FF + i * 96 : FF + (i + 1) * 96, :]
+        w = ORDER[i]
+        inner[w * 96 : (w + 1) * 96, :] = (gate / (1.0 + jnp.exp(-gate)) * up).astype(BF)
+    loads[2].wait()
+    rows64 = down[...].reshape(NW * 64, 512)
+    for j in range(3):
+        product = mm(rows64, inner[j * 512 : (j + 1) * 512, :])
+        for i, w in enumerate(ORDER):
+            piece = product[i * 64 + j * 18 : i * 64 + j * 18 + 18, :]
+            if j:
+                mixed[w * 18 : w * 18 + 18, :] += piece
+            else:
+                mixed[w * 18 : w * 18 + 18, :] = piece
+    last = middle + mixed[0:D, :]
+    h2[...] = last
+    final[...] = rms(last, columns[:, 2:3]).astype(BF)
+
+
+def forward(hidden, packed, gains, rot, tok):
+    def out(rows, kind):
+        return jax.ShapeDtypeStruct((rows, T), kind)
+
+    return pl.pallas_call(
+        forward_kernel,
+        name="forward",
+        out_shape=(
+            out(D, BF), out(D, F32), out(D, BF), out(D, BF), out(KVH * HD, BF), out(KVH * HD, BF), out(16, F32),
+            out(D, BF), out(D, F32), out(D, BF), out(2 * FF, F32), out(FF, BF), out(D, F32),
+        ),
+        in_specs=[VMEM, ANY, VMEM, VMEM, VMEM],
+        out_specs=(VMEM,) * 13,
+        scratch_shapes=TRUNK_SCRATCH + [pltpu.VMEM((QKV, T), F32)],
+        compiler_params=pltpu.CompilerParams(vmem_limit_bytes=48 * MIB),
+        cost_estimate=pl.CostEstimate(flops=4 * 10**9, bytes_accessed=2 * 10**7, transcendentals=10**6),
+    )(hidden, packed, gains, rot, tok)
 
 
 def more_rows_kernel(msg, table, got, emb, hot, rows, msg_s, msg_r, emb_s, emb_r):
@@ -526,11 +768,10 @@
     ring = Ring(
         lambda Y, Z, first, count: fall.at[pl.ds(first, count), cols(Y * 4 + Z)],
         lambda Y, Z, index: g_r.at[Y * 4 + Z, index],
-        QUART,
+        tuple(QUART * k for k in range(5)),
         g_s,
-        0,
-    )
-    ring.own(final)
+    )
+    ring.own(final, fall.at[:, cols(mine)], 0)
     fall[:, cols(mine)] = final[...]
 
     def logits(j):
@@ -847,12 +1088,14 @@
 
 
 class Reduce:
-    def __init__(self, parts, base, quarter, along_z, refs):
+    def __init__(self, parts, base, sizes, along_z, refs):
         (
-            self.first, self.part1, self.whole1, self.second, self.part2, self.whole2,
+            self.first, part_a, part_b, self.whole1, self.second, next_a, next_b, self.whole2,
             self.third, self.stop, self.third_in, self.s, self.r,
         ) = refs
-        self.parts, self.base, self.q, self.along_z = parts, base, quarter, along_z
+        self.part1, self.part2 = (part_a, part_b), (next_a, next_b)
+        self.parts, self.base, self.sizes, self.along_z = parts, base, sizes, along_z
+        self.rows = (pl.ds(0, sizes[0]), pl.ds(sizes[0], sizes[1]), pl.ds(0, sum(sizes)))
         self.me, self.y, self.xh, self.z = place()
         self.sent = []
 
@@ -864,17 +1107,14 @@
     def wait(self, dst, at):
         remote(dst, dst, self.s.at[at], self.r.at[at], wide=self.me).wait_recv()
 
-    def item1(self, step, first, count):
-        rows = pl.ds(self.base + first * self.q, count * self.q)
+    def item1(self, step, which):
+        rows = pl.ds(self.base + self.rows[which].start, self.rows[which].size)
         if self.along_z:
-            return (slice(None), slice(None), turn4(self.z, step), rows)
+            return (slice(None), turn4(self.z, step), slice(None), rows)
         return (turn4(self.y, step), slice(None), slice(None), rows)
 
-    def item2(self, step, first, count):
-        rows = pl.ds(first * self.q, count * self.q)
-        if self.along_z:
-            return (turn4(self.y, step), slice(None), rows)
-        return (slice(None), turn4(self.z, step), rows)
+    def item2(self, step, which):
+        return (turn4(self.y if self.along_z else self.z, step), slice(None), self.rows[which])
 
     def to(self, stage, step):
         if self.along_z == (stage == 1):
@@ -883,19 +1123,17 @@
 
     def split(self, stage, ref, item, part, base):
         for index, step in enumerate((1, 3)):
-            self.send(ref.at[item(2, index, 1)], part.at[index], base + index, wide=self.to(stage, step))
+            self.send(ref.at[item(2, index)], part[index], base + index, wide=self.to(stage, step))
 
     def join(self, stage, ref, item, part, whole, base):
         for index, step in enumerate((1, 3)):
-            self.wait(part.at[index], base + index)
-            at = item(step, index, 1)
-            ref[at] = (ref[at].astype(F32) + part[index].astype(F32)).astype(BF)
-            self.send(
-                ref.at[item(step, 0, 2)], whole.at[index], base + 2 + index, wide=self.to(stage, step)
-            )
+            self.wait(part[index], base + index)
+            at = item(step, index)
+            ref[at] = (ref[at].astype(F32) + part[index][...].astype(F32)).astype(BF)
+            self.send(ref.at[item(step, 2)], whole.at[index], base + 2 + index, wide=self.to(stage, step))
 
     def add(self, ref, item, whole, base):
-        acc = ref[item(0, 0, 2)].astype(F32)
+        acc = ref[item(0, 2)].astype(F32)
         for index in range(2):
             self.wait(whole.at[index], base + 2 + index)
             acc = acc + whole[index].astype(F32)
@@ -932,36 +1170,41 @@
             copy.wait_send()
 
 
-def reduce_scratch(half, lanes):
+STREAMS = ((0, (48, 32), True), (80, (48, 32), False), (160, (16, 16), True), (192, (16, 16), False))
+
+
+def reduce_scratch():
     shapes = []
-    for group in ((4, 2), (2, 4)):
-        quarter = half // 2
+    for _, sizes, _ in STREAMS:
+        half = sum(sizes)
         shapes += [
-            pltpu.VMEM(group + (half, lanes), BF),
-            pltpu.VMEM((2,) + group + (quarter, lanes), BF),
-            pltpu.VMEM((2,) + group + (half, lanes), BF),
-            pltpu.VMEM((2, half, lanes), F32),
-            pltpu.VMEM((2, 2, quarter, lanes), BF),
-            pltpu.VMEM((2, 2, half, lanes), BF),
-            pltpu.VMEM((half, lanes), BF),
-            pltpu.VMEM((half, lanes), BF),
-            pltpu.VMEM((half, lanes), BF),
+            pltpu.VMEM((4, 2, half, D), BF),
+            pltpu.VMEM((4, 2, sizes[0], D), BF),
+            pltpu.VMEM((4, 2, sizes[1], D), BF),
+            pltpu.VMEM((2, 4, 2, half, D), BF),
+            pltpu.VMEM((2, half, D), F32),
+            pltpu.VMEM((2, sizes[0], D), BF),
+            pltpu.VMEM((2, sizes[1], D), BF),
+            pltpu.VMEM((2, 2, half, D), BF),
+            pltpu.VMEM((half, D), BF),
+            pltpu.VMEM((half, D), BF),
+            pltpu.VMEM((half, D), BF),
             DMA((10,)),
             DMA((10,)),
         ]
     return shapes
 
 
-def back_kernel(fa_in, wp_in, rows, head_other, extra, fa_sum, wp_sum, rows_in, head_in, extra_sum, *scratch):
+def back_kernel(
+    grad_final, h0, n1, q, k, v, lse, att, h1, n2, gate_up, inner, h2,
+    packed, gains, rot, tok, slot_row, loss, head_other, lay_attn, lay_out, lay_down,
+    summed, rows_in, head_in, extra_sum, grad_embedded,
+    ffn, down, attn, sem, parts, rows, grad_up, grad_mixed, spread, extra, extra_in, stops,
+    row_s, row_r, extra_s, extra_r, swap_s, swap_r, *reducers,
+):
     me, y, xh, z = place()
+    loads = load_trunk(packed, ffn, down, attn, sem)
     greet_wide(me, sides=True)
-    fa, wp, extra_in, stops, row_s, row_r, extra_s, extra_r, swap_s, swap_r, local = scratch[44:]
-    loads = [
-        pltpu.make_async_copy(fa_in, fa, local.at[0]),
-        pltpu.make_async_copy(wp_in, wp, local.at[1]),
-    ]
-    for load in loads:
-        load.start()
     halves = (pl.ds(0, D // 2), pl.ds(D // 2, D // 2))
     trade = Relay(
         [head_other.at[half] for half in halves],
@@ -970,41 +1213,132 @@
         swap_s,
         swap_r,
     )
-    for load in loads:
-        load.wait()
-    streams = []
-    for parts, rows_of, at in ((fa, FA_ROWS, 0), (wp, WP_ROWS, 22)):
-        for half in range(2):
-            refs = scratch[at + 11 * half : at + 11 * half + 11]
-            streams.append(Reduce(parts, half * rows_of // 2, rows_of // 4, half == 0, refs))
-    for stream in streams:
+    trade.start()
+    streams = [
+        Reduce(parts, base, sizes, along, reducers[13 * i : 13 * i + 13])
+        for i, (base, sizes, along) in enumerate(STREAMS)
+    ]
+    early, late = streams[:2], streams[2:]
+    columns = gain_columns(gains)
+
+    grad_h2, gain3 = rms_back(h2[...], columns[:, 2:3], grad_final[...])
+    spread[...] = mm(lay_down[...], grad_h2.astype(BF)).astype(BF)
+    chunk = lax.broadcasted_iota(jnp.int32, (NW * 64, T), 0) & 63
+    zero = jnp.zeros((NW * 64, T), BF)
+    wide = jnp.concatenate(
+        [
+            jnp.where((chunk >= 18 * j) & (chunk < 18 * (j + 1)), spread[...].astype(F32), 0.0).astype(BF)
+            for j in range(3)
+        ],
+        1,
+    )
+    inners = jnp.concatenate([inner[j * 512 : (j + 1) * 512, :] for j in range(3)], 1)
+    grad_down = mm_nt(wide, inners).astype(BF).reshape(4, 4, 2, 64, 512)
+    parts[:, :, :, DOWN_AT:ATTN_AT, 0:512] = grad_down
+    parts[:, :, :, DOWN_AT:ATTN_AT, 512:D] = jnp.zeros((4, 4, 2, 64, D - 512), BF)
+    loads[2].wait()
+    grad_inner = mm_tn(down[...].reshape(NW * 64, 512), wide)
+    for i in range(NW // 2):
+        w = ORDER[i]
+        gate = gate_up[i * 96 : (i + 1) * 96, :]
+        up = gate_up[FF + i * 96 : FF + (i + 1) * 96, :]
+        pieces = []
+        for at in range(w * 96, w * 96 + 96, 32):
+            j, r = at // 512, at % 512
+            pieces.append(grad_inner[r : r + 32, j * T : (j + 1) * T])
+        grad = jnp.concatenate(pieces, 0)
+        sigmoid = 1.0 / (1.0 + jnp.exp(-gate))
+        slope = sigmoid * (1.0 + gate * (1.0 - sigmoid))
+        grad_up[i * 96 : (i + 1) * 96, :] = (grad * up * slope).astype(BF)
+        grad_up[FF + i * 96 : FF + (i + 1) * 96, :] = (grad * (gate * sigmoid)).astype(BF)
+    parts[:, :, :, FFN_AT:DOWN_AT, :] = mm_nt(grad_up[...], n2[...]).astype(BF).reshape(4, 4, 2, 96, D)
+    for stream in early:
         stream.one()
-    trade.start()
+    loads[1].wait()
+    grad_normed = turned(mm_tn(grad_up[...], ffn[...].reshape(NW * 96, D)))
+    part, gain2 = rms_back(h1[...], columns[:, 1:2], grad_normed)
+    grad_h1 = grad_h2 + part
+    out_rows = mm(lay_out[...], grad_h1.astype(BF)).astype(BF)
+    loads[0].wait()
+    rows48 = attn[...].reshape(NW * 48, D)
+    grad_att = turned(mm_tn(out_rows, rows48)).astype(BF)
+    for stream in early:
+        stream.two()
+
+    allowed = mask_of(tok)
+    group = H // KVH
+    for kv in range(KVH):
+        keys = k[kv * HD : (kv + 1) * HD, :]
+        values = v[kv * HD : (kv + 1) * HD, :]
+        grad_k, grad_v = jnp.zeros((HD, T), F32), jnp.zeros((HD, T), F32)
+        for h in range(kv * group, (kv + 1) * group):
+            query = q[h * HD : (h + 1) * HD, :]
+            grad_out = grad_att[h * HD : (h + 1) * HD, :]
+            scores = mm_tn(keys, query) * HD ** (-0.5)
+            scores = jnp.where(allowed, scores, masked_score)
+            soft = jnp.exp(scores - lse[h : h + 1, :])
+            grad_probs = mm_tn(values, grad_out)
+            mean = jnp.sum(soft * grad_probs, 0, keepdims=True)
+            grad_scores = (soft * (grad_probs - mean)).astype(BF)
+            grad_q = mm(keys, grad_scores) * HD ** (-0.5)
+            grad_mixed[h * HD : (h + 1) * HD, :] = unrotated(grad_q, rot[...]).astype(BF)
+            grad_k = grad_k + mm_nt(query, grad_scores) * HD ** (-0.5)
+            grad_v = grad_v + mm_nt(grad_out, soft.astype(BF))
+        at = D + kv * HD
+        grad_mixed[at : at + HD, :] = unrotated(grad_k, rot[...]).astype(BF)
+        at = D + (KVH + kv) * HD
+        grad_mixed[at : at + HD, :] = grad_v.astype(BF)
+    for stream in early:
+        stream.three()
+    attn_rows = mm(lay_attn[...], grad_mixed[...]).astype(BF)
+    both = jnp.concatenate([attn_rows, out_rows], 1)
+    seen = jnp.concatenate([n1[...], att[...]], 1)
+    parts[:, :, :, ATTN_AT:PACKED, :] = mm_nt(both, seen).astype(BF).reshape(4, 4, 2, 48, D)
+    parts[:, :, :, PACKED:SUMMED, :] = jnp.zeros((4, 4, 2, SUMMED - PACKED, D), BF)
+    for stream in late:
+        stream.one()
+    grad_normed = turned(mm_tn(attn_rows, rows48))
+    part, gain1 = rms_back(h0[...], columns[:, 0:1], grad_normed)
+    grad_h0 = (grad_h1 + part).astype(BF)
+    grad_embedded[...] = grad_h0
+    slot = lax.broadcasted_iota(jnp.int32, (NW * CAP, T), 0)
+    picks = jnp.where(slot == slot_row[0:1, :], 1.0, 0.0).astype(BF)
+    rows[...] = mm_nt(picks, grad_h0).astype(BF)
     give = Scatter(lambda p: rows.at[slots(p)], lambda p: rows_in.at[slots(p)], row_s, row_r, me)
     give.start()
+    for stream in early:
+        stream.four()
+    trade.forward()
+    lane = lax.broadcasted_iota(jnp.int32, (D, 128), 1)
+    table = jnp.where(lane == 0, gain1, jnp.where(lane == 1, gain2, jnp.where(lane == 2, gain3, 0.0)))
+    lost = jnp.sum(loss[0:1, :], 1, keepdims=True)
+    table = table.T[0:8, :]
+    extra[...] = jnp.where(lax.broadcasted_iota(jnp.int32, (8, D), 0) == 3, lost, table)
     share = Scatter(lambda p: extra, lambda p: extra_in.at[p], extra_s, extra_r, me)
     share.start()
     rows_in[slots(me), :] = rows[slots(me), :]
     extra_in[me] = extra[...]
-    for stream in streams:
+    for stream in late:
         stream.two()
-    trade.forward()
-    for stream in streams:
+    for stream in early:
+        stream.five()
+    for stream in late:
         stream.three()
-    for stream in streams:
+    for stream in late:
         stream.four()
-    for stream in streams:
+    for stream in early:
+        stream.six()
+    for stream in late:
         stream.five()
     share.wait_recv()
     total = extra_in[0]
     for w in range(1, NW):
         total = total + extra_in[w]
     extra_sum[...] = total
+    for stream in late:
+        stream.six()
     for stream in streams:
-        stream.six()
-    for out, pair, half in ((fa_sum, streams[:2], FA_ROWS // 2), (wp_sum, streams[2:], WP_ROWS // 2)):
-        out[0:half, :] = pair[0].total()
-        out[half : 2 * half, :] = pair[1].total()
+        summed[stream.base : stream.base + sum(stream.sizes), :] = stream.total()
     give.wait_recv()
     trade.wait()
     for stream in streams:
@@ -1014,32 +1348,41 @@
     trade.finish()
 
 
-def back(fa, wp, rows, head_other, extra):
+def back(grad_final, kept, packed, gains, rot, tok, slot_row, loss, head_other):
+    lays = [
+        jnp.asarray(spread_rows(30, 48, 0), BF),
+        jnp.asarray(spread_rows(18, 48, 30), BF),
+        jnp.asarray(spread_rows(18, 64, 0, 3), BF),
+    ]
     return pl.pallas_call(
         back_kernel,
         name="back",
         out_shape=(
-            jax.ShapeDtypeStruct((FA_ROWS, D), F32),
-            jax.ShapeDtypeStruct((WP_ROWS, 128), F32),
+            jax.ShapeDtypeStruct((SUMMED, D), F32),
             jax.ShapeDtypeStruct((NW * CAP, D), BF),
             jax.ShapeDtypeStruct((D, SHARD), BF),
-            jax.ShapeDtypeStruct((8, 640), F32),
+            jax.ShapeDtypeStruct((8, D), F32),
+            jax.ShapeDtypeStruct((D, T), BF),
         ),
-        in_specs=[ANY, ANY, VMEM, ANY, VMEM],
-        out_specs=(VMEM, VMEM, VMEM, ANY, VMEM),
-        scratch_shapes=reduce_scratch(FA_ROWS // 2, D)
-        + reduce_scratch(WP_ROWS // 2, 128)
+        in_specs=[VMEM] * 13 + [ANY] + [VMEM] * 5 + [ANY] + [VMEM] * 3,
+        out_specs=(VMEM, VMEM, ANY, VMEM, VMEM),
+        scratch_shapes=TRUNK_SCRATCH
         + [
-            pltpu.VMEM((4, 2, 4, FA_ROWS, D), BF),
-            pltpu.VMEM((4, 2, 4, WP_ROWS, 128), BF),
-            pltpu.VMEM((NW, 8, 640), F32),
+            pltpu.VMEM((4, 4, 2, SUMMED, D), BF),
+            pltpu.VMEM((NW * CAP, D), BF),
+            pltpu.VMEM((2 * FF, T), BF),
+            pltpu.VMEM((QKV, T), BF),
+            pltpu.VMEM((NW * 64, T), BF),
+            pltpu.VMEM((8, D), F32),
+            pltpu.VMEM((NW, 8, D), F32),
             pltpu.VMEM((2, D // 2, SHARD), BF),
         ]
         + [DMA((NW,))] * 4
-        + [DMA((4,)), DMA((4,)), DMA((2,))],
-        compiler_params=params(5, 48),
-        cost_estimate=pl.CostEstimate(flops=10**8, bytes_accessed=3 * 10**7, transcendentals=0),
-    )(fa, wp, rows, head_other, extra)
+        + [DMA((4,)), DMA((4,))]
+        + reduce_scratch(),
+        compiler_params=params(5, 60),
+        cost_estimate=pl.CostEstimate(flops=10**10, bytes_accessed=3 * 10**7, transcendentals=10**6),
+    )(grad_final, *kept, packed, gains, rot, tok, slot_row, loss, head_other, *lays)
 
 
 def norm_kernel(value, out, landing, s, r):
@@ -1153,113 +1496,6 @@
     return jnp.einsum(spec, a, b, preferred_element_type=F32)
 
 
-def rms_normed(values, gain):
-    scale = lax.rsqrt(jnp.mean(values * values, 0, keepdims=True) + norm_eps)
-    return values * scale * gain[:, None]
-
-
-def norm_back(values, gain, grad):
-    scale = lax.rsqrt(jnp.mean(values * values, 0, keepdims=True) + norm_eps)
-    pulled = grad * gain[:, None]
-    middle = jnp.mean(values * pulled, 0, keepdims=True)
-    return (
-        scale * pulled - values * (scale * scale * scale) * middle,
-        jnp.sum(grad * values * scale, 1),
-    )
-
-
-def rotary():
-    half = HD // 2
-    freqs = rope_base ** (-(jnp.arange(half, dtype=F32) * 2.0) / HD)
-    angles = freqs[:, None] * jnp.arange(T, dtype=F32)[None, :]
-    return (jnp.concatenate([jnp.cos(angles)] * 2, 0), jnp.concatenate([jnp.sin(angles)] * 2, 0))
-
-
-def rotate(values, cosine, sine):
-    half = HD // 2
-    turned = jnp.concatenate([-values[..., half:, :], values[..., :half, :]], -2)
-    return values * cosine + turned * sine
-
-
-def unrotate(grad, cosine, sine):
-    half = HD // 2
-    part = grad * sine
-    return grad * cosine + jnp.concatenate([part[..., half:, :], -part[..., :half, :]], -2)
-
-
-def layer_forward(hidden0, gains, wa, wf, wp, allowed, cosine, sine):
-    kv = KVH * HD
-    group = H // KVH
-    normed1 = rms_normed(hidden0, gains[0]).astype(BF)
-    mixed = dot("ed,dt->et", wa, normed1)
-    queries = rotate(mixed[:D].reshape(KVH, group, HD, T), cosine, sine).astype(BF)
-    keys = rotate(mixed[D : D + kv].reshape(KVH, HD, T), cosine, sine).astype(BF)
-    values = mixed[D + kv :].reshape(KVH, HD, T).astype(BF)
-    scores = dot("kct,kgcq->kgtq", keys, queries) * HD ** (-0.5)
-    scores = jnp.where(allowed, scores, masked_score)
-    expo = jnp.exp(scores - jnp.max(scores, -2, keepdims=True))
-    soft = expo / jnp.sum(expo, -2, keepdims=True)
-    probs = soft.astype(BF)
-    attended = dot("kct,kgtq->kgcq", values, probs).reshape(D, T).astype(BF)
-    hidden1 = hidden0 + dot("de,et->dt", wp[:, :D], attended)
-    normed2 = rms_normed(hidden1, gains[1]).astype(BF)
-    gate_up = dot("ed,dt->et", wf, normed2)
-    inner = (jax.nn.silu(gate_up[:FF]) * gate_up[FF:]).astype(BF)
-    hidden2 = hidden1 + dot("df,ft->dt", wp[:, D:], inner)
-    final = rms_normed(hidden2, gains[2]).astype(BF)
-    kept = (
-        hidden0, normed1, queries, keys, values, soft, probs,
-        attended, hidden1, normed2, gate_up, inner, hidden2,
-    )
-    return final, kept
-
-
-def layer_backward(grad_final, kept, gains, wa, wf, wp, cosine, sine):
-    (
-        hidden0, normed1, queries, keys, values, soft, probs,
-        attended, hidden1, normed2, gate_up, inner, hidden2,
-    ) = kept
-    group = H // KVH
-    grad_h2, grad_g3 = norm_back(hidden2, gains[2], grad_final)
-    branch = grad_h2.astype(BF)
-    grad_down = dot("dt,ft->df", branch, inner)
-    grad_inner = dot("df,dt->ft", wp[:, D:], branch)
-    gate, up = gate_up[:FF], gate_up[FF:]
-    sigmoid = jax.nn.sigmoid(gate)
-    slope = sigmoid * (1.0 + gate * (1.0 - sigmoid))
-    grad_gate_up = jnp.concatenate(
-        [grad_inner * up * slope, grad_inner * (gate * sigmoid)], 0
-    ).astype(BF)
-    grad_ffn = dot("et,dt->ed", grad_gate_up, normed2)
-    grad_normed2 = dot("ed,et->dt", wf, grad_gate_up)
-    grad_part, grad_g2 = norm_back(hidden1, gains[1], grad_normed2)
-    grad_h1 = grad_h2 + grad_part
-    branch = grad_h1.astype(BF)
-    grad_wo = dot("dt,et->de", branch, attended)
-    grad_att = dot("de,dt->et", wp[:, :D], branch).astype(BF).reshape(KVH, group, HD, T)
-    grad_probs = dot("kct,kgcq->kgtq", values, grad_att)
-    grad_scores = (
-        soft * (grad_probs - jnp.sum(soft * grad_probs, -2, keepdims=True))
-    ).astype(BF)
-    grad_q = dot("kct,kgtq->kgcq", keys, grad_scores) * HD ** (-0.5)
-    grad_k = dot("kgcq,kgtq->kct", queries, grad_scores) * HD ** (-0.5)
-    grad_v = dot("kgcq,kgtq->kct", grad_att, probs)
-    grad_q = unrotate(grad_q, cosine, sine).reshape(D, T)
-    grad_k = unrotate(grad_k, cosine, sine).reshape(KVH * HD, T)
-    grad_mixed = jnp.concatenate([grad_q, grad_k, grad_v.reshape(KVH * HD, T)], 0).astype(BF)
-    grad_attn = dot("et,dt->ed", grad_mixed, normed1)
-    grad_normed1 = dot("ed,et->dt", wa, grad_mixed)
-    grad_part, grad_g1 = norm_back(hidden0, gains[0], grad_normed1)
-    grad_proj = jnp.concatenate([grad_wo, grad_down], 1)
-    return (
-        (grad_h1 + grad_part).astype(BF),
-        grad_attn,
-        grad_ffn,
-        grad_proj,
-        jnp.stack([grad_g1, grad_g2, grad_g3]),
-    )
-
-
 def adam_update(weight, grad, first, second, rate, decay):
     first = beta_one * first + (1.0 - beta_one) * grad
     second = beta_two * second + (1.0 - beta_two) * grad * grad
@@ -1309,127 +1545,88 @@
     norm_gains_anchor,
     norm_gains_momentum,
 ):
-    me = lax.axis_index("wide")
-    xh = lax.rem(me // 4, 2)
-    other = flat(me // 8, 1 - xh, lax.rem(me, 4))
     ids = token_ids[0]
     gains = norm_gains_master[0]
     table = embed_table_master[0].T.astype(BF)
     weight = jnp.sum(row_counts[0, 0] * jnp.arange(1, 4))
-
-    owner = ids // SHARD
-    local = ids - owner * SHARD
-    place_of = jnp.arange(T)
-    same = ids[:, None] == ids[None, :]
-    first_seen = ~jnp.any(same & (place_of[None, :] < place_of[:, None]), 1)
-    rank = jnp.sum(
-        (first_seen[None, :] & (owner[None, :] == owner[:, None]) & (ids[None, :] < ids[:, None])),
-        1,
-        dtype=jnp.int32,
-    )
-    most = jnp.max(rank) + 1
-    slot_place = jnp.arange(NW * CAP)
-
-    def slot_picks(turn):
-        at = rank - turn * CAP
-        slot = jnp.where((at >= 0) & (at < CAP), owner * CAP + at, -1)
-        return slot_place[:, None] == slot[None, :]
-
-    def message(picks):
-        asked = jnp.max(jnp.where(picks, local[None, :], -1), 1).reshape(NW, 1, CAP)
+    proj = proj_out_master[0].T
+    packed = jnp.concatenate(
+        [
+            ffn_in_master[0].T,
+            jnp.pad(proj[:, D:].reshape(18, 3, 512).transpose(1, 0, 2).reshape(54, 512), ((0, 10), (0, D - 512))),
+            attn_in_master[0].T,
+            proj[:, :D],
+        ],
+        0,
+    ).astype(BF)
+    tok = jnp.concatenate(
+        [
+            token_ids, targets, segment_ids, jnp.broadcast_to(weight, (1, T)), jnp.zeros((4, T), jnp.int32),
+        ],
+        0,
+    )
+    got, rows, most_all, table_other, rows_t, packed_all, picks, slot_row, hot, goals, weights = front(
+        tok, table, packed
+    )
+    turns = (jnp.max(most_all) + CAP - 1) // CAP
+
+    def asked_in(turn):
+        ids_now = jnp.where(turn > 0, ids, 0)
+        owner = ids_now // SHARD
+        same = ids_now[:, None] == ids_now[None, :]
+        before = jnp.arange(T)[None, :] < jnp.arange(T)[:, None]
+        first_seen = ~jnp.any(same & before, 1)
+        smaller = (owner[None, :] == owner[:, None]) & (ids_now[None, :] < ids_now[:, None])
+        rank = jnp.sum(first_seen[None, :] & smaller, 1, dtype=jnp.int32) - turn * CAP
+        slot = jnp.where((rank >= 0) & (rank < CAP), owner * CAP + rank, -1)
+        chosen = jnp.arange(NW * CAP)[:, None] == slot[None, :]
+        asked = jnp.max(jnp.where(chosen, (ids_now - owner * SHARD)[None, :], -1), 1).reshape(NW, 1, CAP)
         asked = jnp.pad(asked, ((0, 0), (0, 0), (0, 128 - CAP)), constant_values=-1)
-        rest = jnp.concatenate(
-            [
-                targets[0].reshape(2, 128),
-                jnp.broadcast_to(weight, (1, 128)),
-                jnp.broadcast_to(most, (1, 128)),
-                jnp.zeros((3, 128), jnp.int32),
-            ],
-            0,
-        )
-        return jnp.concatenate([asked, jnp.broadcast_to(rest[None], (NW, 7, 128))], 1)
-
-    picks = slot_picks(0)
-    fa = pack_fa(attn_in_master[0].T, ffn_in_master[0].T).astype(BF)
-    wp = pack_wp(proj_out_master[0].T).astype(BF)
-    got, rows, most_all, table_other, rows_t, fa_all, wp_all = front(message(picks), table, fa, wp)
-    turns = (jnp.max(most_all) + CAP - 1) // CAP
-
-    def to_tokens(rows, picks):
-        return dot("sd,st->dt", rows, picks.astype(BF))
+        return jnp.pad(asked, ((0, 0), (0, 7), (0, 0))), chosen.astype(BF)
 
     def more_tokens(carry):
         turn, hidden = carry
-        picks = slot_picks(turn)
-        return turn + 1, hidden + to_tokens(more_rows(message(picks), table), picks)
+        message, chosen = asked_in(turn)
+        return turn + 1, hidden + dot("sd,st->td", more_rows(message, table), chosen)
 
     hidden0 = lax.while_loop(
-        lambda carry: carry[0] < turns, more_tokens, (jnp.int32(1), to_tokens(rows, picks))
+        lambda carry: carry[0] < turns, more_tokens, (jnp.int32(1), dot("ts,sd->td", picks, rows))
     )[1]
 
-    wf_full = fa_all[:, :96].reshape(2 * FF, D)
-    wa_full = fa_all[:, 96:126].reshape(QKV, D)
-    wp_full = wp_all[:, :297].reshape(D, D + FF)
-    segments = segment_ids[0]
-    allowed = (place_of[:, None] <= place_of[None, :]) & (segments[:, None] == segments[None, :])
-    cosine, sine = rotary()
-    final, kept = layer_forward(hidden0, gains, wa_full, wf_full, wp_full, allowed, cosine, sine)
-
-    total = jnp.sum(got[:, 3, 0]).astype(F32) * T
-    goals = got[:, 1:3, :].reshape(4, 2, 4, T)
-    goals = jnp.where(xh == 0, goals[:, 0], goals[:, 1]).reshape(16, 1, T)
-    near, far = goals - me * SHARD, goals - other * SHARD
-    goals = jnp.where(
-        (near >= 0) & (near < SHARD), near, jnp.where((far >= 0) & (far < SHARD), far + SHARD, -1)
-    )
-    goals = jnp.broadcast_to(goals, (16, 8, T))
-    plain = weight.astype(F32)
-    weights = jnp.concatenate(
-        [jnp.full((1, T), plain / total, F32), jnp.full((1, T), plain, F32), jnp.zeros((6, T), F32)], 0
-    )
+    gains8 = jnp.pad(gains, ((0, 5), (0, 0)))
+    rot = jnp.asarray(rope())
+    final, *kept = forward(hidden0, packed_all, gains8, rot, tok)
+    total = weights[2, 0]
     grad_final, head_own, head_other, loss = head(final, rows_t, table, table_other, goals, weights)
-
-    grad_embedded, grad_attn, grad_ffn, grad_proj, grad_gains = layer_backward(
-        grad_final, kept, gains, wa_full, wf_full, wp_full, cosine, sine
-    )
-    fa_parts = pack_fa(
-        grad_attn.astype(BF).reshape(NW, 30, D), grad_ffn.astype(BF).reshape(NW, 96, D)
-    ).reshape(4, 2, 4, FA_ROWS, D)
-    wp_parts = pack_wp(grad_proj.astype(BF).reshape(NW, 18, D + FF)).reshape(4, 2, 4, WP_ROWS, 128)
-    extra = jnp.zeros((8, 640), F32).at[:3, :D].set(grad_gains).at[3, 0].set(jnp.sum(loss[0]))
-
-    def to_slots(picks):
-        return dot("st,dt->sd", picks.astype(BF), grad_embedded).astype(BF)
-
-    fa_sum, wp_sum, rows_in, head_in, extra_sum = back(
-        fa_parts, wp_parts, to_slots(picks), head_other, extra
-    )
-
-    def to_table(got, rows):
-        asked = got[:, 0, :CAP].reshape(NW * CAP)
-        hot = (asked[:, None] == jnp.arange(SHARD)[None, :]).astype(BF)
-        return dot("sd,sv->dv", rows, hot)
+    summed, rows_in, head_in, extra_sum, grad_embedded = back(
+        grad_final, kept, packed_all, gains8, rot, tok, slot_row, loss, head_other
+    )
 
     def more_table(carry):
         turn, grad = carry
-        picks = slot_picks(turn)
-        return turn + 1, grad + to_table(*more_grads(message(picks), to_slots(picks)))
+        message, chosen = asked_in(turn)
+        mine = dot("st,dt->sd", chosen, grad_embedded).astype(BF)
+        got_now, rows_now = more_grads(message, mine)
+        asked = got_now[:, 0, :CAP].reshape(NW * CAP)
+        hot_now = (asked[:, None] == jnp.arange(SHARD)[None, :]).astype(BF)
+        return turn + 1, grad + dot("sd,sv->dv", rows_now, hot_now)
 
     table_grad = lax.while_loop(
         lambda carry: carry[0] < turns,
         more_table,
-        (jnp.int32(1), head_own + head_in.astype(F32) + to_table(got, rows_in)),
+        (jnp.int32(1), head_own + head_in.astype(F32) + dot("sd,sv->dv", rows_in, hot)),
     )[1]
 
     sum_gains = extra_sum[:3, :D]
     loss_total = extra_sum[3, 0]
-    squares = jnp.sum(table_grad * table_grad) + jnp.sum(fa_sum * fa_sum) + jnp.sum(wp_sum * wp_sum)
+    squares = jnp.sum(table_grad * table_grad) + jnp.sum(summed * summed)
     squares = norm_sum(jnp.broadcast_to(squares, (8, 128)))[0, 0]
     norm = jnp.sqrt(squares + jnp.sum(sum_gains * sum_gains))
     factor = jnp.minimum(1.0, clip_norm / norm)
 
-    sum_ffn, sum_attn = fa_sum[:96], fa_sum[96:126]
-    sum_proj = wp_sum[:297].reshape(18, D + FF)
+    sum_ffn, sum_attn = summed[FFN_AT:DOWN_AT], summed[ATTN_AT : ATTN_AT + 30]
+    sum_down = summed[DOWN_AT : DOWN_AT + 54, :512].reshape(3, 18, 512).transpose(1, 0, 2).reshape(18, FF)
+    sum_proj = jnp.concatenate([summed[ATTN_AT + 30 : PACKED], sum_down], 1)
     kinds = (
         (
             embed_table_master[0].T,

time: 476 us -> 438 us (0.920)
  Pallas kernels: 306 us -> 366 us
  local copies, waits for them, and re-layouts: 60.6 us -> 21.5 us
  other arithmetic: 61.7 us -> 27.9 us
  matrix products: 28.6 us -> 7.47 us
    pallas_call x1, Pallas kernels: 77.1 us -> 96.5 us  [back(): pl.pallas_call(back_kernel, name='back', out_shape=(jax.ShapeDtypeStruct(...]
    dot_general x20 -> x2, matrix products: 26.3 us -> 7.47 us  [dot(): return jnp.einsum(spec, a, b, preferred_element_type=F32)]
    pallas_call x1, Pallas kernels: 75.1 us -> 89.4 us  [front(): pl.pallas_call(front_kernel, name='front', out_shape=(jax.ShapeDtypeStruc...]
    pallas_call x0 -> x1, Pallas kernels: none -> 12.1 us  [forward(): pl.pallas_call(forward_kernel, name='forward', out_shape=(out(D, BF), out...]
    convert_element_type x4 -> x0, local copies, waits for them, and re-layouts: 12 us -> none  [the longest x1 6.33 us: on_device(): grad_ffn.astype(BF).reshape(NW, 96, D)]
    slice x9 -> x5, local copies, waits for them, and re-layouts: 10.7 us -> 1.3 us  [the longest x1 1.19 us: on_device(): total = weights[2, 0]]
    transpose x5 -> x4, other arithmetic: 16.5 us -> 7.71 us  [on_device(): values = [value.T for value in values]]
    reshape x5 -> x4, local copies, waits for them, and re-layouts: 8.14 us -> 0.16 us  [the longest x2 0.09 us: on_device(): summed[DOWN_AT:DOWN_AT + 54, :512].reshape(3, 18, 512).transpose(1, 0, 2)]
where the time goes in v3:
time: 438 us; the launch traced here: 430 us
  Pallas kernels  366 us (84%)
  other arithmetic  27.9 us (6%)
  local copies, waits for them, and re-layouts  21.5 us (5%)
  matrix products  7.47 us (2%)
  between operations  6.29 us (1%)
    pallas_call x1, Pallas kernels, head(): pl.pallas_call(head_kernel, name='head', out_shape=(jax.ShapeDtypeStruct(...  109 us
    pallas_call x1, Pallas kernels, back(): pl.pallas_call(back_kernel, name='back', out_shape=(jax.ShapeDtypeStruct(...  96.5 us
    pallas_call x1, Pallas kernels, front(): pl.pallas_call(front_kernel, name='front', out_shape=(jax.ShapeDtypeStruc...  89.4 us
    pallas_call x1, Pallas kernels, group_sum(): pl.pallas_call(group_kernel, name='group_sum', out_shape=tuple((jax.Shape...  44.8 us
    unnamed x113, local copies, waits for them, and re-layouts  17.8 us
    pallas_call x1, Pallas kernels, norm_sum(): pl.pallas_call(norm_kernel, name='norm_sum', out_shape=jax.ShapeDtypeStru...  14.2 us
    pallas_call x1, Pallas kernels, forward(): pl.pallas_call(forward_kernel, name='forward', out_shape=(out(D, BF), out...  12.1 us
    broadcast_in_dim x5, other arithmetic, on_device(): results += values[:3] + [values[3][None], values[4][None]]  9.78 us

profile of v3, /device:TPU:1, one launch (start us, length us, event | category | flops | bytes accessed | tf_op | source)
XLA Modules:
  0.0 430.0 jit_solution(12480021568302311994)
XLA Ops:
  0.7 3.5 bitcast_convert_fusion.table
  4.3 0.1 slice.84
  4.6 0.6 fusion.49
  5.2 0.6 broadcast_in_dim.109
  6.0 89.4 %front.1 = (s32[32,8,128]{2,1,0:T(8,128)}, bf16[1024,576]{1,0:T(8,128)(2,1)S(1)}, s32[4,8,128]{2,1,0:T(8,128)S(1)}, bf16[576,1536]{1,0:T(8,128)(2,1)S(1)}, bf16[...) custom-call(s32[8,256]{1,0:T(8,128)S(1)} %concatenate.15.tok, ...), custom_call_target="tpu_custom_call" | custom-call | flops 2000000000 | bytes 30000000 | tf_op jit(solution)/shard_map/front/pallas_call | solution.py:443
  95.4 0.6 copy-done.3
  95.9 1.2 copy-done.4
  97.2 0.7 copy-done.14
  97.8 0.6 copy-done.18
  98.4 0.6 reduce_max.33
  99.7 0.6 fusion.52
  100.4 0.0 copy-start.2
  100.4 0.2 while.25
  100.6 0.2 copy.95.hidden
  100.9 0.2 copy-done.42
  101.1 0.1 copy-done.2
  101.2 12.1 %forward.1 = (bf16[576,256]{1,0:T(8,128)(2,1)S(1)}, f32[576,256]{1,0:T(8,128)S(1)}, bf16[576,256]{1,0:T(8,128)(2,1)S(1)}, bf16[576,256]{1,0:T(8,128)(2,1)S(1)}, ...) custom-call(f32[256,576]{1,0:T(8,128)S(1)} %copy.95.hidden, ...), custom_call_target="tpu_custom_call" | custom-call | flops 4000000000 | bytes 20000000 | tf_op jit(solution)/shard_map/forward/pallas_call | solution.py:646
  113.3 0.0 copy-start.5
  113.3 0.9 copy-done.5
  114.2 0.8 copy-done.6
  115.0 0.8 copy-done.7
  115.9 0.8 copy-done.8
  116.7 0.7 copy-done.9
  117.4 0.7 copy-done.10
  118.2 0.7 copy-done.11
  118.9 0.7 copy-done.12
  119.6 0.7 copy-done.13
  120.3 0.6 copy-done.15
  121.0 0.6 copy-done.16
  121.6 0.6 copy-done.17
  122.2 109.4 %head.1 = (f32[576,256]{1,0:T(8,128)}, f32[576,1536]{1,0:T(8,128)}, bf16[576,1536]{1,0:T(8,128)(2,1)}, f32[8,256]{1,0:T(8,128)}) custom-call(bf16[576,256]{1,0:T(8,128)(2,1)} %copy-done.13, bf16[3072,576]{1,0:T(8,128)(2,1)} %get-tuple-element.222.rows_t, bf16[576,1536]{1,0:T(8,128)(2,1)S(1)} %copy-done.19, bf16[576,1536]{1,0:T(8,128)(2,1)} %copy-done.4, ...), custom_call_target="tpu_custom_call" | custom-call | flops 43486543872 | bytes 20000000 | tf_op jit(solution)/shard_map/head/pallas_call | solution.py:1036
  231.6 96.5 %back.1 = (f32[224,576]{1,0:T(8,128)}, bf16[1024,576]{1,0:T(8,128)(2,1)}, bf16[576,1536]{1,0:T(8,128)(2,1)}, f32[8,576]{1,0:T(8,128)}, bf16[576,256]{1,0:T(8,128)(2,1)S(1)}) custom-call(f32[576,256]{1,0:T(8,128)} %get-tuple-element.226.grad_final, f32[576,256]{1,0:T(8,128)} %copy-done.6, bf16[576,256]{1,0:T(8,128)(2,1)} %copy-done.9, ...), custom_call_target="tpu_custom_call" | custom-call | flops 10000000000 | bytes 30000000 | tf_op jit(solution)/shard_map/back/pallas_call | solution.py:1357
  328.2 6.8 %add_add_fusion = f32[576,1536]{1,0:T(8,128)} fusion(f32[576,1536]{1,0:T(8,128)} %get-tuple-element.243, bf16[576,1536]{1,0:T(8,128)(2,1)} %get-tuple-element.244, bf16[1024,576]{1,0:T(8,128)(2,1)} %get-tuple-element.245, bf16[1024,1536]{1,0:T(8,128)(2,1)S(1)} %copy-done.50), kind=kOutput, calls=%fused_computation.46 | convolution fusion | flops 1814593536 | bytes 13172736 | tf_op jit(solution)/shard_map/sd,sv->dv/dot_general | solution.py:1496
  335.0 0.2 while.26
  335.3 0.0 copy-start.46
  335.4 3.6 multiply_reduce_fusion
  339.0 0.7 multiply_reduce_fusion.1
  341.1 14.2 %norm_sum.1 = f32[8,128]{1,0:T(8,128)S(1)} custom-call(f32[8,128]{1,0:T(8,128)S(1)} %broadcast_in_dim.111.value), custom_call_target="tpu_custom_call" | custom-call | tf_op jit(solution)/shard_map/norm_sum/pallas_call | solution.py:1403
  355.2 0.5 slice.74
  355.7 0.6 multiply_reduce_fusion.2
  357.9 0.1 copy.173
  358.0 0.1 copy.112
  358.1 0.2 fusion.45
  358.3 0.1 reshape.252
  358.5 1.0 fusion.43
  359.5 0.1 fusion.48
  359.6 1.0 copy-done.20
  360.6 8.5 %fusion.16 = (f32[1,1536,576]{1,2,0:T(8,128)}, f32[576,1536]{1,0:T(8,128)S(1)}, f32[1,1536,576]{1,2,0:T(8,128)}) fusion(f32[576,1536]{1,0:T(8,128)} %get-tuple-element.248, f32[]{:T(128)S(6)} %min_shard_map.3, f32[1,1536,576]{1,2,0:T(8,128)} %param.45, f32[1,1536,576]{1,2,0:T(8,128)} %param.44, f32[1,1536,576]{1,2,0:T(8,128)S(1)} %copy-done.20, ...), kind=kLoop, calls=%fused_computation.52 | loop fusion | flops 15040512 | bytes 28311556 | tf_op jit(solution)/shard_map/broadcast_in_dim | solution.py:1707
  369.1 44.8 %group_sum.1 = (f32[576,1536]{1,0:T(8,128)S(1)}, f32[128,576]{1,0:T(8,128)S(1)}, f32[320,128]{1,0:T(8,128)S(1)}, f32[8,640]{1,0:T(8,128)S(1)}) custom-call(f32[576,1536]{1,0:T(8,128)S(1)} %get-tuple-element.368.refs_0_, f32[128,576]{1,0:T(8,128)S(1)} %select_maximum_fusion.refs_1_, f32[320,128]{1,0:T(8,128)S(1)} %pad.46.refs_2_, f32[8,640]{1,0:T(8,128)S(1)} %scatter.4.refs_3_), custom_call_target="tpu_custom_call" | custom-call | flops 10000000 | bytes 20000000 | tf_op jit(solution)/shard_map/group_sum/pallas_call | solution.py:1483
  413.9 5.3 %fusion.13 = (f32[1536,576]{0,1:T(8,128)}, f32[1536,576]{0,1:T(8,128)}, f32[1536,576]{0,1:T(8,128)}) fusion(f32[1536,576]{0,1:T(8,128)S(1)} %copy-done.21, f32[1536,576]{0,1:T(8,128)S(1)} %copy-done.22, f32[576,1536]{1,0:T(8,128)S(1)} %get-tuple-element.250), kind=kLoop, calls=%fused_computation.44 | loop fusion | flops 6193152 | bytes 21233664 | tf_op jit(solution)/shard_map/transpose | solution.py:1706
  419.2 0.1 div.217
  419.3 0.0 copy-start.27
  419.3 0.8 fusion.32
  420.2 0.9 fusion.26
  421.1 0.7 fusion.39
  421.8 0.6 multiply_subtract_fusion.2
  422.4 0.6 copy.107
  423.0 0.6 copy.108
  423.6 0.8 copy.105
  424.4 0.8 copy.106
  425.3 0.7 copy.103
  426.0 0.7 copy.104
  426.7 0.5 slice.72
  427.2 1.2 slice.73
  (101 shorter events, 0.6 us)
Async XLA Ops:
  0.7 3.6 copy-start.28
  0.7 3.8 copy-start.24
  0.7 3.8 copy-start.30
  0.7 3.9 copy-start.49
  0.7 5.2 %copy-start.37 = (s32[1,256]{1,0:T(1,128)S(1)}, s32[1,256]{1,0:T(1,128)}, u32[]{:S(2)}) copy-start(s32[1,256]{1,0:T(1,128)} %param.39) | copy-start | bytes 3076
  0.7 5.2 %copy-start.47 = (s32[1,256]{1,0:T(1,128)S(1)}, s32[1,256]{1,0:T(1,128)}, u32[]{:S(2)}) copy-start(s32[1,256]{1,0:T(1,128)} %param.40) | copy-start | bytes 3076
  0.7 5.2 %copy-start.48 = (s32[1,256]{1,0:T(1,128)S(1)}, s32[1,256]{1,0:T(1,128)}, u32[]{:S(2)}) copy-start(s32[1,256]{1,0:T(1,128)} %param.41) | copy-start | bytes 3076
  6.0 95.1 %copy-start.1 = (s32[8,256]{1,0:T(8,128)}, s32[8,256]{1,0:T(8,128)S(1)}, u32[]{:S(2)}) copy-start(s32[8,256]{1,0:T(8,128)S(1)} %concatenate.15.tok) | copy-start | bytes 24580
  95.4 0.6 copy-start.3
  95.9 1.2 copy-start.4
  97.2 0.7 copy-start.14
  97.8 0.6 copy-start.18
  100.4 0.7 copy-start.42
  100.4 0.8 copy-start.2
  101.2 12.1 %copy-start = (f32[8,576]{1,0:T(8,128)}, f32[8,576]{1,0:T(8,128)S(1)}, u32[]{:S(2)}) copy-start(f32[8,576]{1,0:T(8,128)S(1)} %pad.44.gains) | copy-start | bytes 55300
  101.2 21.0 %copy-start.19 = (bf16[576,1536]{1,0:T(8,128)(2,1)S(1)}, bf16[576,1536]{1,0:T(8,128)(2,1)}, u32[]{:S(2)}) copy-start(bf16[576,1536]{1,0:T(8,128)(2,1)} %get-tuple-element.523) | copy-start | bytes 5308420
  113.3 0.9 copy-start.5
  114.2 0.8 copy-start.6
  115.0 0.8 copy-start.7
  115.9 0.8 copy-start.8
  116.7 0.7 copy-start.9
  117.4 0.7 copy-start.10
  118.2 0.7 copy-start.11
  118.9 0.7 copy-start.12
  119.6 0.7 copy-start.13
  120.3 0.6 copy-start.15
  121.0 0.6 copy-start.16
  121.6 0.6 copy-start.17
  231.6 96.6 %copy-start.50 = (bf16[1024,1536]{1,0:T(8,128)(2,1)S(1)}, bf16[1024,1536]{1,0:T(8,128)(2,1)}, u32[]{:S(2)}) copy-start(bf16[1024,1536]{1,0:T(8,128)(2,1)} %get-tuple-element.246) | copy-start | bytes 9437188
  335.2 3.8 copy-start.23
  335.2 20.5 %copy-start.43 = (f32[8,576]{1,0:T(8,128)S(1)}, f32[8,576]{1,0:T(8,128)}, u32[]{:S(2)}) copy-start(f32[8,576]{1,0:T(8,128)} %get-tuple-element.242) | copy-start | bytes 55300
  335.3 22.5 %copy-start.41 = (f32[3,576]{1,0:T(4,128)S(1)}, f32[3,576]{1,0:T(4,128)}, u32[]{:S(2)}) copy-start(f32[3,576]{1,0:T(4,128)} %param.66) | copy-start | bytes 20740
  335.3 22.5 %copy-start.45 = (f32[1,3,576]{2,0,1:T(1,128)S(1)}, f32[1,3,576]{2,0,1:T(1,128)}, u32[]{:S(2)}) copy-start(f32[1,3,576]{2,0,1:T(1,128)} %param.65) | copy-start | bytes 20740
  335.3 22.5 %copy-start.46 = (f32[1,3,576]{2,0,1:T(1,128)S(1)}, f32[1,3,576]{2,0,1:T(1,128)}, u32[]{:S(2)}) copy-start(f32[1,3,576]{2,0,1:T(1,128)} %param.64) | copy-start | bytes 20740
  335.3 22.8 %copy-start.26 = (f32[2112,18]{0,1:T(8,128)S(1)}, f32[2112,18]{0,1:T(8,128)}, u32[]{:S(2)}) copy-start(f32[2112,18]{0,1:T(8,128)} %param.61) | copy-start | bytes 456196
  335.3 22.8 %copy-start.35 = (f32[1,2112,18]{1,0,2:T(1,128)S(1)}, f32[1,2112,18]{1,0,2:T(1,128)}, u32[]{:S(2)}) copy-start(f32[1,2112,18]{1,0,2:T(1,128)} %param.60) | copy-start | bytes 456196
  335.3 22.8 %copy-start.36 = (f32[1,2112,18]{1,0,2:T(1,128)S(1)}, f32[1,2112,18]{1,0,2:T(1,128)}, u32[]{:S(2)}) copy-start(f32[1,2112,18]{1,0,2:T(1,128)} %param.59) | copy-start | bytes 456196
  335.3 23.1 %copy-start.25 = (f32[576,96]{0,1:T(8,128)S(1)}, f32[576,96]{0,1:T(8,128)}, u32[]{:S(2)}) copy-start(f32[576,96]{0,1:T(8,128)} %param.56) | copy-start | bytes 663556
  335.3 23.1 %copy-start.31 = (f32[1,576,96]{1,2,0:T(8,128)S(1)}, f32[1,576,96]{1,2,0:T(8,128)}, u32[]{:S(2)}) copy-start(f32[1,576,96]{1,2,0:T(8,128)} %param.55) | copy-start | bytes 663556
  335.4 23.1 %copy-start.32 = (f32[1,576,96]{1,2,0:T(8,128)S(1)}, f32[1,576,96]{1,2,0:T(8,128)}, u32[]{:S(2)}) copy-start(f32[1,576,96]{1,2,0:T(8,128)} %param.54) | copy-start | bytes 663556
  339.0 20.5 %copy-start.29 = (f32[576,30]{0,1:T(8,128)S(1)}, f32[576,30]{0,1:T(8,128)}, u32[]{:S(2)}) copy-start(f32[576,30]{0,1:T(8,128)} %param.51) | copy-start | bytes 207364
  339.0 20.5 %copy-start.39 = (f32[1,576,30]{1,0,2:T(1,128)S(1)}, f32[1,576,30]{1,0,2:T(1,128)}, u32[]{:S(2)}) copy-start(f32[1,576,30]{1,0,2:T(1,128)} %param.50) | copy-start | bytes 207364
  339.0 20.5 %copy-start.40 = (f32[1,576,30]{1,0,2:T(1,128)S(1)}, f32[1,576,30]{1,0,2:T(1,128)}, u32[]{:S(2)}) copy-start(f32[1,576,30]{1,0,2:T(1,128)} %param.49) | copy-start | bytes 207364
  358.4 2.2 copy-start.20
  360.6 53.3 %copy-start.22 = (f32[1536,576]{0,1:T(8,128)S(1)}, f32[1536,576]{0,1:T(8,128)}, u32[]{:S(2)}) copy-start(f32[1536,576]{0,1:T(8,128)} %param.47) | copy-start | bytes 10616836
  369.1 44.8 %copy-start.21 = (f32[1536,576]{0,1:T(8,128)S(1)}, f32[1536,576]{0,1:T(8,128)}, u32[]{:S(2)}) copy-start(f32[1536,576]{0,1:T(8,128)} %param.46) | copy-start | bytes 10616836
  413.9 5.4 %copy-start.34 = (f32[2112,18]{0,1:T(8,128)S(1)}, f32[2112,18]{0,1:T(8,128)}, u32[]{:S(2)}) copy-start(f32[2112,18]{0,1:T(8,128)} %param.62) | copy-start | bytes 456196
  413.9 6.3 %copy-start.33 = (f32[576,96]{0,1:T(8,128)S(1)}, f32[576,96]{0,1:T(8,128)}, u32[]{:S(2)}) copy-start(f32[576,96]{0,1:T(8,128)} %param.57) | copy-start | bytes 663556
  413.9 7.2 %copy-start.38 = (f32[576,30]{0,1:T(8,128)S(1)}, f32[576,30]{0,1:T(8,128)}, u32[]{:S(2)}) copy-start(f32[576,30]{0,1:T(8,128)} %param.52) | copy-start | bytes 207364
  419.2 2.6 copy-start.44
  419.3 9.1 %copy-start.27 = (f32[18,2112]{1,0:T(8,128)}, f32[18,2112]{1,0:T(8,128)S(1)}, u32[]{:S(2)}) copy-start(f32[18,2112]{1,0:T(8,128)S(1)} %div.217) | copy-start | bytes 456196
